TPU v7x, 32 devices: a whole 2x2x4 slice. The times are simulated.
32 devices in a mesh: dp: 4 (over x, core), expert: 2 (over y), tp: 4 (over z).
Axes of the slice: x: 2, y: 2, z: 4, core: 2. Of those that a mesh axis runs over, the one named last changes fastest.
Arguments:
- hidden: bfloat16 [16, 8, 96, 5632], P('expert', 'dp', None, 'tp'), parts along dimension 1, may hold values from -6 to 6
- down_weight: bfloat16 [16, 5632, 3072], P('expert', 'tp'), may hold values from -0.078125 to 0.078125
- routes: int32 [2048, 4], P(('dp', 'expert')), parts along dimension 0, may hold values from 0 to 15, all different within a row; in each aligned block of 256 rows (0 to 255, 256 to 511, ...) at most 96 rows name the same one
- route_weight: float32 [2048, 4], P(('dp', 'expert')), parts along dimension 0, may hold values from 0.05 to 1
- residual: bfloat16 [2048, 3072], P(('dp', 'expert'), 'tp'), parts along dimension 0, may hold values from -6 to 6
Outputs:
- mixed: bfloat16 [2048, 3072], P(('dp', 'expert'), 'tp'), parts along dimension 0
There are 4 independent parts, one for each index of `dp`. A program takes and returns all parts, laid end to end along the dimension named above; an argument that names none is the same for every part. Nothing has to cross between parts.
Inputs may be any that keep to these rules, and one draw needn't show every extreme that they name: `routes`: each row names 4 different experts. Among the 256 rows of one source group no expert is named by more than 96 rows, a bound that some of them reach.
All inputs are finite; a program needn't handle non-finite values.
Results may differ from a plain program's by a relative error of at most 0.0095.
Values may be sent and summed in bfloat16 or wider, within the bound.
No kernel may reach another device: no remote copies, remote signals or barrier semaphores. Data moves between devices by JAX's collectives and lax.ppermute only.
A program may use at most 128 MiB of HBM per device.

v0:
```python
import jax
import jax.numpy as jnp
from jax import lax
from jax.sharding import PartitionSpec as P

EXPERTS = 16


def slot_table(routes):
    expert_ids = jnp.arange(EXPERTS, dtype=jnp.int32)
    matches = (routes[:, :, None] == expert_ids[None, None, :]).astype(jnp.int32)
    onehot = jnp.sum(matches, axis=1)
    before = jnp.cumsum(onehot, axis=0) - onehot
    return jnp.sum(matches * before[:, None, :], axis=2)


def combine(received, routes, route_weight, slot_of):
    capacity = received.shape[1]
    width = received.shape[2]
    flattened = received.reshape(-1, width)
    slot_index = (routes * capacity + slot_of).reshape(-1)
    picked = (
        flattened[slot_index].astype(jnp.float32).reshape(routes.shape[0], routes.shape[1], width)
    )
    share = route_weight / jnp.sum(route_weight, axis=1, keepdims=True)
    return jnp.sum(share[:, :, None] * picked, axis=1)


def on_device(hidden, down_weight, routes, route_weight, residual):
    slot_of = slot_table(routes)
    partial_value = jnp.einsum(
        "lsch,lhd->slcd", hidden, down_weight, preferred_element_type=jnp.float32
    ).astype(jnp.bfloat16)
    received = lax.all_to_all(partial_value, "expert", split_axis=0, concat_axis=1, tiled=True)
    mixed_part = combine(received[0], routes, route_weight, slot_of)
    expert_mix = lax.psum_scatter(
        mixed_part.astype(jnp.bfloat16), "tp", scatter_dimension=1, tiled=True
    ).astype(jnp.float32)
    return (residual.astype(jnp.float32) + expert_mix).astype(jnp.bfloat16)


def solution(mesh):
    return jax.shard_map(
        on_device,
        mesh=mesh,
        in_specs=(
            P("expert", "dp", None, "tp"),
            P("expert", "tp", None),
            P(("dp", "expert"), None),
            P(("dp", "expert"), None),
            P(("dp", "expert"), "tp"),
        ),
        out_specs=P(("dp", "expert"), "tp"),
        check_vma=False,
    )
```

profile of v0, /device:TPU:0, one launch (start us, length us, event | category | flops | bytes accessed | tf_op | source)
XLA Modules:
  0.0 243.8 jit_solution(4155577088709496349)
XLA Ops:
  6.5 30.0 %convert_bitcast_fusion = bf16[2,8,96,3072]{3,2,0,1:T(8,128)(2,1)} fusion(bf16[8,2,96,1408]{3,2,1,0:T(8,128)(2,1)} %param.5, bf16[8,1408,3072]{2,1,0:T(8,128)(2,1)} %param.6), kind=kOutput, calls=%fused_computation.4 | convolution fusion | flops 13292273664 | bytes 82968576 | tf_op jit(solution)/shard_map/lsch,lhd->slcd/dot_general | solution.py:31
  36.5 8.5 %copy.23 = bf16[2,8,96,3072]{3,2,1,0:T(8,128)(2,1)} copy(bf16[2,8,96,3072]{3,2,0,1:T(8,128)(2,1)} %convert_bitcast_fusion) | data formatting | bytes 18874368 | tf_op jit(solution)/shard_map/convert_element_type | solution.py:33
  45.0 0.0 copy-start.1
  45.0 0.0 copy-start.2
  45.0 7.4 %all-to-all-start = ((bf16[2,8,96,3072]{3,2,1,0:T(8,128)(2,1)}), bf16[2,8,96,3072]{3,2,1,0:T(8,128)(2,1)}, u32[]{:S(2)}, u32[]{:S(2)}) async-start(bf16[2,8,96,3072]{3,2,1,0:T(8,128)(2,1)} %copy.23), calls=%async_computation | async-start | bytes 18874368 | tf_op jit(solution)/shard_map/all_to_all | solution.py:34
  52.5 0.0 reduce-scatter.2.cloned.1.call-start
  52.5 0.0 copy-done.1
  52.6 0.6 reduce-window.6
  53.1 0.2 slice_reduce_fusion
  53.4 0.1 fusion.4
  53.5 0.1 copy.26
  53.6 0.1 reshape.55
  53.8 0.0 copy-done.2
  53.8 0.1 copy.22
  54.0 103.6 %all-to-all-done = bf16[2,8,96,3072]{3,2,1,0:T(8,128)(2,1)} async-done(((bf16[2,8,96,3072]{3,2,1,0:T(8,128)(2,1)}), bf16[2,8,96,3072]{3,2,1,0:T(8,128)(2,1)}, u32[]{:S(2)}, u32[]{:S(2)}) %all-to-all-start) | async-done | bytes 9437216 | tf_op jit(solution)/shard_map/all_to_all | solution.py:34
  157.6 17.1 %gather_fusion = bf16[1024,3072]{1,0:T(8,128)(2,1)} fusion(bf16[1536,3072]{1,0:T(8,128)(2,1)} %bitcast.3, s32[1024]{0:T(1024)S(1)} %broadcast_clamp_fusion), kind=kCustom, calls=%fused_computation | custom fusion | bytes 12587008 | tf_op jit(solution)/shard_map/gather | solution.py:23
  174.7 12.2 %reshape.56 = f32[256,4,3072]{2,1,0:T(4,128)} reshape(bf16[1024,3072]{1,0:T(8,128)(2,1)} %gather_fusion) | data formatting | bytes 18874368 | tf_op jit(solution)/shard_map/convert_element_type | solution.py:23
  186.9 0.0 copy-start
  186.9 12.2 %multiply_reduce_fusion = bf16[256,3072]{1,0:T(8,128)(2,1)} fusion(f32[256,4,3072]{2,1,0:T(4,128)} %reshape.56, f32[256,4]{1,0:T(8,128)S(1)} %copy.22), kind=kLoop, calls=%fused_computation.3 | loop fusion | flops 5505024 | bytes 14159872 | tf_op jit(solution)/shard_map/reduce_sum | solution.py:26
  199.2 0.0 reduce-scatter.2.cloned.1.call-update
  199.2 35.9 %reduce-scatter.2.cloned.1.call-done = bf16[256,768]{1,0:T(8,128)(2,1)} async-done(((bf16[256,3072]{1,0:T(8,128)(2,1)}), bf16[256,768]{1,0:T(8,128)(2,1)}) %reduce-scatter.2.cloned.1.call-update) | async-done | bytes 393232 | tf_op jit(solution)/shard_map/reduce_scatter | solution.py:36
  235.1 0.0 copy-done
  235.1 1.8 add_convert_fusion
  (10 shorter events, 0.1 us)
Async XLA Ops:
  45.0 7.5 %copy-start.1 = (s32[256,4]{0,1:T(4,128)S(1)}, s32[256,4]{0,1:T(4,128)}, u32[]{:S(2)}) copy-start(s32[256,4]{0,1:T(4,128)} %param.7) | copy-start | bytes 12292
  45.0 8.7 %copy-start.2 = (f32[256,4]{0,1:T(4,128)S(1)}, f32[256,4]{0,1:T(4,128)}, u32[]{:S(2)}) copy-start(f32[256,4]{0,1:T(4,128)} %param.8) | copy-start | bytes 12292
  45.0 112.6 %all-to-all-start = ((bf16[2,8,96,3072]{3,2,1,0:T(8,128)(2,1)}), bf16[2,8,96,3072]{3,2,1,0:T(8,128)(2,1)}, u32[]{:S(2)}, u32[]{:S(2)}) async-start(bf16[2,8,96,3072]{3,2,1,0:T(8,128)(2,1)} %copy.23), calls=%async_computation | async-start | bytes 18874368 | tf_op jit(solution)/shard_map/all_to_all | solution.py:34
  52.5 182.7 %reduce-scatter.2.cloned.1.call-start = ((), (), s32[]{:S(2)}) async-start(), calls=%async_computation.2 | async-start | bytes 1966080 | tf_op jit(solution)/shard_map/reduce_scatter | solution.py:36
  186.9 48.2 %copy-start = (bf16[256,768]{1,0:T(8,128)(2,1)S(1)}, bf16[256,768]{1,0:T(8,128)(2,1)}, u32[]{:S(2)}) copy-start(bf16[256,768]{1,0:T(8,128)(2,1)} %param.9) | copy-start | bytes 1179652
Sparse Core Ops, SparseCore 0:
  199.3 35.7 reduce-scatter.1
where the time goes:
time: 245 us; the launch traced here: 244 us
  waiting for transfers between devices  140 us (57%)
  local copies, waits for them, and re-layouts  38.5 us (16%)
  matrix products  30 us (12%)
  other arithmetic  14.9 us (6%)
  between operations  13.5 us (6%)
  starting transfers between devices  7.48 us (3%)
    all_to_all x1, waiting for transfers between devices, on_device(): lax.all_to_all(partial_value, 'expert', split_axis=0, concat_axis=1, tile...  104 us
    reduce_scatter x1, waiting for transfers between devices, on_device(): lax.psum_scatter(mixed_part.astype(jnp.bfloat16), 'tp', scatter_dimension...  35.9 us
    dot_general x1, matrix products, on_device(): jnp.einsum('lsch,lhd->slcd', hidden, down_weight, preferred_element_type=...  30 us
    gather x1, local copies, waits for them, and re-layouts, combine(): flattened[slot_index].astype(jnp.float32)  17.1 us
    reduce_sum x1, other arithmetic, combine(): return jnp.sum(share[:, :, None] * picked, axis=1)  12.2 us
    convert_element_type x1, local copies, waits for them, and re-layouts, combine(): flattened[slot_index].astype(jnp.float32)  12.2 us
    convert_element_type x1, local copies, waits for them, and re-layouts, on_device(): partial_value = jnp.einsum('lsch,lhd->slcd', hidden, down_weight, preferr...  8.5 us
    all_to_all x1, starting transfers between devices, on_device(): lax.all_to_all(partial_value, 'expert', split_axis=0, concat_axis=1, tile...  7.43 us
  transfers between devices with their start and end apart: 2, of which 2 were waited for; matrix products, arithmetic and copies ran while one was open for 1% of the time, Pallas kernels for 0%

commit v1 on v0

v1 whole, which is shorter than its diff:
```python
import functools

import jax
import jax.numpy as jnp
from jax import lax
from jax.experimental import pallas as pl
from jax.experimental.pallas import tpu as pltpu
from jax.sharding import PartitionSpec as P

LANES = 128
AHEAD = 2
BLOCKS = (3, 1, 2, 0)

VMEM = pl.BlockSpec(memory_space=pltpu.VMEM)
SMEM = pl.BlockSpec(memory_space=pltpu.SMEM)
ANY = pl.BlockSpec(memory_space=pl.ANY)


def table_kernel(capacity, ids_ref, routes_ref, weight_ref, table_ref):
    sources, tokens, width = table_ref.shape
    top = routes_ref.shape[2]
    local = width // capacity
    first = ids_ref[0] * local
    rows = lax.broadcasted_iota(jnp.int32, (tokens, tokens), 0)
    cols = lax.broadcasted_iota(jnp.int32, (tokens, tokens), 1)
    earlier = (cols < rows).astype(jnp.float32).astype(jnp.bfloat16)
    lanes = lax.broadcasted_iota(jnp.int32, (tokens, LANES), 1)
    places = lax.broadcasted_iota(jnp.int32, (tokens, width), 1)
    for source in range(sources):
        routes = routes_ref[source]
        weight = weight_ref[source]
        share = weight / jnp.sum(weight, axis=1, keepdims=True)
        matches = [(routes[:, k : k + 1] == lanes).astype(jnp.float32) for k in range(top)]
        onehot = functools.reduce(jnp.add, matches)
        before = jnp.dot(earlier, onehot.astype(jnp.bfloat16), preferred_element_type=jnp.float32)
        entry = jnp.zeros((tokens, width), jnp.float32)
        for k in range(top):
            slot = jnp.sum(matches[k] * before, axis=1, keepdims=True).astype(jnp.int32)
            expert = routes[:, k : k + 1] - first
            at = jnp.where((expert >= 0) & (expert < local), expert * capacity + slot, -1)
            entry = entry + jnp.where(places == at, share[:, k : k + 1], 0.0)
        table_ref[source] = entry.astype(table_ref.dtype)


def share_tables(ids, routes, weight, local, capacity):
    sources, tokens = routes.shape[:2]
    return pl.pallas_call(
        functools.partial(table_kernel, capacity),
        in_specs=[SMEM, VMEM, VMEM],
        out_specs=VMEM,
        out_shape=jax.ShapeDtypeStruct((sources, tokens, local * capacity), jnp.bfloat16),
        compiler_params=pltpu.CompilerParams(vmem_limit_bytes=16 << 20),
        name="tables",
    )(ids, routes, weight)


def chunk_kernel(chunk, chunks, pair, *refs):
    first, last = chunk == 0, chunk == chunks - 1
    refs = list(refs)
    ids_ref, hidden_ref, weight_ref, table_ref = refs[:4]
    del refs[:4]
    held_ref = None if first else refs.pop(0)
    outs = [refs.pop(0) for _ in range(2 if pair else 1)]
    stay_ref = refs.pop(0) if first else None
    next_ref = None if last else refs.pop(0)
    weights, partial, sems, next_sems = refs[:4]
    hidden_sems = refs[4] if first else None

    local, sources, capacity, depth = hidden_ref.shape
    blocks = len(BLOCKS)
    width = partial.shape[2] // blocks
    mine, rank = ids_ref[0], ids_ref[1]
    ahead = 0 if first else held_ref.shape[0]

    def strip(which, expert, q, target, sem):
        dest = lax.bitwise_xor(rank, BLOCKS[q])
        start = pl.multiple_of((dest * chunks + which) * width, LANES)
        return pltpu.make_async_copy(
            weight_ref.at[expert, :, pl.ds(start, width)], target.at[:, pl.ds(q * width, width)], sem
        )

    def bring(expert):
        at = expert - ahead
        return [strip(chunk, expert, q, weights.at[at], sems.at[at, q]) for q in range(blocks)]

    def bring_next(expert):
        return [strip(chunk + 1, expert, q, next_ref.at[expert], next_sems.at[expert, q]) for q in range(blocks)]

    def bring_hidden(expert):
        return pltpu.make_async_copy(hidden_ref.at[expert], stay_ref.at[expert], hidden_sems.at[expert])

    for expert in range(local):
        if first:
            bring_hidden(expert).start()
        if expert >= ahead:
            for copy in bring(expert):
                copy.start()
    if not last:
        for expert in range(next_ref.shape[0]):
            for copy in bring_next(expert):
                copy.start()

    for expert in range(local):
        if first:
            bring_hidden(expert).wait()
        if expert >= ahead:
            for copy in bring(expert):
                copy.wait()
            weight = weights[expert - ahead]
        else:
            weight = held_ref[expert]
        rows = (stay_ref if first else hidden_ref)[expert].reshape(sources * capacity, depth)
        product = jnp.dot(rows, weight, preferred_element_type=jnp.float32).astype(partial.dtype)
        for source in range(sources):
            partial[source, expert * capacity : (expert + 1) * capacity, :] = product[
                source * capacity : (source + 1) * capacity
            ]

    def combine(source):
        total = jnp.dot(table_ref[source], partial[source], preferred_element_type=jnp.float32)
        return total.astype(outs[0].dtype)

    if pair:
        for out_ref, source in zip(outs, (1 - mine, mine)):
            total = combine(source)
            for q in range(blocks):
                out_ref[q] = total[:, q * width : (q + 1) * width]
    else:
        for source in range(sources):
            total = combine(source)
            for q in range(blocks):
                outs[0][source, q] = total[:, q * width : (q + 1) * width]
    if not last:
        for expert in range(next_ref.shape[0]):
            for copy in bring_next(expert):
                copy.wait()


def chunk_sums(chunk, chunks, pair, ids, hidden, weight, table, held):
    first, last = chunk == 0, chunk == chunks - 1
    local, sources, capacity, depth = hidden.shape
    tokens = table.shape[1]
    blocks = len(BLOCKS)
    width = weight.shape[2] // (blocks * chunks)
    ahead = min(AHEAD, local)
    brought = local if first else local - ahead
    bf16 = jnp.bfloat16
    group = jax.ShapeDtypeStruct((blocks, tokens, width), bf16)
    if pair:
        out_shape = [group, group]
    else:
        out_shape = [jax.ShapeDtypeStruct((sources, blocks, tokens, width), bf16)]
    if first:
        out_shape.append(jax.ShapeDtypeStruct(hidden.shape, bf16))
    if not last:
        out_shape.append(jax.ShapeDtypeStruct((ahead, depth, blocks * width), bf16))
    scratch = [
        pltpu.VMEM((max(brought, 1), depth, blocks * width), bf16),
        pltpu.VMEM((sources, local * capacity, blocks * width), bf16),
        pltpu.SemaphoreType.DMA((max(brought, 1), blocks)),
        pltpu.SemaphoreType.DMA((ahead, blocks)),
    ]
    if first:
        scratch.append(pltpu.SemaphoreType.DMA((local,)))
    operands = [ids, hidden, weight, table] + ([] if first else [held])
    flops = 2 * sources * local * capacity * blocks * width * (depth + tokens)
    results = pl.pallas_call(
        functools.partial(chunk_kernel, chunk, chunks, pair),
        in_specs=[SMEM, ANY if first else VMEM, ANY, VMEM] + ([] if first else [VMEM]),
        out_specs=[VMEM] * len(out_shape),
        out_shape=out_shape,
        scratch_shapes=scratch,
        cost_estimate=pl.CostEstimate(
            flops=flops, bytes_accessed=2 * local * depth * blocks * width, transcendentals=0
        ),
        compiler_params=pltpu.CompilerParams(vmem_limit_bytes=32 << 20),
        name=f"chunk{chunk}",
    )(*operands)
    results = list(results)
    sums = [results.pop(0) for _ in range(2 if pair else 1)]
    hidden = results.pop(0) if first else hidden
    held = None if last else results.pop(0)
    return sums, hidden, held


def on_device(experts, ranks, hidden, down_weight, routes, route_weight, residual):
    f32, bf16 = jnp.float32, jnp.bfloat16
    local, sources, capacity, _ = hidden.shape
    tokens = routes.shape[0]
    pair = experts == 2
    me, rank = lax.axis_index("expert"), lax.axis_index("tp")
    ids = jnp.stack([me, rank]).astype(jnp.int32)
    if pair:
        swap = [(0, 1), (1, 0)]
        other_routes = lax.ppermute(routes, "expert", swap)
        other_weight = lax.ppermute(route_weight, "expert", swap)

        def by_source(own, other):
            return jnp.where(me == 0, jnp.stack([own, other]), jnp.stack([other, own]))

        all_routes, all_weight = by_source(routes, other_routes), by_source(route_weight, other_weight)
    else:
        all_routes = lax.all_gather(routes, "expert").reshape(sources, -1, routes.shape[1])
        all_weight = lax.all_gather(route_weight, "expert").reshape(sources, -1, routes.shape[1])
    table = share_tables(ids, all_routes, all_weight, local, capacity)

    features = residual.shape[1]
    chunks = features // LANES
    near = [(i, i ^ 1) for i in range(ranks)]
    far = [(i, i ^ 2) for i in range(ranks)]
    held, pieces = None, []
    for chunk in range(chunks):
        sums, hidden, held = chunk_sums(chunk, chunks, pair, ids, hidden, down_weight, table, held)
        if pair:
            other, own = sums
            got = lax.ppermute(other, "expert", swap)
            send = (own[:2].astype(f32) + got[:2].astype(f32)).astype(bf16)
            base = own[2:].astype(f32) + got[2:].astype(f32)
        else:
            whole = lax.psum_scatter(sums[0], "expert", scatter_dimension=0, tiled=True)
            whole = jnp.moveaxis(whole, 0, 1).reshape(len(BLOCKS), tokens, LANES)
            send, base = whole[:2], whole[2:].astype(f32)
        near_got = lax.ppermute(send, "tp", near).astype(f32)
        far_got = lax.ppermute((base[0] + near_got[0]).astype(bf16), "tp", far).astype(f32)
        here = residual[:, chunk * LANES : (chunk + 1) * LANES].astype(f32)
        pieces.append((here + (base[1] + near_got[1] + far_got)).astype(bf16))
    return jnp.concatenate(pieces, axis=1)


def solution(mesh):
    return jax.shard_map(
        functools.partial(on_device, mesh.shape["expert"], mesh.shape["tp"]),
        mesh=mesh,
        in_specs=(
            P("expert", "dp", None, "tp"),
            P("expert", "tp", None),
            P(("dp", "expert"), None),
            P(("dp", "expert"), None),
            P(("dp", "expert"), "tp"),
        ),
        out_specs=P(("dp", "expert"), "tp"),
        check_vma=False,
    )
```

time: 245 us -> 94.8 us (0.39)
  waiting for transfers between devices: 140 us -> 16.8 us
  Pallas kernels: 0 us -> 45.3 us
  local copies, waits for them, and re-layouts: 38.5 us -> 2.91 us
  matrix products: 30 us -> 0 us
  starting transfers between devices: 7.48 us -> 26.1 us
  between operations: 13.5 us -> 0.3 us
  other arithmetic: 14.9 us -> 3.12 us
    all_to_all x1 -> x0, waiting for transfers between devices: 104 us -> none  [on_device(): lax.all_to_all(partial_value, 'expert', split_axis=0, concat_axis=1, tile...]
    pallas_call x0 -> x7, Pallas kernels: none -> 45.3 us  [the longest x6 41.9 us: chunk_sums(): pl.pallas_call(functools.partial(chunk_kernel, chunk, chunks, pair), in_s...]
    reduce_scatter x1 -> x0, waiting for transfers between devices: 35.9 us -> none  [on_device(): lax.psum_scatter(mixed_part.astype(jnp.bfloat16), 'tp', scatter_dimension...]
    dot_general x1 -> x0, matrix products: 30 us -> none  [on_device(): jnp.einsum('lsch,lhd->slcd', hidden, down_weight, preferred_element_type=...]
    ppermute x0 -> x20, starting transfers between devices: none -> 26.1 us  [the longest x6 9.1 us: on_device(): lax.ppermute((base[0] + near_got[0]).astype(bf16), 'tp', far).astype(f32)]
    convert_element_type x2 -> x0, local copies, waits for them, and re-layouts: 20.7 us -> none  [the longest x1 12.2 us: combine(): flattened[slot_index].astype(jnp.float32)]
    gather x1 -> x0, local copies, waits for them, and re-layouts: 17.1 us -> none  [combine(): flattened[slot_index].astype(jnp.float32)]
    ppermute x0 -> x20, waiting for transfers between devices: none -> 16.8 us  [the longest x6 6.18 us: on_device(): lax.ppermute((base[0] + near_got[0]).astype(bf16), 'tp', far).astype(f32)]
  transfers between devices with their start and end apart: 2 -> 20, of which waited for: 2 -> 10; matrix products, arithmetic and copies ran while one was open for 1% -> 2% of each run, Pallas kernels for 0% -> 36%
where the time goes in v1:
time: 94.8 us; the launch traced here: 94.5 us
  Pallas kernels  45.3 us (48%)
  starting transfers between devices  26.1 us (28%)
  waiting for transfers between devices  16.8 us (18%)
  other arithmetic  3.12 us (3%)
  local copies, waits for them, and re-layouts  2.91 us (3%)
    pallas_call x6, Pallas kernels, chunk_sums(): pl.pallas_call(functools.partial(chunk_kernel, chunk, chunks, pair), in_s...  41.9 us
    ppermute x6, starting transfers between devices, on_device(): lax.ppermute((base[0] + near_got[0]).astype(bf16), 'tp', far).astype(f32)  9.1 us
    ppermute x6, starting transfers between devices, on_device(): near_got = lax.ppermute(send, 'tp', near).astype(f32)  7.56 us
    ppermute x6, starting transfers between devices, on_device(): got = lax.ppermute(other, 'expert', swap)  6.4 us
    ppermute x6, waiting for transfers between devices, on_device(): lax.ppermute((base[0] + near_got[0]).astype(bf16), 'tp', far).astype(f32)  6.18 us
    ppermute x1, waiting for transfers between devices, on_device(): other_weight = lax.ppermute(route_weight, 'expert', swap)  3.71 us
    ppermute x6, waiting for transfers between devices, on_device(): near_got = lax.ppermute(send, 'tp', near).astype(f32)  3.67 us
    pallas_call x1, Pallas kernels, share_tables(): pl.pallas_call(functools.partial(table_kernel, capacity), in_specs=[SMEM,...  3.39 us
  transfers between devices with their start and end apart: 20, of which 10 were waited for; matrix products, arithmetic and copies ran while one was open for 2% of the time, Pallas kernels for 36%

profile of v1, /device:TPU:0, one launch (start us, length us, event | category | flops | bytes accessed | tf_op | source)
XLA Modules:
  0.0 94.5 jit_solution(15362157711909532375)
XLA Ops:
  0.0 3.0 %collective-permute-start = (s32[256,4]{0,1:T(4,128)}, s32[256,4]{0,1:T(4,128)S(1)}, u32[]{:S(2)}, u32[]{:S(2)}) collective-permute-start(s32[256,4]{0,1:T(4,128)} %param.7), channel_id=1, source_target_pairs={{0,4},{4,0},{1,5},{5,1},{2,6},{6,2},{3,7},{7,3},{8,12},{12,8},{9,1... | collective-permute-start | bytes 12296 | tf_op jit(solution)/shard_map/ppermute | solution.py:195
  3.1 3.7 %collective-permute-done.1 = f32[256,4]{0,1:T(4,128)S(1)} collective-permute-done((f32[256,4]{0,1:T(4,128)}, f32[256,4]{0,1:T(4,128)S(1)}, u32[]{:S(2)}, u32[]{:S(2)}) %collective-permute-start.1) | collective-permute-done | bytes 4128 | tf_op jit(solution)/shard_map/ppermute | solution.py:196
  6.8 0.8 pad_maximum_fusion.1
  7.7 0.8 pad_add_fusion.1
  9.0 3.4 %tables.1.refs_3_ = bf16[2,256,768]{2,1,0:T(8,128)(2,1)S(1)} custom-call(s32[2]{0:T(128)S(1)} %pad_add_fusion.2.ids_ref.refs_0_, s32[2,256,4]{2,1,0:T(8,128)S(1)} %broadcast_select_fusion.1.routes_ref, f32[2,256,4]{2,1,0:T(8,128)S(1)} %broadcast_select_fusion.weight_ref), custom_call_target="tpu_custom_call" | custom-call | tf_op jit(solution)/shard_map/tables/pallas_call | solution.py:47
  12.4 2.2 %copy-done = bf16[8,2,96,1408]{3,2,1,0:T(8,128)(2,1)S(1)} copy-done((bf16[8,2,96,1408]{3,2,1,0:T(8,128)(2,1)S(1)}, bf16[8,2,96,1408]{3,2,1,0:T(8,128)(2,1)}, u32[]{:S(2)}) %copy-start) | copy-done | bytes 4325400
  14.7 7.6 %chunk0.1 = (bf16[4,256,128]{2,1,0:T(8,128)(2,1)S(1)}, bf16[4,256,128]{2,1,0:T(8,128)(2,1)S(1)}, bf16[8,2,96,1408]{3,2,1,0:T(8,128)(2,1)S(1)}, bf16[2,1408,512]{2,1,0:T(8,128)(2,1)S(1)}) custom-call(s32[2]{0:T(128)S(1)} %pad_add_fusion.2.ids_ref.refs_0_, bf16[8,2,96,1408]{3,2,1,0:T(8,128)(2,1)S(1)} %copy-done, bf16[8,1408,3072]{2,1,0:T(8,128)(2,1)} %refs_2_.11, ...), custom_call_target="tpu_custom_call" | custom-call | flops 2617245696 | bytes 11534336 | tf_op jit(solution)/shard_map/chunk0/pallas_call | solution.py:167
  22.4 6.9 %chunk1.1 = (bf16[4,256,128]{2,1,0:T(8,128)(2,1)S(1)}, bf16[4,256,128]{2,1,0:T(8,128)(2,1)S(1)}, bf16[2,1408,512]{2,1,0:T(8,128)(2,1)S(1)}) custom-call(s32[2]{0:T(128)S(1)} %pad_add_fusion.2.ids_ref.refs_0_, bf16[8,2,96,1408]{3,2,1,0:T(8,128)(2,1)S(1)} %get-tuple-element.25.refs_1_, bf16[8,1408,3072]{2,1,0:T(8,128)(2,1)} %refs_2_.11, ...), custom_call_target="tpu_custom_call" | custom-call | flops 2617245696 | bytes 11534336 | tf_op jit(solution)/shard_map/chunk1/pallas_call | solution.py:167
  29.4 2.1 %collective-permute-start.5 = (bf16[4,256,128]{2,1,0:T(8,128)(2,1)S(1)}, bf16[4,256,128]{2,1,0:T(8,128)(2,1)S(1)}, u32[]{:S(2)}, u32[]{:S(2)}) collective-permute-start(bf16[4,256,128]{2,1,0:T(8,128)(2,1)S(1)} %get-tuple-element.28), channel_id=1, source_target_pairs={{0,4},{4,0},{1,5},{5,1},{2,6},{6,2},{3,7},{7,3},{8,12},{12,8},{9,1... | collective-permute-start | bytes 786440 | tf_op jit(solution)/shard_map/ppermute | solution.py:216
  31.4 6.9 %chunk2.1 = (bf16[4,256,128]{2,1,0:T(8,128)(2,1)S(1)}, bf16[4,256,128]{2,1,0:T(8,128)(2,1)S(1)}, bf16[2,1408,512]{2,1,0:T(8,128)(2,1)S(1)}) custom-call(s32[2]{0:T(128)S(1)} %pad_add_fusion.2.ids_ref.refs_0_, bf16[8,2,96,1408]{3,2,1,0:T(8,128)(2,1)S(1)} %get-tuple-element.25.refs_1_, bf16[8,1408,3072]{2,1,0:T(8,128)(2,1)} %refs_2_.11, ...), custom_call_target="tpu_custom_call" | custom-call | flops 2617245696 | bytes 11534336 | tf_op jit(solution)/shard_map/chunk2/pallas_call | solution.py:167
  38.5 7.1 %chunk3.1 = (bf16[4,256,128]{2,1,0:T(8,128)(2,1)S(1)}, bf16[4,256,128]{2,1,0:T(8,128)(2,1)S(1)}, bf16[2,1408,512]{2,1,0:T(8,128)(2,1)S(1)}) custom-call(s32[2]{0:T(128)S(1)} %pad_add_fusion.2.ids_ref.refs_0_, bf16[8,2,96,1408]{3,2,1,0:T(8,128)(2,1)S(1)} %get-tuple-element.25.refs_1_, bf16[8,1408,3072]{2,1,0:T(8,128)(2,1)} %refs_2_.11, ...), custom_call_target="tpu_custom_call" | custom-call | flops 2617245696 | bytes 11534336 | tf_op jit(solution)/shard_map/chunk3/pallas_call | solution.py:167
  45.6 2.1 %collective-permute-start.11 = (bf16[4,256,128]{2,1,0:T(8,128)(2,1)S(1)}, bf16[4,256,128]{2,1,0:T(8,128)(2,1)S(1)}, u32[]{:S(2)}, u32[]{:S(2)}) collective-permute-start(bf16[4,256,128]{2,1,0:T(8,128)(2,1)S(1)} %get-tuple-element.34), channel_id=1, source_target_pairs={{0,4},{4,0},{1,5},{5,1},{2,6},{6,2},{3,7},{7,3},{8,12},{12,8},{9,1... | collective-permute-start | bytes 786440 | tf_op jit(solution)/shard_map/ppermute | solution.py:216
  47.6 7.2 %chunk4.1 = (bf16[4,256,128]{2,1,0:T(8,128)(2,1)S(1)}, bf16[4,256,128]{2,1,0:T(8,128)(2,1)S(1)}, bf16[2,1408,512]{2,1,0:T(8,128)(2,1)S(1)}) custom-call(s32[2]{0:T(128)S(1)} %pad_add_fusion.2.ids_ref.refs_0_, bf16[8,2,96,1408]{3,2,1,0:T(8,128)(2,1)S(1)} %get-tuple-element.25.refs_1_, bf16[8,1408,3072]{2,1,0:T(8,128)(2,1)} %refs_2_.11, ...), custom_call_target="tpu_custom_call" | custom-call | flops 2617245696 | bytes 11534336 | tf_op jit(solution)/shard_map/chunk4/pallas_call | solution.py:167
  54.8 6.1 %chunk5.1 = (bf16[4,256,128]{2,1,0:T(8,128)(2,1)S(1)}, bf16[4,256,128]{2,1,0:T(8,128)(2,1)S(1)}) custom-call(s32[2]{0:T(128)S(1)} %pad_add_fusion.2.ids_ref.refs_0_, bf16[8,2,96,1408]{3,2,1,0:T(8,128)(2,1)S(1)} %get-tuple-element.25.refs_1_, bf16[8,1408,3072]{2,1,0:T(8,128)(2,1)} %refs_2_.11, bf16[2,256,768]{2,1,0:T(8,128)(2,1)S(1)} %tables.1.refs_3_, ...), custom_call_target="tpu_custom_call" | custom-call | flops 2617245696 | bytes 11534336 | tf_op jit(solution)/shard_map/chunk5/pallas_call | solution.py:167
  61.0 2.0 %collective-permute-start.17 = (bf16[4,256,128]{2,1,0:T(8,128)(2,1)S(1)}, bf16[4,256,128]{2,1,0:T(8,128)(2,1)S(1)}, u32[]{:S(2)}, u32[]{:S(2)}) collective-permute-start(bf16[4,256,128]{2,1,0:T(8,128)(2,1)S(1)} %get-tuple-element.40), channel_id=1, source_target_pairs={{0,4},{4,0},{1,5},{5,1},{2,6},{6,2},{3,7},{7,3},{8,12},{12,8},{9,1... | collective-permute-start | bytes 786440 | tf_op jit(solution)/shard_map/ppermute | solution.py:216
  63.1 1.6 %collective-permute-start.3 = (bf16[2,256,128]{2,1,0:T(8,128)(2,1)S(1)}, bf16[2,256,128]{2,1,0:T(8,128)(2,1)S(1)}, u32[]{:S(2)}, u32[]{:S(2)}) collective-permute-start(bf16[2,256,128]{2,1,0:T(8,128)(2,1)S(1)} %get-tuple-element.52), channel_id=1, source_target_pairs={{0,1},{1,0},{2,3},{3,2},{4,5},{5,4},{6,7},{7,6},{8,9},{9,8},{10,11... | collective-permute-start | bytes 393224 | tf_op jit(solution)/shard_map/ppermute | solution.py:223
  65.4 1.6 %collective-permute-start.9 = (bf16[2,256,128]{2,1,0:T(8,128)(2,1)S(1)}, bf16[2,256,128]{2,1,0:T(8,128)(2,1)S(1)}, u32[]{:S(2)}, u32[]{:S(2)}) collective-permute-start(bf16[2,256,128]{2,1,0:T(8,128)(2,1)S(1)} %get-tuple-element.48), channel_id=1, source_target_pairs={{0,1},{1,0},{2,3},{3,2},{4,5},{5,4},{6,7},{7,6},{8,9},{9,8},{10,11... | collective-permute-start | bytes 393224 | tf_op jit(solution)/shard_map/ppermute | solution.py:223
  67.1 2.2 %collective-permute-done.14 = bf16[4,256,128]{2,1,0:T(8,128)(2,1)S(1)} collective-permute-done((bf16[4,256,128]{2,1,0:T(8,128)(2,1)S(1)}, bf16[4,256,128]{2,1,0:T(8,128)(2,1)S(1)}, u32[]{:S(2)}, u32[]{:S(2)}) %collective-permute-start.14) | collective-permute-done | bytes 262176 | tf_op jit(solution)/shard_map/ppermute | solution.py:216
  69.3 1.7 %collective-permute-start.12 = (bf16[2,256,128]{2,1,0:T(8,128)(2,1)S(1)}, bf16[2,256,128]{2,1,0:T(8,128)(2,1)S(1)}, u32[]{:S(2)}, u32[]{:S(2)}) collective-permute-start(bf16[2,256,128]{2,1,0:T(8,128)(2,1)S(1)} %get-tuple-element.46), channel_id=1, source_target_pairs={{0,1},{1,0},{2,3},{3,2},{4,5},{5,4},{6,7},{7,6},{8,9},{9,8},{10,11... | collective-permute-start | bytes 393224 | tf_op jit(solution)/shard_map/ppermute | solution.py:223
  71.1 1.0 %collective-permute-done.17 = bf16[4,256,128]{2,1,0:T(8,128)(2,1)S(1)} collective-permute-done((bf16[4,256,128]{2,1,0:T(8,128)(2,1)S(1)}, bf16[4,256,128]{2,1,0:T(8,128)(2,1)S(1)}, u32[]{:S(2)}, u32[]{:S(2)}) %collective-permute-start.17) | collective-permute-done | bytes 262176 | tf_op jit(solution)/shard_map/ppermute | solution.py:216
  72.1 1.7 %collective-permute-start.15 = (bf16[2,256,128]{2,1,0:T(8,128)(2,1)S(1)}, bf16[2,256,128]{2,1,0:T(8,128)(2,1)S(1)}, u32[]{:S(2)}, u32[]{:S(2)}) collective-permute-start(bf16[2,256,128]{2,1,0:T(8,128)(2,1)S(1)} %get-tuple-element.44), channel_id=1, source_target_pairs={{0,1},{1,0},{2,3},{3,2},{4,5},{5,4},{6,7},{7,6},{8,9},{9,8},{10,11... | collective-permute-start | bytes 393224 | tf_op jit(solution)/shard_map/ppermute | solution.py:223
  74.3 2.8 %collective-permute-start.4 = (bf16[256,128]{1,0:T(8,128)(2,1)S(1)}, bf16[256,128]{1,0:T(8,128)(2,1)S(1)}, u32[]{:S(2)}, u32[]{:S(2)}) collective-permute-start(bf16[256,128]{1,0:T(8,128)(2,1)S(1)} %fusion.31), channel_id=1, source_target_pairs={{0,2},{1,3},{2,0},{3,1},{4,6},{5,7},{6,4},{7,5},{8,10},{9,11},{10,... | collective-permute-start | bytes 196616 | tf_op jit(solution)/shard_map/ppermute | solution.py:224
  77.5 1.1 %collective-permute-done.12 = bf16[2,256,128]{2,1,0:T(8,128)(2,1)S(1)} collective-permute-done((bf16[2,256,128]{2,1,0:T(8,128)(2,1)S(1)}, bf16[2,256,128]{2,1,0:T(8,128)(2,1)S(1)}, u32[]{:S(2)}, u32[]{:S(2)}) %collective-permute-start.12) | collective-permute-done | bytes 131104 | tf_op jit(solution)/shard_map/ppermute | solution.py:223
  78.6 1.7 %collective-permute-start.10 = (bf16[256,128]{1,0:T(8,128)(2,1)S(1)}, bf16[256,128]{1,0:T(8,128)(2,1)S(1)}, u32[]{:S(2)}, u32[]{:S(2)}) collective-permute-start(bf16[256,128]{1,0:T(8,128)(2,1)S(1)} %fusion.35), channel_id=1, source_target_pairs={{0,2},{1,3},{2,0},{3,1},{4,6},{5,7},{6,4},{7,5},{8,10},{9,11},{10,... | collective-permute-start | bytes 196616 | tf_op jit(solution)/shard_map/ppermute | solution.py:224
  80.3 1.3 %collective-permute-done.15 = bf16[2,256,128]{2,1,0:T(8,128)(2,1)S(1)} collective-permute-done((bf16[2,256,128]{2,1,0:T(8,128)(2,1)S(1)}, bf16[2,256,128]{2,1,0:T(8,128)(2,1)S(1)}, u32[]{:S(2)}, u32[]{:S(2)}) %collective-permute-start.15) | collective-permute-done | bytes 131104 | tf_op jit(solution)/shard_map/ppermute | solution.py:223
  81.6 1.4 %collective-permute-start.13 = (bf16[256,128]{1,0:T(8,128)(2,1)S(1)}, bf16[256,128]{1,0:T(8,128)(2,1)S(1)}, u32[]{:S(2)}, u32[]{:S(2)}) collective-permute-start(bf16[256,128]{1,0:T(8,128)(2,1)S(1)} %fusion.37), channel_id=1, source_target_pairs={{0,2},{1,3},{2,0},{3,1},{4,6},{5,7},{6,4},{7,5},{8,10},{9,11},{10,... | collective-permute-start | bytes 196616 | tf_op jit(solution)/shard_map/ppermute | solution.py:224
  83.0 1.3 %collective-permute-done.18 = bf16[2,256,128]{2,1,0:T(8,128)(2,1)S(1)} collective-permute-done((bf16[2,256,128]{2,1,0:T(8,128)(2,1)S(1)}, bf16[2,256,128]{2,1,0:T(8,128)(2,1)S(1)}, u32[]{:S(2)}, u32[]{:S(2)}) %collective-permute-start.18) | collective-permute-done | bytes 131104 | tf_op jit(solution)/shard_map/ppermute | solution.py:223
  84.8 2.6 %collective-permute-start.19 = (bf16[256,128]{1,0:T(8,128)(2,1)S(1)}, bf16[256,128]{1,0:T(8,128)(2,1)S(1)}, u32[]{:S(2)}, u32[]{:S(2)}) collective-permute-start(bf16[256,128]{1,0:T(8,128)(2,1)S(1)} %fusion.41), channel_id=1, source_target_pairs={{0,2},{1,3},{2,0},{3,1},{4,6},{5,7},{6,4},{7,5},{8,10},{9,11},{10,... | collective-permute-start | bytes 196616 | tf_op jit(solution)/shard_map/ppermute | solution.py:224
  87.4 2.1 %collective-permute-done.10 = bf16[256,128]{1,0:T(8,128)(2,1)S(1)} collective-permute-done((bf16[256,128]{1,0:T(8,128)(2,1)S(1)}, bf16[256,128]{1,0:T(8,128)(2,1)S(1)}, u32[]{:S(2)}, u32[]{:S(2)}) %collective-permute-start.10) | collective-permute-done | bytes 65568 | tf_op jit(solution)/shard_map/ppermute | solution.py:224
  89.6 2.7 %collective-permute-done.13 = bf16[256,128]{1,0:T(8,128)(2,1)S(1)} collective-permute-done((bf16[256,128]{1,0:T(8,128)(2,1)S(1)}, bf16[256,128]{1,0:T(8,128)(2,1)S(1)}, u32[]{:S(2)}, u32[]{:S(2)}) %collective-permute-start.13) | collective-permute-done | bytes 65568 | tf_op jit(solution)/shard_map/ppermute | solution.py:224
  92.4 0.7 collective-permute-done.16
  93.8 0.7 fusion.40
  (54 shorter events, 4.2 us)
Async XLA Ops:
  0.0 7.7 %collective-permute-start = (s32[256,4]{0,1:T(4,128)}, s32[256,4]{0,1:T(4,128)S(1)}, u32[]{:S(2)}, u32[]{:S(2)}) collective-permute-start(s32[256,4]{0,1:T(4,128)} %param.7), channel_id=1, source_target_pairs={{0,4},{4,0},{1,5},{5,1},{2,6},{6,2},{3,7},{7,3},{8,12},{12,8},{9,1... | collective-permute-start | bytes 12296 | tf_op jit(solution)/shard_map/ppermute | solution.py:195
  3.0 3.8 %collective-permute-start.1 = (f32[256,4]{0,1:T(4,128)}, f32[256,4]{0,1:T(4,128)S(1)}, u32[]{:S(2)}, u32[]{:S(2)}) collective-permute-start(f32[256,4]{0,1:T(4,128)} %param.8), channel_id=1, source_target_pairs={{0,4},{4,0},{1,5},{5,1},{2,6},{6,2},{3,7},{7,3},{8,12},{12,8},{9,1... | collective-permute-start | bytes 12296 | tf_op jit(solution)/shard_map/ppermute | solution.py:196
  12.4 2.2 %copy-start = (bf16[8,2,96,1408]{3,2,1,0:T(8,128)(2,1)S(1)}, bf16[8,2,96,1408]{3,2,1,0:T(8,128)(2,1)}, u32[]{:S(2)}) copy-start(bf16[8,2,96,1408]{3,2,1,0:T(8,128)(2,1)} %refs_1_.1) | copy-start | bytes 12976132
  22.3 38.7 %collective-permute-start.2 = (bf16[4,256,128]{2,1,0:T(8,128)(2,1)S(1)}, bf16[4,256,128]{2,1,0:T(8,128)(2,1)S(1)}, u32[]{:S(2)}, u32[]{:S(2)}) collective-permute-start(bf16[4,256,128]{2,1,0:T(8,128)(2,1)S(1)} %get-tuple-element.24), channel_id=1, source_target_pairs={{0,4},{4,0},{1,5},{5,1},{2,6},{6,2},{3,7},{7,3},{8,12},{12,8},{9,1... | collective-permute-start | bytes 786440 | tf_op jit(solution)/shard_map/ppermute | solution.py:216
  29.4 33.7 %collective-permute-start.5 = (bf16[4,256,128]{2,1,0:T(8,128)(2,1)S(1)}, bf16[4,256,128]{2,1,0:T(8,128)(2,1)S(1)}, u32[]{:S(2)}, u32[]{:S(2)}) collective-permute-start(bf16[4,256,128]{2,1,0:T(8,128)(2,1)S(1)} %get-tuple-element.28), channel_id=1, source_target_pairs={{0,4},{4,0},{1,5},{5,1},{2,6},{6,2},{3,7},{7,3},{8,12},{12,8},{9,1... | collective-permute-start | bytes 786440 | tf_op jit(solution)/shard_map/ppermute | solution.py:216
  38.4 26.4 %collective-permute-start.8 = (bf16[4,256,128]{2,1,0:T(8,128)(2,1)S(1)}, bf16[4,256,128]{2,1,0:T(8,128)(2,1)S(1)}, u32[]{:S(2)}, u32[]{:S(2)}) collective-permute-start(bf16[4,256,128]{2,1,0:T(8,128)(2,1)S(1)} %get-tuple-element.31), channel_id=1, source_target_pairs={{0,4},{4,0},{1,5},{5,1},{2,6},{6,2},{3,7},{7,3},{8,12},{12,8},{9,1... | collective-permute-start | bytes 786440 | tf_op jit(solution)/shard_map/ppermute | solution.py:216
  45.6 19.8 %collective-permute-start.11 = (bf16[4,256,128]{2,1,0:T(8,128)(2,1)S(1)}, bf16[4,256,128]{2,1,0:T(8,128)(2,1)S(1)}, u32[]{:S(2)}, u32[]{:S(2)}) collective-permute-start(bf16[4,256,128]{2,1,0:T(8,128)(2,1)S(1)} %get-tuple-element.34), channel_id=1, source_target_pairs={{0,4},{4,0},{1,5},{5,1},{2,6},{6,2},{3,7},{7,3},{8,12},{12,8},{9,1... | collective-permute-start | bytes 786440 | tf_op jit(solution)/shard_map/ppermute | solution.py:216
  60.9 8.4 %collective-permute-start.14 = (bf16[4,256,128]{2,1,0:T(8,128)(2,1)S(1)}, bf16[4,256,128]{2,1,0:T(8,128)(2,1)S(1)}, u32[]{:S(2)}, u32[]{:S(2)}) collective-permute-start(bf16[4,256,128]{2,1,0:T(8,128)(2,1)S(1)} %get-tuple-element.37), channel_id=1, source_target_pairs={{0,4},{4,0},{1,5},{5,1},{2,6},{6,2},{3,7},{7,3},{8,12},{12,8},{9,1... | collective-permute-start | bytes 786440 | tf_op jit(solution)/shard_map/ppermute | solution.py:216
  61.0 11.1 %collective-permute-start.17 = (bf16[4,256,128]{2,1,0:T(8,128)(2,1)S(1)}, bf16[4,256,128]{2,1,0:T(8,128)(2,1)S(1)}, u32[]{:S(2)}, u32[]{:S(2)}) collective-permute-start(bf16[4,256,128]{2,1,0:T(8,128)(2,1)S(1)} %get-tuple-element.40), channel_id=1, source_target_pairs={{0,4},{4,0},{1,5},{5,1},{2,6},{6,2},{3,7},{7,3},{8,12},{12,8},{9,1... | collective-permute-start | bytes 786440 | tf_op jit(solution)/shard_map/ppermute | solution.py:216
  63.1 10.8 %collective-permute-start.3 = (bf16[2,256,128]{2,1,0:T(8,128)(2,1)S(1)}, bf16[2,256,128]{2,1,0:T(8,128)(2,1)S(1)}, u32[]{:S(2)}, u32[]{:S(2)}) collective-permute-start(bf16[2,256,128]{2,1,0:T(8,128)(2,1)S(1)} %get-tuple-element.52), channel_id=1, source_target_pairs={{0,1},{1,0},{2,3},{3,2},{4,5},{5,4},{6,7},{7,6},{8,9},{9,8},{10,11... | collective-permute-start | bytes 393224 | tf_op jit(solution)/shard_map/ppermute | solution.py:223
  64.8 9.5 %collective-permute-start.6 = (bf16[2,256,128]{2,1,0:T(8,128)(2,1)S(1)}, bf16[2,256,128]{2,1,0:T(8,128)(2,1)S(1)}, u32[]{:S(2)}, u32[]{:S(2)}) collective-permute-start(bf16[2,256,128]{2,1,0:T(8,128)(2,1)S(1)} %get-tuple-element.50), channel_id=1, source_target_pairs={{0,1},{1,0},{2,3},{3,2},{4,5},{5,4},{6,7},{7,6},{8,9},{9,8},{10,11... | collective-permute-start | bytes 393224 | tf_op jit(solution)/shard_map/ppermute | solution.py:223
  65.4 11.8 %collective-permute-start.9 = (bf16[2,256,128]{2,1,0:T(8,128)(2,1)S(1)}, bf16[2,256,128]{2,1,0:T(8,128)(2,1)S(1)}, u32[]{:S(2)}, u32[]{:S(2)}) collective-permute-start(bf16[2,256,128]{2,1,0:T(8,128)(2,1)S(1)} %get-tuple-element.48), channel_id=1, source_target_pairs={{0,1},{1,0},{2,3},{3,2},{4,5},{5,4},{6,7},{7,6},{8,9},{9,8},{10,11... | collective-permute-start | bytes 393224 | tf_op jit(solution)/shard_map/ppermute | solution.py:223
  69.3 9.3 %collective-permute-start.12 = (bf16[2,256,128]{2,1,0:T(8,128)(2,1)S(1)}, bf16[2,256,128]{2,1,0:T(8,128)(2,1)S(1)}, u32[]{:S(2)}, u32[]{:S(2)}) collective-permute-start(bf16[2,256,128]{2,1,0:T(8,128)(2,1)S(1)} %get-tuple-element.46), channel_id=1, source_target_pairs={{0,1},{1,0},{2,3},{3,2},{4,5},{5,4},{6,7},{7,6},{8,9},{9,8},{10,11... | collective-permute-start | bytes 393224 | tf_op jit(solution)/shard_map/ppermute | solution.py:223
  71.0 16.3 %copy-start.1 = (bf16[256,768]{1,0:T(8,128)(2,1)S(1)}, bf16[256,768]{1,0:T(8,128)(2,1)}, u32[]{:S(2)}) copy-start(bf16[256,768]{1,0:T(8,128)(2,1)} %param.9) | copy-start | bytes 1179652
  72.1 9.5 %collective-permute-start.15 = (bf16[2,256,128]{2,1,0:T(8,128)(2,1)S(1)}, bf16[2,256,128]{2,1,0:T(8,128)(2,1)S(1)}, u32[]{:S(2)}, u32[]{:S(2)}) collective-permute-start(bf16[2,256,128]{2,1,0:T(8,128)(2,1)S(1)} %get-tuple-element.44), channel_id=1, source_target_pairs={{0,1},{1,0},{2,3},{3,2},{4,5},{5,4},{6,7},{7,6},{8,9},{9,8},{10,11... | collective-permute-start | bytes 393224 | tf_op jit(solution)/shard_map/ppermute | solution.py:223
  73.9 10.4 %collective-permute-start.18 = (bf16[2,256,128]{2,1,0:T(8,128)(2,1)S(1)}, bf16[2,256,128]{2,1,0:T(8,128)(2,1)S(1)}, u32[]{:S(2)}, u32[]{:S(2)}) collective-permute-start(bf16[2,256,128]{2,1,0:T(8,128)(2,1)S(1)} %get-tuple-element.42), channel_id=1, source_target_pairs={{0,1},{1,0},{2,3},{3,2},{4,5},{5,4},{6,7},{7,6},{8,9},{9,8},{10,11... | collective-permute-start | bytes 393224 | tf_op jit(solution)/shard_map/ppermute | solution.py:223
  74.3 10.5 %collective-permute-start.4 = (bf16[256,128]{1,0:T(8,128)(2,1)S(1)}, bf16[256,128]{1,0:T(8,128)(2,1)S(1)}, u32[]{:S(2)}, u32[]{:S(2)}) collective-permute-start(bf16[256,128]{1,0:T(8,128)(2,1)S(1)} %fusion.31), channel_id=1, source_target_pairs={{0,2},{1,3},{2,0},{3,1},{4,6},{5,7},{6,4},{7,5},{8,10},{9,11},{10,... | collective-permute-start | bytes 196616 | tf_op jit(solution)/shard_map/ppermute | solution.py:224
  77.2 10.2 %collective-permute-start.7 = (bf16[256,128]{1,0:T(8,128)(2,1)S(1)}, bf16[256,128]{1,0:T(8,128)(2,1)S(1)}, u32[]{:S(2)}, u32[]{:S(2)}) collective-permute-start(bf16[256,128]{1,0:T(8,128)(2,1)S(1)} %fusion.33), channel_id=1, source_target_pairs={{0,2},{1,3},{2,0},{3,1},{4,6},{5,7},{6,4},{7,5},{8,10},{9,11},{10,... | collective-permute-start | bytes 196616 | tf_op jit(solution)/shard_map/ppermute | solution.py:224
  78.6 11.0 %collective-permute-start.10 = (bf16[256,128]{1,0:T(8,128)(2,1)S(1)}, bf16[256,128]{1,0:T(8,128)(2,1)S(1)}, u32[]{:S(2)}, u32[]{:S(2)}) collective-permute-start(bf16[256,128]{1,0:T(8,128)(2,1)S(1)} %fusion.35), channel_id=1, source_target_pairs={{0,2},{1,3},{2,0},{3,1},{4,6},{5,7},{6,4},{7,5},{8,10},{9,11},{10,... | collective-permute-start | bytes 196616 | tf_op jit(solution)/shard_map/ppermute | solution.py:224
  81.6 10.7 %collective-permute-start.13 = (bf16[256,128]{1,0:T(8,128)(2,1)S(1)}, bf16[256,128]{1,0:T(8,128)(2,1)S(1)}, u32[]{:S(2)}, u32[]{:S(2)}) collective-permute-start(bf16[256,128]{1,0:T(8,128)(2,1)S(1)} %fusion.37), channel_id=1, source_target_pairs={{0,2},{1,3},{2,0},{3,1},{4,6},{5,7},{6,4},{7,5},{8,10},{9,11},{10,... | collective-permute-start | bytes 196616 | tf_op jit(solution)/shard_map/ppermute | solution.py:224
  84.3 8.8 %collective-permute-start.16 = (bf16[256,128]{1,0:T(8,128)(2,1)S(1)}, bf16[256,128]{1,0:T(8,128)(2,1)S(1)}, u32[]{:S(2)}, u32[]{:S(2)}) collective-permute-start(bf16[256,128]{1,0:T(8,128)(2,1)S(1)} %fusion.39), channel_id=1, source_target_pairs={{0,2},{1,3},{2,0},{3,1},{4,6},{5,7},{6,4},{7,5},{8,10},{9,11},{10,... | collective-permute-start | bytes 196616 | tf_op jit(solution)/shard_map/ppermute | solution.py:224
  84.8 9.0 %collective-permute-start.19 = (bf16[256,128]{1,0:T(8,128)(2,1)S(1)}, bf16[256,128]{1,0:T(8,128)(2,1)S(1)}, u32[]{:S(2)}, u32[]{:S(2)}) collective-permute-start(bf16[256,128]{1,0:T(8,128)(2,1)S(1)} %fusion.41), channel_id=1, source_target_pairs={{0,2},{1,3},{2,0},{3,1},{4,6},{5,7},{6,4},{7,5},{8,10},{9,11},{10,... | collective-permute-start | bytes 196616 | tf_op jit(solution)/shard_map/ppermute | solution.py:224
  93.1 0.7 copy-start.2

commit v2 on v0

v2 whole, which is shorter than its diff:
```python
import functools

import jax
import jax.numpy as jnp
from jax import lax
from jax.experimental import pallas as pl
from jax.experimental.pallas import tpu as pltpu
from jax.sharding import PartitionSpec as P

LANES = 128
AHEAD = 2
BLOCKS = (3, 1, 2, 0)
WIDTHS = (1, 2, 2, 1)

VMEM = pl.BlockSpec(memory_space=pltpu.VMEM)
SMEM = pl.BlockSpec(memory_space=pltpu.SMEM)
ANY = pl.BlockSpec(memory_space=pl.ANY)
HBM = pl.BlockSpec(memory_space=pltpu.HBM)
BF16 = jnp.bfloat16


def strips(ids_ref, weight_ref, chunk, expert, target, sems):
    start, width, features = chunk
    rank = ids_ref[1]
    copies = []
    for q, flip in enumerate(BLOCKS):
        at = pl.multiple_of(lax.bitwise_xor(rank, flip) * features + start, LANES)
        source = weight_ref.at[expert, :, pl.ds(at, width)]
        copies.append(pltpu.make_async_copy(source, target.at[:, pl.ds(q * width, width)], sems.at[q]))
    return copies


def product(rows_ref, weight, partial, expert):
    sources, capacity, depth = rows_ref.shape
    rows = rows_ref[...].reshape(sources * capacity, depth)
    value = jnp.dot(rows, weight, preferred_element_type=jnp.float32).astype(partial.dtype)
    for source in range(sources):
        partial[source, expert * capacity : (expert + 1) * capacity, :] = value[
            source * capacity : (source + 1) * capacity
        ]


def combine(ids_ref, table_ref, partial, outs):
    sources = table_ref.shape[0]
    width = partial.shape[2] // len(BLOCKS)
    mine = ids_ref[0]
    pair = len(outs) == 2
    order = [(outs[0], 1 - mine), (outs[1], mine)] if pair else [(outs[0].at[s], s) for s in range(sources)]
    for out_ref, source in order:
        total = jnp.dot(table_ref[source], partial[source], preferred_element_type=jnp.float32)
        total = total.astype(out_ref.dtype)
        for q in range(len(BLOCKS)):
            out_ref[q] = total[:, q * width : (q + 1) * width]


def first_kernel(chunk, ids_ref, hidden_ref, weight_ref, partial, stay_ref, weights, sems, hidden_sems):
    local = hidden_ref.shape[0]

    def bring(expert):
        copy = pltpu.make_async_copy(hidden_ref.at[expert], stay_ref.at[expert], hidden_sems.at[expert])
        return [copy] + strips(ids_ref, weight_ref, chunk, expert, weights.at[expert], sems.at[expert])

    for expert in range(local):
        for copy in bring(expert):
            copy.start()
    for expert in range(local):
        for copy in bring(expert):
            copy.wait()
        product(stay_ref.at[expert], weights[expert], partial, expert)


def table_kernel(chunk, capacity, groups, *refs):
    refs = list(refs)
    ids_ref, partial, weight_ref = refs[:3]
    routes_refs, score_refs = refs[3 : 3 + groups], refs[3 + groups : 3 + 2 * groups]
    table_ref, *outs, next_ref, next_sems = refs[3 + 2 * groups :]
    sources, tokens, width = table_ref.shape
    local = width // capacity
    f32 = jnp.float32
    mine = ids_ref[0]
    first = mine * local
    copies = [
        strips(ids_ref, weight_ref, chunk, expert, next_ref.at[expert], next_sems.at[expert])
        for expert in range(next_ref.shape[0])
    ]
    for copy in sum(copies, []):
        copy.start()

    rows = lax.broadcasted_iota(jnp.int32, (tokens, tokens), 0)
    cols = lax.broadcasted_iota(jnp.int32, (tokens, tokens), 1)
    earlier = (rows < cols).astype(f32).astype(BF16)
    if groups == 2:
        parts = [(routes_refs[1][...], score_refs[1][...], 1 - mine), (routes_refs[0][...], score_refs[0][...], mine)]
    else:
        parts = [(routes_refs[0][s], score_refs[0][s], s) for s in range(sources)]
    for routes, score, source in parts:
        top = routes.shape[0]
        share = score / jnp.sum(score, axis=0, keepdims=True)
        experts = lax.broadcasted_iota(jnp.int32, (LANES // 8, tokens), 0)
        matches = [(experts == routes[k : k + 1]).astype(f32) for k in range(top)]
        onehot = functools.reduce(jnp.add, matches)
        before = jnp.dot(onehot.astype(BF16), earlier, preferred_element_type=f32)
        places = lax.broadcasted_iota(jnp.int32, (width, tokens), 0)
        entry = jnp.zeros((width, tokens), f32)
        for k in range(top):
            slot = jnp.sum(matches[k] * before, axis=0, keepdims=True).astype(jnp.int32)
            expert = routes[k : k + 1] - first
            at = jnp.where((expert >= 0) & (expert < local), expert * capacity + slot, -1)
            entry = jnp.where(places == at, share[k : k + 1], entry)
        table_ref[source] = entry.T.astype(table_ref.dtype)
    combine(ids_ref, table_ref, partial, outs)
    for copy in sum(copies, []):
        copy.wait()


def chunk_kernel(chunk, following, pair, ids_ref, hidden_ref, weight_ref, table_ref, held_ref, *refs):
    refs = list(refs[1:])
    outs = [refs.pop(0) for _ in range(2 if pair else 1)]
    next_ref = refs.pop(0) if following else None
    weights, partial, sems, next_sems = refs
    local, ahead = hidden_ref.shape[0], held_ref.shape[0]

    def bring(expert):
        at = expert - ahead
        return strips(ids_ref, weight_ref, chunk, expert, weights.at[at], sems.at[at])

    def bring_next(expert):
        return strips(ids_ref, weight_ref, following, expert, next_ref.at[expert], next_sems.at[expert])

    for expert in range(ahead, local):
        for copy in bring(expert):
            copy.start()
    if following:
        for expert in range(ahead):
            for copy in bring_next(expert):
                copy.start()
    for expert in range(local):
        if expert >= ahead:
            for copy in bring(expert):
                copy.wait()
            product(hidden_ref.at[expert], weights[expert - ahead], partial, expert)
        else:
            product(hidden_ref.at[expert], held_ref[expert], partial, expert)
    combine(ids_ref, table_ref, partial, outs)
    if following:
        for expert in range(ahead):
            for copy in bring_next(expert):
                copy.wait()


def shape(*dims):
    return jax.ShapeDtypeStruct(dims, BF16)


def cost(flops, *arrays):
    return pl.CostEstimate(flops=flops, bytes_accessed=sum(2 * a for a in arrays), transcendentals=0)


def first_products(chunk, ids, hidden, weight):
    local, sources, capacity, depth = hidden.shape
    columns = len(BLOCKS) * chunk[1]
    rows = local * sources * capacity
    return pl.pallas_call(
        functools.partial(first_kernel, chunk),
        in_specs=[SMEM, HBM, HBM],
        out_specs=[VMEM] * 2,
        out_shape=[shape(sources, local * capacity, columns), shape(*hidden.shape)],
        scratch_shapes=[
            pltpu.VMEM((local, depth, columns), BF16),
            pltpu.SemaphoreType.DMA((local, len(BLOCKS))),
            pltpu.SemaphoreType.DMA((local,)),
        ],
        cost_estimate=cost(2 * rows * depth * columns, local * depth * columns, rows * depth),
        compiler_params=pltpu.CompilerParams(vmem_limit_bytes=48 << 20),
        name="first",
    )(ids, hidden, weight)


def group_shapes(pair, sources, tokens, width):
    group = (len(BLOCKS), tokens, width)
    return [shape(*group)] * 2 if pair else [shape(sources, *group)]


def tables(chunk, following, pair, ids, partial, weight, routes, scores, capacity):
    sources, width, columns = partial.shape
    tokens = routes[0].shape[-1]
    depth = weight.shape[1]
    ahead = min(AHEAD, width // capacity)
    outs = group_shapes(pair, sources, tokens, chunk[1])
    table, *sums, held = pl.pallas_call(
        functools.partial(table_kernel, following, capacity, len(routes)),
        in_specs=[SMEM, VMEM, HBM] + [VMEM] * (2 * len(routes)),
        out_specs=[VMEM] * (len(outs) + 2),
        out_shape=[shape(sources, tokens, width)] + outs + [shape(ahead, depth, len(BLOCKS) * following[1])],
        scratch_shapes=[pltpu.SemaphoreType.DMA((ahead, len(BLOCKS)))],
        cost_estimate=cost(2 * sources * tokens * width * columns, ahead * depth * columns),
        compiler_params=pltpu.CompilerParams(vmem_limit_bytes=24 << 20),
        name="tables",
    )(ids, partial, weight, *routes, *scores)
    return table, sums, held


def chunk_sums(chunk, following, pair, ids, hidden, weight, table, held, after):
    local, sources, capacity, depth = hidden.shape
    tokens = table.shape[1]
    columns = len(BLOCKS) * chunk[1]
    ahead = held.shape[0]
    brought = max(local - ahead, 1)
    outs = group_shapes(pair, sources, tokens, chunk[1])
    groups = len(outs)
    if following:
        outs.append(shape(ahead, depth, len(BLOCKS) * following[1]))
    rows = sources * local * capacity
    results = pl.pallas_call(
        functools.partial(chunk_kernel, chunk, following, pair),
        in_specs=[SMEM, VMEM, HBM, VMEM, VMEM, ANY],
        out_specs=[VMEM] * len(outs),
        out_shape=outs,
        scratch_shapes=[
            pltpu.VMEM((brought, depth, columns), BF16),
            pltpu.VMEM((sources, local * capacity, columns), BF16),
            pltpu.SemaphoreType.DMA((brought, len(BLOCKS))),
            pltpu.SemaphoreType.DMA((ahead, len(BLOCKS))),
        ],
        cost_estimate=cost(2 * rows * columns * (depth + tokens), local * depth * columns),
        compiler_params=pltpu.CompilerParams(vmem_limit_bytes=28 << 20),
        name="chunk",
    )(ids, hidden, weight, table, held, after)
    return results[:groups], results[groups] if following else None


def on_device(experts, ranks, hidden, down_weight, routes, route_weight, residual):
    f32 = jnp.float32
    capacity = hidden.shape[2]
    tokens, features = residual.shape
    pair = experts == 2
    ids = jnp.stack([lax.axis_index("expert"), lax.axis_index("tp")]).astype(jnp.int32)
    routes, scores = routes.T, route_weight.T
    swap = [(0, 1), (1, 0)]
    if pair:
        all_routes = [routes, lax.ppermute(routes, "expert", swap)]
        all_scores = [scores, lax.ppermute(scores, "expert", swap)]
    else:
        all_routes = [lax.all_gather(routes, "expert")]
        all_scores = [lax.all_gather(scores, "expert")]

    near = [(i, i ^ 1) for i in range(ranks)]
    far = [(i, i ^ 2) for i in range(ranks)]
    chunks, start = [], 0
    for width in WIDTHS:
        chunks.append((start, width * LANES, features))
        start += width * LANES
    partial, hidden = first_products(chunks[0], ids, hidden, down_weight)
    table, sums, held = tables(
        chunks[0], chunks[1], pair, ids, partial, down_weight, all_routes, all_scores, capacity
    )
    pieces, sent = [], []
    for i, (start, width, _) in enumerate(chunks):
        if i:
            following = chunks[i + 1] if i + 1 < len(chunks) else None
            after = sent[i - 2] if i > 1 else ids
            sums, held = chunk_sums(chunks[i], following, pair, ids, hidden, down_weight, table, held, after)
        if pair:
            other, own = sums
            got = lax.ppermute(other, "expert", swap)
            send = (own[:2].astype(f32) + got[:2].astype(f32)).astype(BF16)
            base = own[2:].astype(f32) + got[2:].astype(f32)
        else:
            whole = lax.psum_scatter(sums[0], "expert", scatter_dimension=0, tiled=True)
            whole = jnp.moveaxis(whole, 0, 1).reshape(len(BLOCKS), tokens, width)
            send, base = whole[:2], whole[2:].astype(f32)
        sent.append(send)
        near_got = lax.ppermute(send, "tp", near).astype(f32)
        far_got = lax.ppermute((base[0] + near_got[0]).astype(BF16), "tp", far).astype(f32)
        here = residual[:, start : start + width].astype(f32)
        pieces.append((here + (base[1] + near_got[1] + far_got)).astype(BF16))
    return jnp.concatenate(pieces, axis=1)


def solution(mesh):
    return jax.shard_map(
        functools.partial(on_device, mesh.shape["expert"], mesh.shape["tp"]),
        mesh=mesh,
        in_specs=(
            P("expert", "dp", None, "tp"),
            P("expert", "tp", None),
            P(("dp", "expert"), None),
            P(("dp", "expert"), None),
            P(("dp", "expert"), "tp"),
        ),
        out_specs=P(("dp", "expert"), "tp"),
        check_vma=False,
    )
```

time: 245 us -> 81.5 us (0.33)
  waiting for transfers between devices: 140 us -> 22 us
  Pallas kernels: 0 us -> 41.5 us
  local copies, waits for them, and re-layouts: 38.5 us -> 0.01 us
  matrix products: 30 us -> 0 us
  other arithmetic: 14.9 us -> 1.6 us
  between operations: 13.5 us -> 0.2 us
  starting transfers between devices: 7.48 us -> 16.1 us
    all_to_all x1 -> x0, waiting for transfers between devices: 104 us -> none  [on_device(): lax.all_to_all(partial_value, 'expert', split_axis=0, concat_axis=1, tile...]
    pallas_call x0 -> x5, Pallas kernels: none -> 41.5 us  [the longest x3 28.3 us: chunk_sums(): pl.pallas_call(functools.partial(chunk_kernel, chunk, following, pair), i...]
    reduce_scatter x1 -> x0, waiting for transfers between devices: 35.9 us -> none  [on_device(): lax.psum_scatter(mixed_part.astype(jnp.bfloat16), 'tp', scatter_dimension...]
    dot_general x1 -> x0, matrix products: 30 us -> none  [on_device(): jnp.einsum('lsch,lhd->slcd', hidden, down_weight, preferred_element_type=...]
    ppermute x0 -> x14, waiting for transfers between devices: none -> 22 us  [the longest x4 9.89 us: on_device(): near_got = lax.ppermute(send, 'tp', near).astype(f32)]
    convert_element_type x2 -> x0, local copies, waits for them, and re-layouts: 20.7 us -> none  [the longest x1 12.2 us: combine(): flattened[slot_index].astype(jnp.float32)]
    gather x1 -> x0, local copies, waits for them, and re-layouts: 17.1 us -> none  [combine(): flattened[slot_index].astype(jnp.float32)]
    ppermute x0 -> x14, starting transfers between devices: none -> 16.1 us  [the longest x4 5.75 us: on_device(): lax.ppermute((base[0] + near_got[0]).astype(BF16), 'tp', far).astype(f32)]
  transfers between devices with their start and end apart: 2 -> 14, of which waited for: 2 -> 6; matrix products, arithmetic and copies ran while one was open for 1% -> 1% of each run, Pallas kernels for 0% -> 45%
where the time goes in v2:
time: 81.5 us; the launch traced here: 81.3 us
  Pallas kernels  41.5 us (51%)
  waiting for transfers between devices  22 us (27%)
  starting transfers between devices  16.1 us (20%)
  other arithmetic  1.6 us (2%)
    pallas_call x3, Pallas kernels, chunk_sums(): pl.pallas_call(functools.partial(chunk_kernel, chunk, following, pair), i...  28.3 us
    ppermute x4, waiting for transfers between devices, on_device(): near_got = lax.ppermute(send, 'tp', near).astype(f32)  9.89 us
    pallas_call x1, Pallas kernels, first_products(): pl.pallas_call(functools.partial(first_kernel, chunk), in_specs=[SMEM, HB...  8.68 us
    ppermute x4, waiting for transfers between devices, on_device(): got = lax.ppermute(other, 'expert', swap)  6.13 us
    ppermute x4, waiting for transfers between devices, on_device(): lax.ppermute((base[0] + near_got[0]).astype(BF16), 'tp', far).astype(f32)  5.94 us
    ppermute x4, starting transfers between devices, on_device(): lax.ppermute((base[0] + near_got[0]).astype(BF16), 'tp', far).astype(f32)  5.75 us
    pallas_call x1, Pallas kernels, tables(): pl.pallas_call(functools.partial(table_kernel, following, capacity, len(r...  4.55 us
    ppermute x4, starting transfers between devices, on_device(): got = lax.ppermute(other, 'expert', swap)  4.33 us
  transfers between devices with their start and end apart: 14, of which 6 were waited for; matrix products, arithmetic and copies ran while one was open for 1% of the time, Pallas kernels for 45%

profile of v2, /device:TPU:0, one launch (start us, length us, event | category | flops | bytes accessed | tf_op | source)
XLA Modules:
  0.0 81.3 jit_solution(7096466381679156968)
XLA Ops:
  0.0 3.0 %collective-permute-start = (s32[4,256]{1,0:T(4,128)}, s32[4,256]{1,0:T(4,128)S(1)}, u32[]{:S(2)}, u32[]{:S(2)}) collective-permute-start(s32[4,256]{1,0:T(4,128)} %bitcast.44), channel_id=1, source_target_pairs={{0,4},{4,0},{1,5},{5,1},{2,6},{6,2},{3,7},{7,3},{8,12},{12,8},{9,1... | collective-permute-start | bytes 12296 | tf_op jit(solution)/shard_map/ppermute | solution.py:241
  3.0 0.1 pad_add_fusion.ids_ref.refs_0_
  3.1 8.7 %first.1 = (bf16[2,768,512]{2,1,0:T(8,128)(2,1)S(1)}, bf16[8,2,96,1408]{3,2,1,0:T(8,128)(2,1)S(1)}) custom-call(s32[2]{0:T(128)S(1)} %pad_add_fusion.ids_ref.refs_0_, bf16[8,2,96,1408]{3,2,1,0:T(8,128)(2,1)} %hidden_ref.1, bf16[8,1408,3072]{2,1,0:T(8,128)(2,1)} %weight_ref.7), custom_call_target="tpu_custom_call" | custom-call | flops 2214592512 | bytes 15859712 | tf_op jit(solution)/shard_map/first/pallas_call | solution.py:163
  11.8 4.6 %tables.1 = (bf16[2,256,768]{2,1,0:T(8,128)(2,1)S(1)}, bf16[4,256,128]{2,1,0:T(8,128)(2,1)S(1)}, bf16[4,256,128]{2,1,0:T(8,128)(2,1)S(1)}, bf16[2,1408,1024]{2,1,0:T(8,128)(2,1)S(1)}) custom-call(s32[2]{0:T(128)S(1)} %pad_add_fusion.ids_ref.refs_0_, bf16[2,768,512]{2,1,0:T(8,128)(2,1)S(1)} %get-tuple-element.19.refs_1_, bf16[8,1408,3072]{2,1,0:T(8,128)(2,1)} %weight_ref.7, ...), custom_call_target="tpu_custom_call" | custom-call | flops 402653184 | bytes 2883584 | tf_op jit(solution)/shard_map/tables/pallas_call | solution.py:190
  16.4 2.1 %collective-permute-start.2 = (bf16[4,256,128]{2,1,0:T(8,128)(2,1)S(1)}, bf16[4,256,128]{2,1,0:T(8,128)(2,1)S(1)}, u32[]{:S(2)}, u32[]{:S(2)}) collective-permute-start(bf16[4,256,128]{2,1,0:T(8,128)(2,1)S(1)} %get-tuple-element.21), channel_id=1, source_target_pairs={{0,4},{4,0},{1,5},{5,1},{2,6},{6,2},{3,7},{7,3},{8,12},{12,8},{9,1... | collective-permute-start | bytes 786440 | tf_op jit(solution)/shard_map/ppermute | solution.py:265
  18.4 11.4 %chunk.3 = (bf16[4,256,256]{2,1,0:T(8,128)(2,1)S(1)}, bf16[4,256,256]{2,1,0:T(8,128)(2,1)S(1)}, bf16[2,1408,1024]{2,1,0:T(8,128)(2,1)S(1)}) custom-call(s32[2]{0:T(128)S(1)} %pad_add_fusion.ids_ref.refs_0_, bf16[8,2,96,1408]{3,2,1,0:T(8,128)(2,1)S(1)} %get-tuple-element.22.hidden_ref, bf16[8,1408,3072]{2,1,0:T(8,128)(2,1)} %weight_ref.7, ...), custom_call_target="tpu_custom_call" | custom-call | flops 5234491392 | bytes 23068672 | tf_op jit(solution)/shard_map/chunk/pallas_call | solution.py:214
  29.8 0.1 collective-permute-start.5
  29.9 0.1 convert_add_fusion.3
  30.0 2.1 %collective-permute-start.3 = (bf16[2,256,128]{2,1,0:T(8,128)(2,1)S(1)}, bf16[2,256,128]{2,1,0:T(8,128)(2,1)S(1)}, u32[]{:S(2)}, u32[]{:S(2)}) collective-permute-start(bf16[2,256,128]{2,1,0:T(8,128)(2,1)S(1)} %get-tuple-element.38.refs_0_), channel_id=1, source_target_pairs={{0,1},{1,0},{2,3},{3,2},{4,5},{5,4},{6,7},{7,6},{8,9},{9,8},{10,11... | collective-permute-start | bytes 393224 | tf_op jit(solution)/shard_map/ppermute | solution.py:273
  32.0 10.8 %chunk.4 = (bf16[4,256,256]{2,1,0:T(8,128)(2,1)S(1)}, bf16[4,256,256]{2,1,0:T(8,128)(2,1)S(1)}, bf16[2,1408,512]{2,1,0:T(8,128)(2,1)S(1)}) custom-call(s32[2]{0:T(128)S(1)} %pad_add_fusion.ids_ref.refs_0_, bf16[8,2,96,1408]{3,2,1,0:T(8,128)(2,1)S(1)} %get-tuple-element.22.hidden_ref, bf16[8,1408,3072]{2,1,0:T(8,128)(2,1)} %weight_ref.7, ...), custom_call_target="tpu_custom_call" | custom-call | flops 5234491392 | bytes 23068672 | tf_op jit(solution)/shard_map/chunk/pallas_call | solution.py:214
  42.8 1.6 %collective-permute-start.8 = (bf16[4,256,256]{2,1,0:T(8,128)(2,1)S(1)}, bf16[4,256,256]{2,1,0:T(8,128)(2,1)S(1)}, u32[]{:S(2)}, u32[]{:S(2)}) collective-permute-start(bf16[4,256,256]{2,1,0:T(8,128)(2,1)S(1)} %get-tuple-element.29), channel_id=1, source_target_pairs={{0,4},{4,0},{1,5},{5,1},{2,6},{6,2},{3,7},{7,3},{8,12},{12,8},{9,1... | collective-permute-start | bytes 1572872 | tf_op jit(solution)/shard_map/ppermute | solution.py:265
  44.4 0.1 convert_add_fusion.1
  44.6 6.1 %chunk.5 = (bf16[4,256,128]{2,1,0:T(8,128)(2,1)S(1)}, bf16[4,256,128]{2,1,0:T(8,128)(2,1)S(1)}) custom-call(s32[2]{0:T(128)S(1)} %pad_add_fusion.ids_ref.refs_0_, bf16[8,2,96,1408]{3,2,1,0:T(8,128)(2,1)S(1)} %get-tuple-element.22.hidden_ref, bf16[8,1408,3072]{2,1,0:T(8,128)(2,1)} %weight_ref.7, bf16[2,256,768]{2,1,0:T(8,128)(2,1)S(1)} %get-tuple-element.23.table_ref, ...), custom_call_target="tpu_custom_call" | custom-call | flops 2617245696 | bytes 11534336 | tf_op jit(solution)/shard_map/chunk/pallas_call | solution.py:214
  50.7 0.6 collective-permute-start.11
  51.3 2.6 %collective-permute-start.4 = (bf16[256,128]{1,0:T(8,128)(2,1)S(1)}, bf16[256,128]{1,0:T(8,128)(2,1)S(1)}, u32[]{:S(2)}, u32[]{:S(2)}) collective-permute-start(bf16[256,128]{1,0:T(8,128)(2,1)S(1)} %fusion.22), channel_id=1, source_target_pairs={{0,2},{1,3},{2,0},{3,1},{4,6},{5,7},{6,4},{7,5},{8,10},{9,11},{10,... | collective-permute-start | bytes 196616 | tf_op jit(solution)/shard_map/ppermute | solution.py:274
  53.9 0.5 collective-permute-start.6
  54.4 3.3 %collective-permute-done.8 = bf16[4,256,256]{2,1,0:T(8,128)(2,1)S(1)} collective-permute-done((bf16[4,256,256]{2,1,0:T(8,128)(2,1)S(1)}, bf16[4,256,256]{2,1,0:T(8,128)(2,1)S(1)}, u32[]{:S(2)}, u32[]{:S(2)}) %collective-permute-start.8) | collective-permute-done | bytes 524320 | tf_op jit(solution)/shard_map/ppermute | solution.py:265
  57.8 0.1 convert_add_fusion
  57.9 0.1 collective-permute-start.9
  58.0 2.8 %collective-permute-done.11 = bf16[4,256,128]{2,1,0:T(8,128)(2,1)S(1)} collective-permute-done((bf16[4,256,128]{2,1,0:T(8,128)(2,1)S(1)}, bf16[4,256,128]{2,1,0:T(8,128)(2,1)S(1)}, u32[]{:S(2)}, u32[]{:S(2)}) %collective-permute-start.11) | collective-permute-done | bytes 262176 | tf_op jit(solution)/shard_map/ppermute | solution.py:265
  60.8 0.1 convert_add_fusion.2
  60.8 0.3 collective-permute-start.12
  61.2 3.4 %collective-permute-done.6 = bf16[2,256,256]{2,1,0:T(8,128)(2,1)S(1)} collective-permute-done((bf16[2,256,256]{2,1,0:T(8,128)(2,1)S(1)}, bf16[2,256,256]{2,1,0:T(8,128)(2,1)S(1)}, u32[]{:S(2)}, u32[]{:S(2)}) %collective-permute-start.6) | collective-permute-done | bytes 262176 | tf_op jit(solution)/shard_map/ppermute | solution.py:273
  64.7 0.1 collective-permute-start.7
  64.8 6.5 %collective-permute-done.12 = bf16[2,256,128]{2,1,0:T(8,128)(2,1)S(1)} collective-permute-done((bf16[2,256,128]{2,1,0:T(8,128)(2,1)S(1)}, bf16[2,256,128]{2,1,0:T(8,128)(2,1)S(1)}, u32[]{:S(2)}, u32[]{:S(2)}) %collective-permute-start.12) | collective-permute-done | bytes 131104 | tf_op jit(solution)/shard_map/ppermute | solution.py:273
  71.3 0.1 collective-permute-start.13
  71.5 3.0 %collective-permute-start.10 = (bf16[256,256]{1,0:T(8,128)(2,1)S(1)}, bf16[256,256]{1,0:T(8,128)(2,1)S(1)}, u32[]{:S(2)}, u32[]{:S(2)}) collective-permute-start(bf16[256,256]{1,0:T(8,128)(2,1)S(1)} %fusion.11), channel_id=1, source_target_pairs={{0,2},{1,3},{2,0},{3,1},{4,6},{5,7},{6,4},{7,5},{8,10},{9,11},{10,... | collective-permute-start | bytes 393224 | tf_op jit(solution)/shard_map/ppermute | solution.py:274
  74.4 3.2 %collective-permute-done.13 = bf16[256,128]{1,0:T(8,128)(2,1)S(1)} collective-permute-done((bf16[256,128]{1,0:T(8,128)(2,1)S(1)}, bf16[256,128]{1,0:T(8,128)(2,1)S(1)}, u32[]{:S(2)}, u32[]{:S(2)}) %collective-permute-start.13) | collective-permute-done | bytes 65568 | tf_op jit(solution)/shard_map/ppermute | solution.py:274
  77.6 0.1 fusion.21
  77.7 2.7 %collective-permute-done.10 = bf16[256,256]{1,0:T(8,128)(2,1)S(1)} collective-permute-done((bf16[256,256]{1,0:T(8,128)(2,1)S(1)}, bf16[256,256]{1,0:T(8,128)(2,1)S(1)}, u32[]{:S(2)}, u32[]{:S(2)}) %collective-permute-start.10) | collective-permute-done | bytes 131104 | tf_op jit(solution)/shard_map/ppermute | solution.py:274
  80.4 0.1 fusion.9
  80.5 0.8 pad_maximum_fusion
  (23 shorter events, 0.3 us)
Async XLA Ops:
  0.0 11.8 %collective-permute-start = (s32[4,256]{1,0:T(4,128)}, s32[4,256]{1,0:T(4,128)S(1)}, u32[]{:S(2)}, u32[]{:S(2)}) collective-permute-start(s32[4,256]{1,0:T(4,128)} %bitcast.44), channel_id=1, source_target_pairs={{0,4},{4,0},{1,5},{5,1},{2,6},{6,2},{3,7},{7,3},{8,12},{12,8},{9,1... | collective-permute-start | bytes 12296 | tf_op jit(solution)/shard_map/ppermute | solution.py:241
  3.0 8.8 %collective-permute-start.1 = (f32[4,256]{1,0:T(4,128)}, f32[4,256]{1,0:T(4,128)S(1)}, u32[]{:S(2)}, u32[]{:S(2)}) collective-permute-start(f32[4,256]{1,0:T(4,128)} %bitcast.46), channel_id=1, source_target_pairs={{0,4},{4,0},{1,5},{5,1},{2,6},{6,2},{3,7},{7,3},{8,12},{12,8},{9,1... | collective-permute-start | bytes 12296 | tf_op jit(solution)/shard_map/ppermute | solution.py:242
  3.1 8.7 %copy-start = (s32[256,4]{0,1:T(4,128)S(1)}, s32[256,4]{0,1:T(4,128)}, u32[]{:S(2)}) copy-start(s32[256,4]{0,1:T(4,128)} %param.7) | copy-start | bytes 12292
  3.1 8.7 %copy-start.1 = (f32[256,4]{0,1:T(4,128)S(1)}, f32[256,4]{0,1:T(4,128)}, u32[]{:S(2)}) copy-start(f32[256,4]{0,1:T(4,128)} %param.8) | copy-start | bytes 12292
  16.4 13.5 %collective-permute-start.2 = (bf16[4,256,128]{2,1,0:T(8,128)(2,1)S(1)}, bf16[4,256,128]{2,1,0:T(8,128)(2,1)S(1)}, u32[]{:S(2)}, u32[]{:S(2)}) collective-permute-start(bf16[4,256,128]{2,1,0:T(8,128)(2,1)S(1)} %get-tuple-element.21), channel_id=1, source_target_pairs={{0,4},{4,0},{1,5},{5,1},{2,6},{6,2},{3,7},{7,3},{8,12},{12,8},{9,1... | collective-permute-start | bytes 786440 | tf_op jit(solution)/shard_map/ppermute | solution.py:265
  29.8 14.6 %collective-permute-start.5 = (bf16[4,256,256]{2,1,0:T(8,128)(2,1)S(1)}, bf16[4,256,256]{2,1,0:T(8,128)(2,1)S(1)}, u32[]{:S(2)}, u32[]{:S(2)}) collective-permute-start(bf16[4,256,256]{2,1,0:T(8,128)(2,1)S(1)} %get-tuple-element.26), channel_id=1, source_target_pairs={{0,4},{4,0},{1,5},{5,1},{2,6},{6,2},{3,7},{7,3},{8,12},{12,8},{9,1... | collective-permute-start | bytes 1572872 | tf_op jit(solution)/shard_map/ppermute | solution.py:265
  30.0 14.4 %collective-permute-start.3 = (bf16[2,256,128]{2,1,0:T(8,128)(2,1)S(1)}, bf16[2,256,128]{2,1,0:T(8,128)(2,1)S(1)}, u32[]{:S(2)}, u32[]{:S(2)}) collective-permute-start(bf16[2,256,128]{2,1,0:T(8,128)(2,1)S(1)} %get-tuple-element.38.refs_0_), channel_id=1, source_target_pairs={{0,1},{1,0},{2,3},{3,2},{4,5},{5,4},{6,7},{7,6},{8,9},{9,8},{10,11... | collective-permute-start | bytes 393224 | tf_op jit(solution)/shard_map/ppermute | solution.py:273
  42.8 14.9 %collective-permute-start.8 = (bf16[4,256,256]{2,1,0:T(8,128)(2,1)S(1)}, bf16[4,256,256]{2,1,0:T(8,128)(2,1)S(1)}, u32[]{:S(2)}, u32[]{:S(2)}) collective-permute-start(bf16[4,256,256]{2,1,0:T(8,128)(2,1)S(1)} %get-tuple-element.29), channel_id=1, source_target_pairs={{0,4},{4,0},{1,5},{5,1},{2,6},{6,2},{3,7},{7,3},{8,12},{12,8},{9,1... | collective-permute-start | bytes 1572872 | tf_op jit(solution)/shard_map/ppermute | solution.py:265
  50.7 27.0 %copy-start.2 = (bf16[256,768]{1,0:T(8,128)(2,1)S(1)}, bf16[256,768]{1,0:T(8,128)(2,1)}, u32[]{:S(2)}) copy-start(bf16[256,768]{1,0:T(8,128)(2,1)} %param.9) | copy-start | bytes 1179652
  50.7 10.1 %collective-permute-start.11 = (bf16[4,256,128]{2,1,0:T(8,128)(2,1)S(1)}, bf16[4,256,128]{2,1,0:T(8,128)(2,1)S(1)}, u32[]{:S(2)}, u32[]{:S(2)}) collective-permute-start(bf16[4,256,128]{2,1,0:T(8,128)(2,1)S(1)} %get-tuple-element.32), channel_id=1, source_target_pairs={{0,4},{4,0},{1,5},{5,1},{2,6},{6,2},{3,7},{7,3},{8,12},{12,8},{9,1... | collective-permute-start | bytes 786440 | tf_op jit(solution)/shard_map/ppermute | solution.py:265
  51.3 23.1 %collective-permute-start.4 = (bf16[256,128]{1,0:T(8,128)(2,1)S(1)}, bf16[256,128]{1,0:T(8,128)(2,1)S(1)}, u32[]{:S(2)}, u32[]{:S(2)}) collective-permute-start(bf16[256,128]{1,0:T(8,128)(2,1)S(1)} %fusion.22), channel_id=1, source_target_pairs={{0,2},{1,3},{2,0},{3,1},{4,6},{5,7},{6,4},{7,5},{8,10},{9,11},{10,... | collective-permute-start | bytes 196616 | tf_op jit(solution)/shard_map/ppermute | solution.py:274
  53.9 10.7 %collective-permute-start.6 = (bf16[2,256,256]{2,1,0:T(8,128)(2,1)S(1)}, bf16[2,256,256]{2,1,0:T(8,128)(2,1)S(1)}, u32[]{:S(2)}, u32[]{:S(2)}) collective-permute-start(bf16[2,256,256]{2,1,0:T(8,128)(2,1)S(1)} %get-tuple-element.34.refs_0_), channel_id=1, source_target_pairs={{0,1},{1,0},{2,3},{3,2},{4,5},{5,4},{6,7},{7,6},{8,9},{9,8},{10,11... | collective-permute-start | bytes 786440 | tf_op jit(solution)/shard_map/ppermute | solution.py:273
  57.9 13.5 %collective-permute-start.9 = (bf16[2,256,256]{2,1,0:T(8,128)(2,1)S(1)}, bf16[2,256,256]{2,1,0:T(8,128)(2,1)S(1)}, u32[]{:S(2)}, u32[]{:S(2)}) collective-permute-start(bf16[2,256,256]{2,1,0:T(8,128)(2,1)S(1)} %get-tuple-element.36), channel_id=1, source_target_pairs={{0,1},{1,0},{2,3},{3,2},{4,5},{5,4},{6,7},{7,6},{8,9},{9,8},{10,11... | collective-permute-start | bytes 786440 | tf_op jit(solution)/shard_map/ppermute | solution.py:273
  60.8 10.4 %collective-permute-start.12 = (bf16[2,256,128]{2,1,0:T(8,128)(2,1)S(1)}, bf16[2,256,128]{2,1,0:T(8,128)(2,1)S(1)}, u32[]{:S(2)}, u32[]{:S(2)}) collective-permute-start(bf16[2,256,128]{2,1,0:T(8,128)(2,1)S(1)} %get-tuple-element.40), channel_id=1, source_target_pairs={{0,1},{1,0},{2,3},{3,2},{4,5},{5,4},{6,7},{7,6},{8,9},{9,8},{10,11... | collective-permute-start | bytes 393224 | tf_op jit(solution)/shard_map/ppermute | solution.py:273
  64.7 13.0 %collective-permute-start.7 = (bf16[256,256]{1,0:T(8,128)(2,1)S(1)}, bf16[256,256]{1,0:T(8,128)(2,1)S(1)}, u32[]{:S(2)}, u32[]{:S(2)}) collective-permute-start(bf16[256,256]{1,0:T(8,128)(2,1)S(1)} %fusion.10), channel_id=1, source_target_pairs={{0,2},{1,3},{2,0},{3,1},{4,6},{5,7},{6,4},{7,5},{8,10},{9,11},{10,... | collective-permute-start | bytes 393224 | tf_op jit(solution)/shard_map/ppermute | solution.py:274
  71.3 6.3 %collective-permute-start.13 = (bf16[256,128]{1,0:T(8,128)(2,1)S(1)}, bf16[256,128]{1,0:T(8,128)(2,1)S(1)}, u32[]{:S(2)}, u32[]{:S(2)}) collective-permute-start(bf16[256,128]{1,0:T(8,128)(2,1)S(1)} %fusion.23), channel_id=1, source_target_pairs={{0,2},{1,3},{2,0},{3,1},{4,6},{5,7},{6,4},{7,5},{8,10},{9,11},{10,... | collective-permute-start | bytes 196616 | tf_op jit(solution)/shard_map/ppermute | solution.py:274
  71.5 9.0 %collective-permute-start.10 = (bf16[256,256]{1,0:T(8,128)(2,1)S(1)}, bf16[256,256]{1,0:T(8,128)(2,1)S(1)}, u32[]{:S(2)}, u32[]{:S(2)}) collective-permute-start(bf16[256,256]{1,0:T(8,128)(2,1)S(1)} %fusion.11), channel_id=1, source_target_pairs={{0,2},{1,3},{2,0},{3,1},{4,6},{5,7},{6,4},{7,5},{8,10},{9,11},{10,... | collective-permute-start | bytes 393224 | tf_op jit(solution)/shard_map/ppermute | solution.py:274

commit v3 on v0

v3 whole, which is shorter than its diff:
```python
import functools

import jax
import jax.numpy as jnp
from jax import lax
from jax.experimental import pallas as pl
from jax.experimental.pallas import tpu as pltpu
from jax.sharding import PartitionSpec as P

LANES = 128
TILE = 256
AHEAD = 2
WINDOW = 4
CHUNKS = (((3, 0, 3),), ((2, 0, 3), (1, 0, 1)), ((1, 1, 3), (0, 0, 1)), ((0, 1, 3),))

LATE = 10**10

VMEM = pl.BlockSpec(memory_space=pltpu.VMEM)
SMEM = pl.BlockSpec(memory_space=pltpu.SMEM)
ANY = pl.BlockSpec(memory_space=pl.ANY)
HBM = pl.BlockSpec(memory_space=pltpu.HBM)
BF16 = jnp.bfloat16


class Strips:
    def __init__(self, ids_ref, weight_ref, chunk, expert, target, sem):
        self.rank, self.weight_ref, self.chunk = ids_ref[1], weight_ref.at[expert], chunk
        self.target, self.sem = target, sem

    def start(self):
        column = 0
        for block, start, stop, features in self.chunk:
            at = pl.multiple_of(lax.bitwise_xor(self.rank, block) * features + start, LANES)
            target = self.target.at[:, pl.ds(column, stop - start)]
            pltpu.make_async_copy(self.weight_ref.at[:, pl.ds(at, stop - start)], target, self.sem).start()
            column += stop - start

    def wait(self):
        pltpu.make_async_copy(self.weight_ref.at[:, pl.ds(0, self.target.shape[1])], self.target, self.sem).wait()


def columns_of(chunk):
    return sum(stop - start for _, start, stop, _ in chunk)


def balanced_dot(rows, weight_ref, finish):
    depth, width = weight_ref.shape
    even = width // TILE // 2 * 2 * TILE
    half = -(-depth // 2 // TILE) * TILE
    if width - even != TILE or half >= depth:
        even = width
    f32 = jnp.float32
    finish(0, even, jnp.dot(rows, weight_ref[:, :even], preferred_element_type=f32))
    if even < width:
        low = jnp.dot(rows[:, :half], weight_ref[:half, even:], preferred_element_type=f32)
        high = jnp.dot(rows[:, half:], weight_ref[half:, even:], preferred_element_type=f32)
        finish(even, width, low + high)


def product(rows_ref, weight_ref, partial, expert):
    sources, capacity, depth = rows_ref.shape

    def finish(start, stop, value):
        value = value.astype(partial.dtype)
        for source in range(sources):
            partial[source, expert * capacity : (expert + 1) * capacity, start:stop] = value[
                source * capacity : (source + 1) * capacity
            ]

    balanced_dot(rows_ref[...].reshape(sources * capacity, depth), weight_ref, finish)


def combine(ids_ref, table_refs, partial, outs):
    mine = ids_ref[0]
    if len(outs) == 2:
        order = [(outs[0], table_refs[0], 1 - mine), (outs[1], table_refs[1], mine)]
    else:
        order = [(outs[0].at[s], table_refs[0].at[s], s) for s in range(partial.shape[0])]
    for out_ref, table_ref, source in order:

        def finish(start, stop, value, out_ref=out_ref):
            out_ref[:, start:stop] = value.astype(out_ref.dtype)

        balanced_dot(table_ref[...], partial.at[source], finish)


def share_table(ids_ref, routes, score, local, capacity):
    f32 = jnp.float32
    top, tokens = routes.shape
    width = local * capacity
    first = ids_ref[0] * local
    rows = lax.broadcasted_iota(jnp.int32, (tokens, tokens), 0)
    cols = lax.broadcasted_iota(jnp.int32, (tokens, tokens), 1)
    earlier = (rows < cols).astype(f32).astype(BF16)
    share = score / jnp.sum(score, axis=0, keepdims=True)
    experts = lax.broadcasted_iota(jnp.int32, (LANES // 8, tokens), 0)
    matches = [(experts == routes[k : k + 1]).astype(f32) for k in range(top)]
    onehot = functools.reduce(jnp.add, matches)
    before = jnp.dot(onehot.astype(BF16), earlier, preferred_element_type=f32)
    places = lax.broadcasted_iota(jnp.int32, (width, tokens), 0)
    entry = jnp.zeros((width, tokens), f32)
    for k in range(top):
        slot = jnp.sum(matches[k] * before, axis=0, keepdims=True).astype(jnp.int32)
        expert = routes[k : k + 1] - first
        at = jnp.where((expert >= 0) & (expert < local), expert * capacity + slot, -1)
        entry = jnp.where(places == at, share[k : k + 1], entry)
    return entry.T.astype(BF16)


class Stream:
    def __init__(self, groups):
        self.groups, self.begun, self.ended = groups, 0, 0
        for _ in range(WINDOW):
            self.begin()

    def begin(self):
        if self.begun < len(self.groups):
            for copy in self.groups[self.begun]:
                copy.start()
            self.begun += 1

    def end(self):
        for copy in self.groups[self.ended]:
            copy.wait()
        self.ended += 1
        self.begin()

    def finish(self):
        while self.ended < len(self.groups):
            self.end()


def first_kernel(chunk, ids_ref, hidden_ref, weight_ref, partial, stay_ref, weights, sems, hidden_sems):
    def bring(expert):
        copy = pltpu.make_async_copy(hidden_ref.at[expert], stay_ref.at[expert], hidden_sems.at[expert])
        return [copy, Strips(ids_ref, weight_ref, chunk, expert, weights.at[expert], sems.at[expert])]

    local = hidden_ref.shape[0]
    stream = Stream([bring(expert) for expert in range(local)])
    for expert in range(local):
        stream.end()
        product(stay_ref.at[expert], weights.at[expert], partial, expert)


def table_kernel(chunk, pair, capacity, *refs):
    refs = list(refs)
    ids_ref, partial, weight_ref = refs[:3]
    count = 2 if pair else 1
    routes_refs, score_refs, table_refs = refs[3 : 3 + count], refs[3 + count : 3 + 2 * count], refs[3 + 2 * count :]
    outs, (next_ref, next_sems) = table_refs[count:-2], table_refs[-2:]
    table_refs = table_refs[:count]
    local = table_refs[0].shape[-1] // capacity
    stream = Stream(
        [
            [Strips(ids_ref, weight_ref, chunk, expert, next_ref.at[expert], next_sems.at[expert])]
            for expert in range(next_ref.shape[0])
        ]
    )
    for routes_ref, score_ref, table_ref in zip(routes_refs, score_refs, table_refs):
        if pair:
            table_ref[...] = share_table(ids_ref, routes_ref[...], score_ref[...], local, capacity)
        else:
            for s in range(table_ref.shape[0]):
                table_ref[s] = share_table(ids_ref, routes_ref[s], score_ref[s], local, capacity)
    combine(ids_ref, table_refs, partial, outs)
    stream.finish()


def chunk_kernel(chunk, following, groups, ids_ref, hidden_ref, weight_ref, held_ref, *refs):
    refs = list(refs)
    table_refs = [refs.pop(0) for _ in range(groups)]
    del refs[0]
    outs = [refs.pop(0) for _ in range(groups)]
    next_ref = refs.pop(0) if following else None
    weights, partial, sems, next_sems = refs
    local, ahead = hidden_ref.shape[0], held_ref.shape[0]

    own = [
        [Strips(ids_ref, weight_ref, chunk, e, weights.at[e - ahead], sems.at[e - ahead])]
        for e in range(ahead, local)
    ]
    later = [
        [Strips(ids_ref, weight_ref, following, e, next_ref.at[e], next_sems.at[e])]
        for e in range(ahead if following else 0)
    ]
    stream = Stream(own + later)
    for expert in range(local):
        if expert >= ahead:
            stream.end()
            product(hidden_ref.at[expert], weights.at[expert - ahead], partial, expert)
        else:
            product(hidden_ref.at[expert], held_ref.at[expert], partial, expert)
    combine(ids_ref, table_refs, partial, outs)
    stream.finish()


def fold_kernel(spans, *refs):
    *terms, _, sum_ref = refs
    edges = sorted({edge for _, at, width in spans for edge in (at, at + width)})
    for low, high in zip(edges[:-1], edges[1:]):
        parts = [
            term[:, source + low - at : source + high - at].astype(jnp.float32)
            for term, (source, at, width) in zip(terms, spans)
            if at <= low < at + width
        ]
        sum_ref[:, low:high] = functools.reduce(jnp.add, parts).astype(sum_ref.dtype)


def shape(*dims):
    return jax.ShapeDtypeStruct(dims, BF16)


def cost(flops, count):
    return pl.CostEstimate(flops=flops, bytes_accessed=2 * count, transcendentals=0)


COST = cost(1000, 1000)


def first_products(chunk, ids, hidden, weight):
    local, sources, capacity, depth = hidden.shape
    columns = columns_of(chunk)
    return pl.pallas_call(
        functools.partial(first_kernel, chunk),
        in_specs=[SMEM, HBM, HBM],
        out_specs=[VMEM] * 2,
        out_shape=[shape(sources, local * capacity, columns), shape(*hidden.shape)],
        scratch_shapes=[
            pltpu.VMEM((local, depth, columns), BF16),
            pltpu.SemaphoreType.DMA((local,)),
            pltpu.SemaphoreType.DMA((local,)),
        ],
        cost_estimate=cost(2 * sources * local * capacity * columns * depth, local * depth * columns),
        compiler_params=pltpu.CompilerParams(vmem_limit_bytes=46 << 20),
        name="first",
    )(ids, hidden, weight)


def group_shapes(pair, sources, tokens, width):
    return [shape(tokens, width)] * 2 if pair else [shape(sources, tokens, width)]


def tables(following, ids, partial, weight, routes, scores, capacity):
    sources, width, columns = partial.shape
    pair = len(routes) == 2
    tokens = routes[0].shape[-1]
    depth = weight.shape[1]
    ahead = min(AHEAD, width // capacity)
    table = [shape(tokens, width)] * 2 if pair else [shape(sources, tokens, width)]
    outs = group_shapes(pair, sources, tokens, columns)
    results = pl.pallas_call(
        functools.partial(table_kernel, following, pair, capacity),
        in_specs=[SMEM, VMEM, HBM] + [VMEM] * (2 * len(routes)),
        out_specs=[VMEM] * (len(table) + len(outs) + 1),
        out_shape=table + outs + [shape(ahead, depth, columns_of(following))],
        scratch_shapes=[pltpu.SemaphoreType.DMA((ahead,))],
        cost_estimate=COST,
        compiler_params=pltpu.CompilerParams(vmem_limit_bytes=12 << 20),
        name="tables",
    )(ids, partial, weight, *routes, *scores)
    return results[: len(table)], results[len(table) : -1], results[-1]


def chunk_sums(chunk, following, ids, hidden, weight, table, held, after):
    local, sources, capacity, depth = hidden.shape
    tokens = table[0].shape[-2]
    ahead, _, columns = held.shape
    brought = max(local - ahead, 1)
    groups = len(table)
    outs = group_shapes(groups == 2, sources, tokens, columns)
    if following:
        outs.append(shape(ahead, depth, columns_of(following)))
    flops = 2 * sources * local * capacity * columns * (depth + tokens)
    results = pl.pallas_call(
        functools.partial(chunk_kernel, chunk, following, groups),
        in_specs=[SMEM, VMEM, HBM, VMEM] + [VMEM] * groups + [ANY],
        out_specs=[VMEM] * len(outs),
        out_shape=outs,
        scratch_shapes=[
            pltpu.VMEM((brought, depth, columns), BF16),
            pltpu.VMEM((sources, local * capacity, columns), BF16),
            pltpu.SemaphoreType.DMA((brought,)),
            pltpu.SemaphoreType.DMA((ahead,)),
        ],
        cost_estimate=cost(flops, local * depth * columns) if following else COST,
        compiler_params=pltpu.CompilerParams(vmem_limit_bytes=28 << 20),
        name="chunk",
    )(ids, hidden, weight, held, *table, after)
    return results[:groups], results[groups] if following else None


def fold(width, terms, after, dtype=BF16, flops=1000):
    arrays, spans = [term[0] for term in terms], [term[1:] for term in terms]
    return pl.pallas_call(
        functools.partial(fold_kernel, spans),
        in_specs=[VMEM] * len(terms) + [ANY],
        out_specs=VMEM,
        out_shape=jax.ShapeDtypeStruct((arrays[0].shape[0], width), dtype),
        cost_estimate=cost(flops, 1000),
        compiler_params=pltpu.CompilerParams(vmem_limit_bytes=6 << 20),
        name="fold",
    )(*arrays, after)


def on_device(experts, ranks, hidden, down_weight, routes, route_weight, residual):
    f32 = jnp.float32
    capacity = hidden.shape[2]
    tokens, features = residual.shape
    pair = experts == 2
    ids = jnp.stack([lax.axis_index("expert"), lax.axis_index("tp")]).astype(jnp.int32)
    routes, scores = routes.T, route_weight.T
    swap = [(0, 1), (1, 0)]
    if pair:
        routes, scores = [lax.ppermute(routes, "expert", swap), routes], [lax.ppermute(scores, "expert", swap), scores]
    else:
        routes, scores = [lax.all_gather(routes, "expert")], [lax.all_gather(scores, "expert")]

    chunks = [
        tuple((block, start * features // 3, stop * features // 3, features) for block, start, stop in chunk)
        for chunk in CHUNKS
    ]
    over, along = [], {}

    def send_over(sums):
        if pair:
            over.append([sums[1], lax.ppermute(sums[0], "expert", swap)])
        else:
            whole = lax.psum_scatter(sums[0], "expert", scatter_dimension=0, tiled=True)
            over.append([whole.reshape(tokens, -1)])

    def terms(i, block, base):
        column = 0
        for which, start, stop, _ in chunks[i]:
            if which == block:
                found = [(array, column, start - base, stop - start) for array in over[i]]
                for array, first, width in along.get(block, []):
                    low, high = max(start, first), min(stop, first + width)
                    if low < high:
                        found.append((array, low - first, low - base, high - low))
                return found
            column += stop - start

    def send_along(i, block, flip, after):
        start, stop = next((start, stop) for which, start, stop, _ in chunks[i] if which == block)
        total = fold(stop - start, terms(i, block, start), after)
        got = lax.ppermute(total, "tp", [(r, r ^ flip) for r in range(ranks)])
        along.setdefault(block ^ flip, []).append((got, start, stop - start))
        return total

    partial, hidden = first_products(chunks[0], ids, hidden, down_weight)
    table, sums, held = tables(chunks[1], ids, partial, down_weight, routes, scores, capacity)
    send_over(sums)
    sums, held = chunk_sums(chunks[1], chunks[2], ids, hidden, down_weight, table, held, ids)
    send_over(sums)
    total = send_along(0, 3, 1, sums[0])
    sums, held = chunk_sums(chunks[2], chunks[3], ids, hidden, down_weight, table, held, total)
    send_over(sums)
    total = send_along(1, 2, 2, sums[0])
    total = send_along(1, 1, 1, total)
    sums, _ = chunk_sums(chunks[3], None, ids, hidden, down_weight, table, held, total)
    send_over(sums)
    send_along(2, 1, 1, sums[0])
    far, near, last = [(array, 0, first, width) for array, first, width in along[0]]
    here = [(residual, 0, 0, features)]
    rest = fold(features, here + [far, near] + [(a, c, at, w) for a, c, at, w in terms(2, 0, 0)[: len(over[2])]], ids, f32, LATE)
    rest = fold(features, [(rest, 0, 0, features)] + terms(3, 0, 0)[: len(over[3])], ids, f32, LATE)
    return fold(features, [(rest, 0, 0, features), last], ids)


def solution(mesh):
    return jax.shard_map(
        functools.partial(on_device, mesh.shape["expert"], mesh.shape["tp"]),
        mesh=mesh,
        in_specs=(
            P("expert", "dp", None, "tp"),
            P("expert", "tp", None),
            P(("dp", "expert"), None),
            P(("dp", "expert"), None),
            P(("dp", "expert"), "tp"),
        ),
        out_specs=P(("dp", "expert"), "tp"),
        check_vma=False,
    )
```

time: 245 us -> 63.8 us (0.26)
  waiting for transfers between devices: 140 us -> 10.7 us
  local copies, waits for them, and re-layouts: 38.5 us -> 0.01 us
  Pallas kernels: 0 us -> 37.9 us
  matrix products: 30 us -> 0 us
  other arithmetic: 14.9 us -> 0.07 us
  between operations: 13.5 us -> 0.12 us
  starting transfers between devices: 7.48 us -> 14.9 us
    all_to_all x1 -> x0, waiting for transfers between devices: 104 us -> none  [on_device(): lax.all_to_all(partial_value, 'expert', split_axis=0, concat_axis=1, tile...]
    pallas_call x0 -> x12, Pallas kernels: none -> 37.9 us  [the longest x3 23.2 us: chunk_sums(): pl.pallas_call(functools.partial(chunk_kernel, chunk, following, groups),...]
    reduce_scatter x1 -> x0, waiting for transfers between devices: 35.9 us -> none  [on_device(): lax.psum_scatter(mixed_part.astype(jnp.bfloat16), 'tp', scatter_dimension...]
    dot_general x1 -> x0, matrix products: 30 us -> none  [on_device(): jnp.einsum('lsch,lhd->slcd', hidden, down_weight, preferred_element_type=...]
    convert_element_type x2 -> x0, local copies, waits for them, and re-layouts: 20.7 us -> none  [the longest x1 12.2 us: combine(): flattened[slot_index].astype(jnp.float32)]
    gather x1 -> x0, local copies, waits for them, and re-layouts: 17.1 us -> none  [combine(): flattened[slot_index].astype(jnp.float32)]
    ppermute x0 -> x10, starting transfers between devices: none -> 14.9 us  [the longest x4 8.07 us: send_along(): got = lax.ppermute(total, 'tp', [(r, r ^ flip) for r in range(ranks)])]
    reduce_sum x4 -> x0, other arithmetic: 12.3 us -> none  [the longest x1 12.2 us: combine(): return jnp.sum(share[:, :, None] * picked, axis=1)]
  transfers between devices with their start and end apart: 2 -> 10, of which waited for: 2 -> 5; matrix products, arithmetic and copies ran while one was open for 1% -> 0% of each run, Pallas kernels for 0% -> 51%
where the time goes in v3:
time: 63.8 us; the launch traced here: 63.7 us
  Pallas kernels  37.9 us (59%)
  starting transfers between devices  14.9 us (23%)
  waiting for transfers between devices  10.7 us (17%)
    pallas_call x3, Pallas kernels, chunk_sums(): pl.pallas_call(functools.partial(chunk_kernel, chunk, following, groups),...  23.2 us
    pallas_call x1, Pallas kernels, first_products(): pl.pallas_call(functools.partial(first_kernel, chunk), in_specs=[SMEM, HB...  8.94 us
    ppermute x4, waiting for transfers between devices, send_along(): got = lax.ppermute(total, 'tp', [(r, r ^ flip) for r in range(ranks)])  8.82 us
    ppermute x4, starting transfers between devices, send_along(): got = lax.ppermute(total, 'tp', [(r, r ^ flip) for r in range(ranks)])  8.07 us
    pallas_call x1, Pallas kernels, tables(): pl.pallas_call(functools.partial(table_kernel, following, pair, capacity)...  4.47 us
    ppermute x4, starting transfers between devices, send_over(): over.append([sums[1], lax.ppermute(sums[0], 'expert', swap)])  3.8 us
    ppermute x1, starting transfers between devices, on_device(): lax.ppermute(routes, 'expert', swap)  2.97 us
    ppermute x4, waiting for transfers between devices, send_over(): over.append([sums[1], lax.ppermute(sums[0], 'expert', swap)])  1.83 us
  transfers between devices with their start and end apart: 10, of which 5 were waited for; matrix products, arithmetic and copies ran while one was open for 0% of the time, Pallas kernels for 51%

profile of v3, /device:TPU:0, one launch (start us, length us, event | category | flops | bytes accessed | tf_op | source)
XLA Modules:
  0.0 63.7 jit_solution(238677230329666266)
XLA Ops:
  0.0 3.0 %collective-permute-start = (s32[4,256]{1,0:T(4,128)}, s32[4,256]{1,0:T(4,128)S(1)}, u32[]{:S(2)}, u32[]{:S(2)}) collective-permute-start(s32[4,256]{1,0:T(4,128)} %bitcast.4), channel_id=1, source_target_pairs={{0,4},{4,0},{1,5},{5,1},{2,6},{6,2},{3,7},{7,3},{8,12},{12,8},{9,1... | collective-permute-start | bytes 12296 | tf_op jit(solution)/shard_map/ppermute | solution.py:314
  3.0 0.0 collective-permute-start.1
  3.0 0.1 pad_add_fusion.ids_ref.refs_0_.refs_2_.refs_5_.refs_3_
  3.1 8.9 %first.1 = (bf16[2,768,768]{2,1,0:T(8,128)(2,1)S(1)}, bf16[8,2,96,1408]{3,2,1,0:T(8,128)(2,1)S(1)}) custom-call(s32[2]{0:T(128)S(1)} %pad_add_fusion.ids_ref.refs_0_.refs_2_.refs_5_.refs_3_, bf16[8,2,96,1408]{3,2,1,0:T(8,128)(2,1)} %hidden_ref.1, bf16[8,1408,3072]{2,1,0:T(8,128)(2,1)} %weight_ref.7), custom_call_target="tpu_custom_call" | custom-call | flops 3321888768 | bytes 17301504 | tf_op jit(solution)/shard_map/first/pallas_call | solution.py:223
  12.0 0.0 collective-permute-done.refs_3_
  12.0 0.0 collective-permute-done.1.refs_5_
  12.1 4.5 %tables.1 = (bf16[256,768]{1,0:T(8,128)(2,1)S(1)}, bf16[256,768]{1,0:T(8,128)(2,1)S(1)}, bf16[256,768]{1,0:T(8,128)(2,1)S(1)}, bf16[256,768]{1,0:T(8,128)(2,1)S(1)}, bf16[2,1408,1024]{2,1,0:T(8,128)(2,1)S(1)}) custom-call(s32[2]{0:T(128)S(1)} %pad_add_fusion.ids_ref.refs_0_.refs_2_.refs_5_.refs_3_, bf16[2,768,768]{2,1,0:T(8,128)(2,1)S(1)} %get-tuple-element.21.refs_1_, ...), custom_call_target="tpu_custom_call" | custom-call | flops 1000 | bytes 2000 | tf_op jit(solution)/shard_map/tables/pallas_call | solution.py:251
  16.5 2.0 %collective-permute-start.3 = (bf16[256,768]{1,0:T(8,128)(2,1)S(1)}, bf16[256,768]{1,0:T(8,128)(2,1)S(1)}, u32[]{:S(2)}, u32[]{:S(2)}) collective-permute-start(bf16[256,768]{1,0:T(8,128)(2,1)S(1)} %get-tuple-element.28), channel_id=1, source_target_pairs={{0,4},{4,0},{1,5},{5,1},{2,6},{6,2},{3,7},{7,3},{8,12},{12,8},{9,1... | collective-permute-start | bytes 1179656 | tf_op jit(solution)/shard_map/ppermute | solution.py:326
  18.6 8.7 %chunk.3 = (bf16[256,1024]{1,0:T(8,128)(2,1)S(1)}, bf16[256,1024]{1,0:T(8,128)(2,1)S(1)}, bf16[2,1408,768]{2,1,0:T(8,128)(2,1)S(1)}) custom-call(s32[2]{0:T(128)S(1)} %pad_add_fusion.ids_ref.refs_0_.refs_2_.refs_5_.refs_3_, bf16[8,2,96,1408]{3,2,1,0:T(8,128)(2,1)S(1)} %get-tuple-element.20.hidden_ref, bf16[8,1408,3072]{2,1,0:T(8,128)(2,1)} %weight_ref.7, ...), custom_call_target="tpu_custom_call" | custom-call | flops 5234491392 | bytes 23068672 | tf_op jit(solution)/shard_map/chunk/pallas_call | solution.py:274
  27.3 0.1 collective-permute-start.2
  27.4 0.0 collective-permute-done.3.refs_1_
  27.4 0.1 fold.7.refs_2_
  27.5 2.2 %collective-permute-start.4 = (bf16[256,768]{1,0:T(8,128)(2,1)S(1)}, bf16[256,768]{1,0:T(8,128)(2,1)S(1)}, u32[]{:S(2)}, u32[]{:S(2)}) collective-permute-start(bf16[256,768]{1,0:T(8,128)(2,1)S(1)} %fold.7.refs_2_), channel_id=1, source_target_pairs={{0,1},{1,0},{2,3},{3,2},{4,5},{5,4},{6,7},{7,6},{8,9},{9,8},{10,11... | collective-permute-start | bytes 1179656 | tf_op jit(solution)/shard_map/ppermute | solution.py:346
  29.7 8.4 %chunk.4 = (bf16[256,768]{1,0:T(8,128)(2,1)S(1)}, bf16[256,768]{1,0:T(8,128)(2,1)S(1)}, bf16[2,1408,512]{2,1,0:T(8,128)(2,1)S(1)}) custom-call(s32[2]{0:T(128)S(1)} %pad_add_fusion.ids_ref.refs_0_.refs_2_.refs_5_.refs_3_, bf16[8,2,96,1408]{3,2,1,0:T(8,128)(2,1)S(1)} %get-tuple-element.20.hidden_ref, bf16[8,1408,3072]{2,1,0:T(8,128)(2,1)} %weight_ref.7, ...), custom_call_target="tpu_custom_call" | custom-call | flops 3925868544 | bytes 17301504 | tf_op jit(solution)/shard_map/chunk/pallas_call | solution.py:274
  38.1 1.6 %collective-permute-start.7 = (bf16[256,768]{1,0:T(8,128)(2,1)S(1)}, bf16[256,768]{1,0:T(8,128)(2,1)S(1)}, u32[]{:S(2)}, u32[]{:S(2)}) collective-permute-start(bf16[256,768]{1,0:T(8,128)(2,1)S(1)} %get-tuple-element.30.refs_3_), channel_id=1, source_target_pairs={{0,4},{4,0},{1,5},{5,1},{2,6},{6,2},{3,7},{7,3},{8,12},{12,8},{9,1... | collective-permute-start | bytes 1179656 | tf_op jit(solution)/shard_map/ppermute | solution.py:326
  39.7 1.4 %collective-permute-done.2.refs_1_ = bf16[256,1024]{1,0:T(8,128)(2,1)S(1)} collective-permute-done((bf16[256,1024]{1,0:T(8,128)(2,1)S(1)}, bf16[256,1024]{1,0:T(8,128)(2,1)S(1)}, u32[]{:S(2)}, u32[]{:S(2)}) %collective-permute-start.2) | collective-permute-done | bytes 524320 | tf_op jit(solution)/shard_map/ppermute | solution.py:326
  41.1 0.0 collective-permute-done.4.refs_2_
  41.1 0.1 fold.8.refs_2_
  41.2 2.6 %collective-permute-start.5 = (bf16[256,768]{1,0:T(8,128)(2,1)S(1)}, bf16[256,768]{1,0:T(8,128)(2,1)S(1)}, u32[]{:S(2)}, u32[]{:S(2)}) collective-permute-start(bf16[256,768]{1,0:T(8,128)(2,1)S(1)} %fold.8.refs_2_), channel_id=1, source_target_pairs={{0,2},{1,3},{2,0},{3,1},{4,6},{5,7},{6,4},{7,5},{8,10},{9,11},{10,... | collective-permute-start | bytes 1179656 | tf_op jit(solution)/shard_map/ppermute | solution.py:346
  43.8 3.2 %collective-permute-start.6 = (bf16[256,256]{1,0:T(8,128)(2,1)S(1)}, bf16[256,256]{1,0:T(8,128)(2,1)S(1)}, u32[]{:S(2)}, u32[]{:S(2)}) collective-permute-start(bf16[256,256]{1,0:T(8,128)(2,1)S(1)} %fold.9.refs_2_), channel_id=1, source_target_pairs={{0,1},{1,0},{2,3},{3,2},{4,5},{5,4},{6,7},{7,6},{8,9},{9,8},{10,11... | collective-permute-start | bytes 393224 | tf_op jit(solution)/shard_map/ppermute | solution.py:346
  47.0 6.0 %chunk.5 = (bf16[256,512]{1,0:T(8,128)(2,1)S(1)}, bf16[256,512]{1,0:T(8,128)(2,1)S(1)}) custom-call(s32[2]{0:T(128)S(1)} %pad_add_fusion.ids_ref.refs_0_.refs_2_.refs_5_.refs_3_, bf16[8,2,96,1408]{3,2,1,0:T(8,128)(2,1)S(1)} %get-tuple-element.20.hidden_ref, bf16[8,1408,3072]{2,1,0:T(8,128)(2,1)} %weight_ref.7, ...), custom_call_target="tpu_custom_call" | custom-call | flops 1000 | bytes 2000 | tf_op jit(solution)/shard_map/chunk/pallas_call | solution.py:274
  53.1 0.1 collective-permute-start.8
  53.2 0.0 collective-permute-done.7.refs_4_.refs_1_
  53.2 0.1 fold.12
  53.3 0.1 collective-permute-start.9
  53.4 2.0 %collective-permute-done.6.refs_2_ = bf16[256,256]{1,0:T(8,128)(2,1)S(1)} collective-permute-done((bf16[256,256]{1,0:T(8,128)(2,1)S(1)}, bf16[256,256]{1,0:T(8,128)(2,1)S(1)}, u32[]{:S(2)}, u32[]{:S(2)}) %collective-permute-start.6) | collective-permute-done | bytes 131104 | tf_op jit(solution)/shard_map/ppermute | solution.py:346
  55.3 3.6 %collective-permute-done.5.refs_1_ = bf16[256,768]{1,0:T(8,128)(2,1)S(1)} collective-permute-done((bf16[256,768]{1,0:T(8,128)(2,1)S(1)}, bf16[256,768]{1,0:T(8,128)(2,1)S(1)}, u32[]{:S(2)}, u32[]{:S(2)}) %collective-permute-start.5) | collective-permute-done | bytes 393248 | tf_op jit(solution)/shard_map/ppermute | solution.py:346
  58.9 0.1 fold.10.refs_0_
  59.1 0.5 collective-permute-done.8.refs_2_
  59.5 0.1 fold.11.refs_0_
  59.6 3.2 %collective-permute-done.9.refs_1_ = bf16[256,512]{1,0:T(8,128)(2,1)S(1)} collective-permute-done((bf16[256,512]{1,0:T(8,128)(2,1)S(1)}, bf16[256,512]{1,0:T(8,128)(2,1)S(1)}, u32[]{:S(2)}, u32[]{:S(2)}) %collective-permute-start.9) | collective-permute-done | bytes 262176 | tf_op jit(solution)/shard_map/ppermute | solution.py:346
  62.9 0.8 %fold.13 = bf16[256,768]{1,0:T(8,128)(2,1)} custom-call(f32[256,768]{1,0:T(8,128)S(1)} %fold.11.refs_0_, bf16[256,512]{1,0:T(8,128)(2,1)S(1)} %collective-permute-done.9.refs_1_, s32[2]{0:T(128)S(1)} %pad_add_fusion.ids_ref.refs_0_.refs_2_.refs_5_.refs_3_), custom_call_target="tpu_custom_call" | custom-call | flops 1000 | bytes 2000 | tf_op jit(solution)/shard_map/fold/pallas_call | solution.py:294
  (7 shorter events, 0.0 us)
Async XLA Ops:
  0.0 12.0 %collective-permute-start = (s32[4,256]{1,0:T(4,128)}, s32[4,256]{1,0:T(4,128)S(1)}, u32[]{:S(2)}, u32[]{:S(2)}) collective-permute-start(s32[4,256]{1,0:T(4,128)} %bitcast.4), channel_id=1, source_target_pairs={{0,4},{4,0},{1,5},{5,1},{2,6},{6,2},{3,7},{7,3},{8,12},{12,8},{9,1... | collective-permute-start | bytes 12296 | tf_op jit(solution)/shard_map/ppermute | solution.py:314
  3.0 9.1 %collective-permute-start.1 = (f32[4,256]{1,0:T(4,128)}, f32[4,256]{1,0:T(4,128)S(1)}, u32[]{:S(2)}, u32[]{:S(2)}) collective-permute-start(f32[4,256]{1,0:T(4,128)} %bitcast.6), channel_id=1, source_target_pairs={{0,4},{4,0},{1,5},{5,1},{2,6},{6,2},{3,7},{7,3},{8,12},{12,8},{9,1... | collective-permute-start | bytes 12296 | tf_op jit(solution)/shard_map/ppermute | solution.py:314
  3.1 9.0 %copy-start = (s32[256,4]{0,1:T(4,128)S(1)}, s32[256,4]{0,1:T(4,128)}, u32[]{:S(2)}) copy-start(s32[256,4]{0,1:T(4,128)} %param.7) | copy-start | bytes 12292
  3.1 9.0 %copy-start.1 = (f32[256,4]{0,1:T(4,128)S(1)}, f32[256,4]{0,1:T(4,128)}, u32[]{:S(2)}) copy-start(f32[256,4]{0,1:T(4,128)} %param.8) | copy-start | bytes 12292
  16.5 10.9 %collective-permute-start.3 = (bf16[256,768]{1,0:T(8,128)(2,1)S(1)}, bf16[256,768]{1,0:T(8,128)(2,1)S(1)}, u32[]{:S(2)}, u32[]{:S(2)}) collective-permute-start(bf16[256,768]{1,0:T(8,128)(2,1)S(1)} %get-tuple-element.28), channel_id=1, source_target_pairs={{0,4},{4,0},{1,5},{5,1},{2,6},{6,2},{3,7},{7,3},{8,12},{12,8},{9,1... | collective-permute-start | bytes 1179656 | tf_op jit(solution)/shard_map/ppermute | solution.py:326
  27.3 13.8 %collective-permute-start.2 = (bf16[256,1024]{1,0:T(8,128)(2,1)S(1)}, bf16[256,1024]{1,0:T(8,128)(2,1)S(1)}, u32[]{:S(2)}, u32[]{:S(2)}) collective-permute-start(bf16[256,1024]{1,0:T(8,128)(2,1)S(1)} %get-tuple-element.26.refs_2_), channel_id=1, source_target_pairs={{0,4},{4,0},{1,5},{5,1},{2,6},{6,2},{3,7},{7,3},{8,12},{12,8},{9,1... | collective-permute-start | bytes 1572872 | tf_op jit(solution)/shard_map/ppermute | solution.py:326
  27.5 13.6 %collective-permute-start.4 = (bf16[256,768]{1,0:T(8,128)(2,1)S(1)}, bf16[256,768]{1,0:T(8,128)(2,1)S(1)}, u32[]{:S(2)}, u32[]{:S(2)}) collective-permute-start(bf16[256,768]{1,0:T(8,128)(2,1)S(1)} %fold.7.refs_2_), channel_id=1, source_target_pairs={{0,1},{1,0},{2,3},{3,2},{4,5},{5,4},{6,7},{7,6},{8,9},{9,8},{10,11... | collective-permute-start | bytes 1179656 | tf_op jit(solution)/shard_map/ppermute | solution.py:346
  38.1 15.1 %collective-permute-start.7 = (bf16[256,768]{1,0:T(8,128)(2,1)S(1)}, bf16[256,768]{1,0:T(8,128)(2,1)S(1)}, u32[]{:S(2)}, u32[]{:S(2)}) collective-permute-start(bf16[256,768]{1,0:T(8,128)(2,1)S(1)} %get-tuple-element.30.refs_3_), channel_id=1, source_target_pairs={{0,4},{4,0},{1,5},{5,1},{2,6},{6,2},{3,7},{7,3},{8,12},{12,8},{9,1... | collective-permute-start | bytes 1179656 | tf_op jit(solution)/shard_map/ppermute | solution.py:326
  41.2 17.7 %collective-permute-start.5 = (bf16[256,768]{1,0:T(8,128)(2,1)S(1)}, bf16[256,768]{1,0:T(8,128)(2,1)S(1)}, u32[]{:S(2)}, u32[]{:S(2)}) collective-permute-start(bf16[256,768]{1,0:T(8,128)(2,1)S(1)} %fold.8.refs_2_), channel_id=1, source_target_pairs={{0,2},{1,3},{2,0},{3,1},{4,6},{5,7},{6,4},{7,5},{8,10},{9,11},{10,... | collective-permute-start | bytes 1179656 | tf_op jit(solution)/shard_map/ppermute | solution.py:346
  43.8 11.5 %collective-permute-start.6 = (bf16[256,256]{1,0:T(8,128)(2,1)S(1)}, bf16[256,256]{1,0:T(8,128)(2,1)S(1)}, u32[]{:S(2)}, u32[]{:S(2)}) collective-permute-start(bf16[256,256]{1,0:T(8,128)(2,1)S(1)} %fold.9.refs_2_), channel_id=1, source_target_pairs={{0,1},{1,0},{2,3},{3,2},{4,5},{5,4},{6,7},{7,6},{8,9},{9,8},{10,11... | collective-permute-start | bytes 393224 | tf_op jit(solution)/shard_map/ppermute | solution.py:346
  47.0 11.9 %copy-start.2 = (bf16[256,768]{1,0:T(8,128)(2,1)S(1)}, bf16[256,768]{1,0:T(8,128)(2,1)}, u32[]{:S(2)}) copy-start(bf16[256,768]{1,0:T(8,128)(2,1)} %refs_0_.1) | copy-start | bytes 1179652
  53.1 6.4 %collective-permute-start.8 = (bf16[256,512]{1,0:T(8,128)(2,1)S(1)}, bf16[256,512]{1,0:T(8,128)(2,1)S(1)}, u32[]{:S(2)}, u32[]{:S(2)}) collective-permute-start(bf16[256,512]{1,0:T(8,128)(2,1)S(1)} %get-tuple-element.34.refs_2_), channel_id=1, source_target_pairs={{0,4},{4,0},{1,5},{5,1},{2,6},{6,2},{3,7},{7,3},{8,12},{12,8},{9,1... | collective-permute-start | bytes 786440 | tf_op jit(solution)/shard_map/ppermute | solution.py:326
  53.3 9.6 %collective-permute-start.9 = (bf16[256,512]{1,0:T(8,128)(2,1)S(1)}, bf16[256,512]{1,0:T(8,128)(2,1)S(1)}, u32[]{:S(2)}, u32[]{:S(2)}) collective-permute-start(bf16[256,512]{1,0:T(8,128)(2,1)S(1)} %fold.12), channel_id=1, source_target_pairs={{0,1},{1,0},{2,3},{3,2},{4,5},{5,4},{6,7},{7,6},{8,9},{9,8},{10,11... | collective-permute-start | bytes 786440 | tf_op jit(solution)/shard_map/ppermute | solution.py:346

commit v4 on v3

--- a/solution.py
+++ b/solution.py
@@ -9,9 +9,9 @@
 
 LANES = 128
 TILE = 256
-AHEAD = 2
-WINDOW = 4
-CHUNKS = (((3, 0, 3),), ((2, 0, 3), (1, 0, 1)), ((1, 1, 3), (0, 0, 1)), ((0, 1, 3),))
+AHEAD = (2, 4, 4)
+WINDOW = 6
+BLOCKS = (3, 2, 1, 0)
 
 LATE = 10**10
 
@@ -22,25 +22,10 @@
 BF16 = jnp.bfloat16
 
 
-class Strips:
-    def __init__(self, ids_ref, weight_ref, chunk, expert, target, sem):
-        self.rank, self.weight_ref, self.chunk = ids_ref[1], weight_ref.at[expert], chunk
-        self.target, self.sem = target, sem
-
-    def start(self):
-        column = 0
-        for block, start, stop, features in self.chunk:
-            at = pl.multiple_of(lax.bitwise_xor(self.rank, block) * features + start, LANES)
-            target = self.target.at[:, pl.ds(column, stop - start)]
-            pltpu.make_async_copy(self.weight_ref.at[:, pl.ds(at, stop - start)], target, self.sem).start()
-            column += stop - start
-
-    def wait(self):
-        pltpu.make_async_copy(self.weight_ref.at[:, pl.ds(0, self.target.shape[1])], self.target, self.sem).wait()
-
-
-def columns_of(chunk):
-    return sum(stop - start for _, start, stop, _ in chunk)
+def strip(ids_ref, weight_ref, block, expert, target, sem):
+    width = target.shape[1]
+    at = pl.multiple_of(lax.bitwise_xor(ids_ref[1], block) * width, LANES)
+    return pltpu.make_async_copy(weight_ref.at[expert, :, pl.ds(at, width)], target, sem)
 
 
 def balanced_dot(rows, weight_ref, finish):
@@ -130,10 +115,10 @@
             self.end()
 
 
-def first_kernel(chunk, ids_ref, hidden_ref, weight_ref, partial, stay_ref, weights, sems, hidden_sems):
+def first_kernel(block, ids_ref, hidden_ref, weight_ref, partial, stay_ref, weights, sems, hidden_sems):
     def bring(expert):
         copy = pltpu.make_async_copy(hidden_ref.at[expert], stay_ref.at[expert], hidden_sems.at[expert])
-        return [copy, Strips(ids_ref, weight_ref, chunk, expert, weights.at[expert], sems.at[expert])]
+        return [copy, strip(ids_ref, weight_ref, block, expert, weights.at[expert], sems.at[expert])]
 
     local = hidden_ref.shape[0]
     stream = Stream([bring(expert) for expert in range(local)])
@@ -142,7 +127,7 @@
         product(stay_ref.at[expert], weights.at[expert], partial, expert)
 
 
-def table_kernel(chunk, pair, capacity, *refs):
+def table_kernel(block, pair, capacity, *refs):
     refs = list(refs)
     ids_ref, partial, weight_ref = refs[:3]
     count = 2 if pair else 1
@@ -152,7 +137,7 @@
     local = table_refs[0].shape[-1] // capacity
     stream = Stream(
         [
-            [Strips(ids_ref, weight_ref, chunk, expert, next_ref.at[expert], next_sems.at[expert])]
+            [strip(ids_ref, weight_ref, block, expert, next_ref.at[expert], next_sems.at[expert])]
             for expert in range(next_ref.shape[0])
         ]
     )
@@ -166,22 +151,22 @@
     stream.finish()
 
 
-def chunk_kernel(chunk, following, groups, ids_ref, hidden_ref, weight_ref, held_ref, *refs):
+def chunk_kernel(block, following, groups, ids_ref, hidden_ref, weight_ref, held_ref, *refs):
     refs = list(refs)
     table_refs = [refs.pop(0) for _ in range(groups)]
     del refs[0]
     outs = [refs.pop(0) for _ in range(groups)]
-    next_ref = refs.pop(0) if following else None
+    next_ref = refs.pop(0) if following is not None else None
     weights, partial, sems, next_sems = refs
     local, ahead = hidden_ref.shape[0], held_ref.shape[0]
 
     own = [
-        [Strips(ids_ref, weight_ref, chunk, e, weights.at[e - ahead], sems.at[e - ahead])]
+        [strip(ids_ref, weight_ref, block, e, weights.at[e - ahead], sems.at[e - ahead])]
         for e in range(ahead, local)
     ]
     later = [
-        [Strips(ids_ref, weight_ref, following, e, next_ref.at[e], next_sems.at[e])]
-        for e in range(ahead if following else 0)
+        [strip(ids_ref, weight_ref, following, e, next_ref.at[e], next_sems.at[e])]
+        for e in range(next_ref.shape[0] if following is not None else 0)
     ]
     stream = Stream(own + later)
     for expert in range(local):
@@ -217,11 +202,10 @@
 COST = cost(1000, 1000)
 
 
-def first_products(chunk, ids, hidden, weight):
+def first_products(block, columns, ids, hidden, weight):
     local, sources, capacity, depth = hidden.shape
-    columns = columns_of(chunk)
     return pl.pallas_call(
-        functools.partial(first_kernel, chunk),
+        functools.partial(first_kernel, block),
         in_specs=[SMEM, HBM, HBM],
         out_specs=[VMEM] * 2,
         out_shape=[shape(sources, local * capacity, columns), shape(*hidden.shape)],
@@ -245,14 +229,14 @@
     pair = len(routes) == 2
     tokens = routes[0].shape[-1]
     depth = weight.shape[1]
-    ahead = min(AHEAD, width // capacity)
+    ahead = min(AHEAD[0], width // capacity)
     table = [shape(tokens, width)] * 2 if pair else [shape(sources, tokens, width)]
     outs = group_shapes(pair, sources, tokens, columns)
     results = pl.pallas_call(
         functools.partial(table_kernel, following, pair, capacity),
         in_specs=[SMEM, VMEM, HBM] + [VMEM] * (2 * len(routes)),
         out_specs=[VMEM] * (len(table) + len(outs) + 1),
-        out_shape=table + outs + [shape(ahead, depth, columns_of(following))],
+        out_shape=table + outs + [shape(ahead, depth, columns)],
         scratch_shapes=[pltpu.SemaphoreType.DMA((ahead,))],
         cost_estimate=COST,
         compiler_params=pltpu.CompilerParams(vmem_limit_bytes=12 << 20),
@@ -261,18 +245,19 @@
     return results[: len(table)], results[len(table) : -1], results[-1]
 
 
-def chunk_sums(chunk, following, ids, hidden, weight, table, held, after):
+def chunk_sums(block, following, ids, hidden, weight, table, held, after):
     local, sources, capacity, depth = hidden.shape
     tokens = table[0].shape[-2]
     ahead, _, columns = held.shape
     brought = max(local - ahead, 1)
     groups = len(table)
     outs = group_shapes(groups == 2, sources, tokens, columns)
-    if following:
-        outs.append(shape(ahead, depth, columns_of(following)))
+    if following is not None:
+        ahead_next = min(AHEAD[BLOCKS.index(block)], local)
+        outs.append(shape(ahead_next, depth, columns))
     flops = 2 * sources * local * capacity * columns * (depth + tokens)
     results = pl.pallas_call(
-        functools.partial(chunk_kernel, chunk, following, groups),
+        functools.partial(chunk_kernel, block, following, groups),
         in_specs=[SMEM, VMEM, HBM, VMEM] + [VMEM] * groups + [ANY],
         out_specs=[VMEM] * len(outs),
         out_shape=outs,
@@ -280,13 +265,13 @@
             pltpu.VMEM((brought, depth, columns), BF16),
             pltpu.VMEM((sources, local * capacity, columns), BF16),
             pltpu.SemaphoreType.DMA((brought,)),
-            pltpu.SemaphoreType.DMA((ahead,)),
+            pltpu.SemaphoreType.DMA((local,)),
         ],
-        cost_estimate=cost(flops, local * depth * columns) if following else COST,
-        compiler_params=pltpu.CompilerParams(vmem_limit_bytes=28 << 20),
-        name="chunk",
+        cost_estimate=cost(flops, local * depth * columns) if following is not None else COST,
+        compiler_params=pltpu.CompilerParams(vmem_limit_bytes=20 << 20),
+        name=f"chunk{block}",
     )(ids, hidden, weight, held, *table, after)
-    return results[:groups], results[groups] if following else None
+    return results[:groups], results[groups] if following is not None else None
 
 
 def fold(width, terms, after, dtype=BF16, flops=1000):
@@ -315,56 +300,38 @@
     else:
         routes, scores = [lax.all_gather(routes, "expert")], [lax.all_gather(scores, "expert")]
 
-    chunks = [
-        tuple((block, start * features // 3, stop * features // 3, features) for block, start, stop in chunk)
-        for chunk in CHUNKS
-    ]
-    over, along = [], {}
-
-    def send_over(sums):
+    def send_over(sums, width=features):
         if pair:
-            over.append([sums[1], lax.ppermute(sums[0], "expert", swap)])
-        else:
-            whole = lax.psum_scatter(sums[0], "expert", scatter_dimension=0, tiled=True)
-            over.append([whole.reshape(tokens, -1)])
-
-    def terms(i, block, base):
-        column = 0
-        for which, start, stop, _ in chunks[i]:
-            if which == block:
-                found = [(array, column, start - base, stop - start) for array in over[i]]
-                for array, first, width in along.get(block, []):
-                    low, high = max(start, first), min(stop, first + width)
-                    if low < high:
-                        found.append((array, low - first, low - base, high - low))
-                return found
-            column += stop - start
-
-    def send_along(i, block, flip, after):
-        start, stop = next((start, stop) for which, start, stop, _ in chunks[i] if which == block)
-        total = fold(stop - start, terms(i, block, start), after)
-        got = lax.ppermute(total, "tp", [(r, r ^ flip) for r in range(ranks)])
-        along.setdefault(block ^ flip, []).append((got, start, stop - start))
-        return total
-
-    partial, hidden = first_products(chunks[0], ids, hidden, down_weight)
-    table, sums, held = tables(chunks[1], ids, partial, down_weight, routes, scores, capacity)
-    send_over(sums)
-    sums, held = chunk_sums(chunks[1], chunks[2], ids, hidden, down_weight, table, held, ids)
-    send_over(sums)
-    total = send_along(0, 3, 1, sums[0])
-    sums, held = chunk_sums(chunks[2], chunks[3], ids, hidden, down_weight, table, held, total)
-    send_over(sums)
-    total = send_along(1, 2, 2, sums[0])
-    total = send_along(1, 1, 1, total)
-    sums, _ = chunk_sums(chunks[3], None, ids, hidden, down_weight, table, held, total)
-    send_over(sums)
-    send_along(2, 1, 1, sums[0])
-    far, near, last = [(array, 0, first, width) for array, first, width in along[0]]
-    here = [(residual, 0, 0, features)]
-    rest = fold(features, here + [far, near] + [(a, c, at, w) for a, c, at, w in terms(2, 0, 0)[: len(over[2])]], ids, f32, LATE)
-    rest = fold(features, [(rest, 0, 0, features)] + terms(3, 0, 0)[: len(over[3])], ids, f32, LATE)
-    return fold(features, [(rest, 0, 0, features), last], ids)
+            return [sums[1], lax.ppermute(sums[0][:, :width], "expert", swap)]
+        return [lax.psum_scatter(sums[0], "expert", scatter_dimension=0, tiled=True).reshape(tokens, features)]
+
+    def send_along(total, flip):
+        return lax.ppermute(total, "tp", [(r, r ^ flip) for r in range(ranks)])
+
+    def spans(arrays, width=features):
+        return [(array, 0, 0, width) for array in arrays]
+
+    partial, hidden = first_products(BLOCKS[0], features, ids, hidden, down_weight)
+    table, sums, held = tables(BLOCKS[1], ids, partial, down_weight, routes, scores, capacity)
+    over3 = send_over(sums)
+    sums, held = chunk_sums(BLOCKS[1], BLOCKS[2], ids, hidden, down_weight, table, held, ids)
+    over2 = send_over(sums)
+    total3 = fold(features, spans(over3), sums[0])
+    near2 = send_along(total3, 1)
+    sums, held = chunk_sums(BLOCKS[2], BLOCKS[3], ids, hidden, down_weight, table, held, total3)
+    late = features - features // 3 if pair else features
+    over1 = send_over(sums, late)
+    early = [send_along(part[:, late:], 1) for part in sums] if pair else []
+    total2 = fold(features, spans(over2 + [near2]), sums[0])
+    far0 = send_along(total2, 2)
+    sums, _ = chunk_sums(BLOCKS[3], None, ids, hidden, down_weight, table, held, total2)
+    if pair:
+        sums = [fold(features, spans([part]) + [(got, 0, late, features - late)], total2) for part, got in zip(sums, early)]
+    over0 = send_over(sums)
+    near0 = send_along(fold(late, spans(over1, late), sums[0]), 1)
+    rest = fold(features, spans([residual, far0]), ids, f32, LATE)
+    rest = fold(features, spans([rest] + over0), ids, f32, LATE)
+    return fold(features, spans([rest]) + spans([near0], late), ids)
 
 
 def solution(mesh):

time: 63.8 us -> 62.2 us (0.975)
  starting transfers between devices: 14.9 us -> 18.9 us
  waiting for transfers between devices: 10.7 us -> 6.76 us
  Pallas kernels: 37.9 us -> 36.2 us
    ppermute x8 -> x9, starting transfers between devices: 11.9 us -> 15.9 us  [the longest x5 9.62 us: send_along(): return lax.ppermute(total, 'tp', [(r, r ^ flip) for r in range(ranks)])]
    ppermute x8 -> x9, waiting for transfers between devices: 10.7 us -> 6.75 us  [the longest x4 3.95 us: send_over(): return [sums[1], lax.ppermute(sums[0][:, :width], 'expert', swap)]]
    pallas_call x4, Pallas kernels: 32.1 us -> 30.7 us  [the longest x3 21.8 us: chunk_sums(): pl.pallas_call(functools.partial(chunk_kernel, block, following, groups),...]
    pallas_call x7 -> x8, Pallas kernels: 1.36 us -> 1.4 us  [fold(): pl.pallas_call(functools.partial(fold_kernel, spans), in_specs=[VMEM] * l...]
  transfers between devices with their start and end apart: 10 -> 11, of which waited for: 5 -> 6; matrix products, arithmetic and copies ran while one was open for 0% -> 0% of each run, Pallas kernels for 51% -> 50%
where the time goes in v4:
time: 62.2 us; the launch traced here: 62.1 us
  Pallas kernels  36.2 us (58%)
  starting transfers between devices  18.9 us (30%)
  waiting for transfers between devices  6.76 us (11%)
    pallas_call x3, Pallas kernels, chunk_sums(): pl.pallas_call(functools.partial(chunk_kernel, block, following, groups),...  21.8 us
    ppermute x5, starting transfers between devices, send_along(): return lax.ppermute(total, 'tp', [(r, r ^ flip) for r in range(ranks)])  9.62 us
    pallas_call x1, Pallas kernels, first_products(): pl.pallas_call(functools.partial(first_kernel, block), in_specs=[SMEM, HB...  8.92 us
    ppermute x4, starting transfers between devices, send_over(): return [sums[1], lax.ppermute(sums[0][:, :width], 'expert', swap)]  6.27 us
    pallas_call x1, Pallas kernels, tables(): pl.pallas_call(functools.partial(table_kernel, following, pair, capacity)...  4.07 us
    ppermute x4, waiting for transfers between devices, send_over(): return [sums[1], lax.ppermute(sums[0][:, :width], 'expert', swap)]  3.95 us
    ppermute x1, starting transfers between devices, on_device(): lax.ppermute(routes, 'expert', swap)  2.97 us
    ppermute x5, waiting for transfers between devices, send_along(): return lax.ppermute(total, 'tp', [(r, r ^ flip) for r in range(ranks)])  2.81 us
  transfers between devices with their start and end apart: 11, of which 6 were waited for; matrix products, arithmetic and copies ran while one was open for 0% of the time, Pallas kernels for 50%

profile of v4, /device:TPU:0, one launch (start us, length us, event | category | flops | bytes accessed | tf_op | source)
XLA Modules:
  0.0 62.1 jit_solution(6688203142892212483)
XLA Ops:
  0.0 3.0 %collective-permute-start = (s32[4,256]{1,0:T(4,128)}, s32[4,256]{1,0:T(4,128)S(1)}, u32[]{:S(2)}, u32[]{:S(2)}) collective-permute-start(s32[4,256]{1,0:T(4,128)} %bitcast.4), channel_id=1, source_target_pairs={{0,4},{4,0},{1,5},{5,1},{2,6},{6,2},{3,7},{7,3},{8,12},{12,8},{9,1... | collective-permute-start | bytes 12296 | tf_op jit(solution)/shard_map/ppermute | solution.py:299
  3.0 0.0 collective-permute-start.1
  3.0 0.1 pad_add_fusion.ids_ref.refs_0_.refs_2_.refs_3_
  3.1 8.9 %first.1 = (bf16[2,768,768]{2,1,0:T(8,128)(2,1)S(1)}, bf16[8,2,96,1408]{3,2,1,0:T(8,128)(2,1)S(1)}) custom-call(s32[2]{0:T(128)S(1)} %pad_add_fusion.ids_ref.refs_0_.refs_2_.refs_3_, bf16[8,2,96,1408]{3,2,1,0:T(8,128)(2,1)} %hidden_ref.1, bf16[8,1408,3072]{2,1,0:T(8,128)(2,1)} %weight_ref.7), custom_call_target="tpu_custom_call" | custom-call | flops 3321888768 | bytes 17301504 | tf_op jit(solution)/shard_map/first/pallas_call | solution.py:207
  12.0 0.0 collective-permute-done.1.refs_5_
  12.1 4.1 %tables.1 = (bf16[256,768]{1,0:T(8,128)(2,1)S(1)}, bf16[256,768]{1,0:T(8,128)(2,1)S(1)}, bf16[256,768]{1,0:T(8,128)(2,1)S(1)}, bf16[256,768]{1,0:T(8,128)(2,1)S(1)}, bf16[2,1408,768]{2,1,0:T(8,128)(2,1)S(1)}) custom-call(s32[2]{0:T(128)S(1)} %pad_add_fusion.ids_ref.refs_0_.refs_2_.refs_3_, bf16[2,768,768]{2,1,0:T(8,128)(2,1)S(1)} %get-tuple-element.21.refs_1_, ...), custom_call_target="tpu_custom_call" | custom-call | flops 1000 | bytes 2000 | tf_op jit(solution)/shard_map/tables/pallas_call | solution.py:235
  16.1 2.1 %collective-permute-start.3 = (bf16[256,768]{1,0:T(8,128)(2,1)S(1)}, bf16[256,768]{1,0:T(8,128)(2,1)S(1)}, u32[]{:S(2)}, u32[]{:S(2)}) collective-permute-start(bf16[256,768]{1,0:T(8,128)(2,1)S(1)} %get-tuple-element.28), channel_id=1, source_target_pairs={{0,4},{4,0},{1,5},{5,1},{2,6},{6,2},{3,7},{7,3},{8,12},{12,8},{9,1... | collective-permute-start | bytes 1179656 | tf_op jit(solution)/shard_map/ppermute | solution.py:305
  18.2 8.3 %chunk2.1 = (bf16[256,768]{1,0:T(8,128)(2,1)S(1)}, bf16[256,768]{1,0:T(8,128)(2,1)S(1)}, bf16[4,1408,768]{2,1,0:T(8,128)(2,1)S(1)}) custom-call(s32[2]{0:T(128)S(1)} %pad_add_fusion.ids_ref.refs_0_.refs_2_.refs_3_, bf16[8,2,96,1408]{3,2,1,0:T(8,128)(2,1)S(1)} %get-tuple-element.20.hidden_ref, bf16[8,1408,3072]{2,1,0:T(8,128)(2,1)} %weight_ref.7, ...), custom_call_target="tpu_custom_call" | custom-call | flops 3925868544 | bytes 17301504 | tf_op jit(solution)/shard_map/chunk2/pallas_call | solution.py:259
  26.4 0.1 collective-permute-start.2
  26.5 0.2 collective-permute-done.3.refs_1_
  26.8 0.1 fold.8.refs_2_
  26.9 2.0 %collective-permute-start.4 = (bf16[256,768]{1,0:T(8,128)(2,1)S(1)}, bf16[256,768]{1,0:T(8,128)(2,1)S(1)}, u32[]{:S(2)}, u32[]{:S(2)}) collective-permute-start(bf16[256,768]{1,0:T(8,128)(2,1)S(1)} %fold.8.refs_2_), channel_id=1, source_target_pairs={{0,1},{1,0},{2,3},{3,2},{4,5},{5,4},{6,7},{7,6},{8,9},{9,8},{10,11... | collective-permute-start | bytes 1179656 | tf_op jit(solution)/shard_map/ppermute | solution.py:309
  28.9 6.9 %chunk1.1 = (bf16[256,768]{1,0:T(8,128)(2,1)S(1)}, bf16[256,768]{1,0:T(8,128)(2,1)S(1)}, bf16[4,1408,768]{2,1,0:T(8,128)(2,1)S(1)}) custom-call(s32[2]{0:T(128)S(1)} %pad_add_fusion.ids_ref.refs_0_.refs_2_.refs_3_, bf16[8,2,96,1408]{3,2,1,0:T(8,128)(2,1)S(1)} %get-tuple-element.20.hidden_ref, bf16[8,1408,3072]{2,1,0:T(8,128)(2,1)} %weight_ref.7, ...), custom_call_target="tpu_custom_call" | custom-call | flops 3925868544 | bytes 17301504 | tf_op jit(solution)/shard_map/chunk1/pallas_call | solution.py:259
  35.8 0.7 %collective-permute-done.2.refs_1_ = bf16[256,768]{1,0:T(8,128)(2,1)S(1)} collective-permute-done((bf16[256,768]{1,0:T(8,128)(2,1)S(1)}, bf16[256,768]{1,0:T(8,128)(2,1)S(1)}, u32[]{:S(2)}, u32[]{:S(2)}) %collective-permute-start.2) | collective-permute-done | bytes 393248 | tf_op jit(solution)/shard_map/ppermute | solution.py:305
  36.5 0.3 collective-permute-done.4.refs_2_
  36.9 0.1 fold.9.refs_2_
  37.0 2.9 %collective-permute-start.5 = (bf16[256,768]{1,0:T(8,128)(2,1)S(1)}, bf16[256,768]{1,0:T(8,128)(2,1)S(1)}, u32[]{:S(2)}, u32[]{:S(2)}) collective-permute-start(bf16[256,768]{1,0:T(8,128)(2,1)S(1)} %fold.9.refs_2_), channel_id=1, source_target_pairs={{0,2},{1,3},{2,0},{3,1},{4,6},{5,7},{6,4},{7,5},{8,10},{9,11},{10,... | collective-permute-start | bytes 1179656 | tf_op jit(solution)/shard_map/ppermute | solution.py:309
  40.0 1.6 %collective-permute-start.9 = (bf16[256,512]{1,0:T(8,128)(2,1)S(1)}, bf16[256,512]{1,0:T(8,128)(2,1)S(1)}, u32[]{:S(2)}, u32[]{:S(2)}) collective-permute-start(bf16[256,512]{1,0:T(8,128)(2,1)S(1)} %slice.11), channel_id=1, source_target_pairs={{0,4},{4,0},{1,5},{5,1},{2,6},{6,2},{3,7},{7,3},{8,12},{12,8},{9,1... | collective-permute-start | bytes 786440 | tf_op jit(solution)/shard_map/ppermute | solution.py:305
  41.6 1.8 %collective-permute-start.7 = (bf16[256,256]{1,0:T(8,128)(2,1)S(1)}, bf16[256,256]{1,0:T(8,128)(2,1)S(1)}, u32[]{:S(2)}, u32[]{:S(2)}) collective-permute-start(bf16[256,256]{1,0:T(8,128)(2,1)S(1)} %slice.10), channel_id=1, source_target_pairs={{0,1},{1,0},{2,3},{3,2},{4,5},{5,4},{6,7},{7,6},{8,9},{9,8},{10,11... | collective-permute-start | bytes 393224 | tf_op jit(solution)/shard_map/ppermute | solution.py:309
  43.4 0.4 collective-permute-start.6
  43.7 6.6 %chunk0.1 = (bf16[256,768]{1,0:T(8,128)(2,1)S(1)}, bf16[256,768]{1,0:T(8,128)(2,1)S(1)}) custom-call(s32[2]{0:T(128)S(1)} %pad_add_fusion.ids_ref.refs_0_.refs_2_.refs_3_, bf16[8,2,96,1408]{3,2,1,0:T(8,128)(2,1)S(1)} %get-tuple-element.20.hidden_ref, bf16[8,1408,3072]{2,1,0:T(8,128)(2,1)} %weight_ref.7, ...), custom_call_target="tpu_custom_call" | custom-call | flops 1000 | bytes 2000 | tf_op jit(solution)/shard_map/chunk0/pallas_call | solution.py:259
  50.3 0.6 collective-permute-done.7.refs_1_
  50.9 2.5 %collective-permute-start.8 = (bf16[256,768]{1,0:T(8,128)(2,1)S(1)}, bf16[256,768]{1,0:T(8,128)(2,1)S(1)}, u32[]{:S(2)}, u32[]{:S(2)}) collective-permute-start(bf16[256,768]{1,0:T(8,128)(2,1)S(1)} %fold.12.refs_2_), channel_id=1, source_target_pairs={{0,4},{4,0},{1,5},{5,1},{2,6},{6,2},{3,7},{7,3},{8,12},{12,8},{9,1... | collective-permute-start | bytes 1179656 | tf_op jit(solution)/shard_map/ppermute | solution.py:305
  53.5 0.1 fold.14
  53.5 2.5 %collective-permute-start.10 = (bf16[256,512]{1,0:T(8,128)(2,1)S(1)}, bf16[256,512]{1,0:T(8,128)(2,1)S(1)}, u32[]{:S(2)}, u32[]{:S(2)}) collective-permute-start(bf16[256,512]{1,0:T(8,128)(2,1)S(1)} %fold.14), channel_id=1, source_target_pairs={{0,1},{1,0},{2,3},{3,2},{4,5},{5,4},{6,7},{7,6},{8,9},{9,8},{10,11... | collective-permute-start | bytes 786440 | tf_op jit(solution)/shard_map/ppermute | solution.py:309
  56.1 0.0 collective-permute-done.6.refs_1_
  56.1 0.0 collective-permute-done.5.refs_1_
  56.2 0.1 fold.10.refs_0_
  56.3 3.0 %collective-permute-done.8.refs_2_ = bf16[256,768]{1,0:T(8,128)(2,1)S(1)} collective-permute-done((bf16[256,768]{1,0:T(8,128)(2,1)S(1)}, bf16[256,768]{1,0:T(8,128)(2,1)S(1)}, u32[]{:S(2)}, u32[]{:S(2)}) %collective-permute-start.8) | collective-permute-done | bytes 393248 | tf_op jit(solution)/shard_map/ppermute | solution.py:305
  59.2 0.1 fold.13.refs_0_
  59.4 1.9 %collective-permute-done.10.refs_1_ = bf16[256,512]{1,0:T(8,128)(2,1)S(1)} collective-permute-done((bf16[256,512]{1,0:T(8,128)(2,1)S(1)}, bf16[256,512]{1,0:T(8,128)(2,1)S(1)}, u32[]{:S(2)}, u32[]{:S(2)}) %collective-permute-start.10) | collective-permute-done | bytes 262176 | tf_op jit(solution)/shard_map/ppermute | solution.py:309
  61.3 0.8 %fold.15 = bf16[256,768]{1,0:T(8,128)(2,1)} custom-call(f32[256,768]{1,0:T(8,128)S(1)} %fold.13.refs_0_, bf16[256,512]{1,0:T(8,128)(2,1)S(1)} %collective-permute-done.10.refs_1_, s32[2]{0:T(128)S(1)} %pad_add_fusion.ids_ref.refs_0_.refs_2_.refs_3_), custom_call_target="tpu_custom_call" | custom-call | flops 1000 | bytes 2000 | tf_op jit(solution)/shard_map/fold/pallas_call | solution.py:279
  (13 shorter events, 0.2 us)
Async XLA Ops:
  0.0 12.0 %collective-permute-start = (s32[4,256]{1,0:T(4,128)}, s32[4,256]{1,0:T(4,128)S(1)}, u32[]{:S(2)}, u32[]{:S(2)}) collective-permute-start(s32[4,256]{1,0:T(4,128)} %bitcast.4), channel_id=1, source_target_pairs={{0,4},{4,0},{1,5},{5,1},{2,6},{6,2},{3,7},{7,3},{8,12},{12,8},{9,1... | collective-permute-start | bytes 12296 | tf_op jit(solution)/shard_map/ppermute | solution.py:299
  3.0 9.1 %collective-permute-start.1 = (f32[4,256]{1,0:T(4,128)}, f32[4,256]{1,0:T(4,128)S(1)}, u32[]{:S(2)}, u32[]{:S(2)}) collective-permute-start(f32[4,256]{1,0:T(4,128)} %bitcast.6), channel_id=1, source_target_pairs={{0,4},{4,0},{1,5},{5,1},{2,6},{6,2},{3,7},{7,3},{8,12},{12,8},{9,1... | collective-permute-start | bytes 12296 | tf_op jit(solution)/shard_map/ppermute | solution.py:299
  3.1 9.0 %copy-start = (s32[256,4]{0,1:T(4,128)S(1)}, s32[256,4]{0,1:T(4,128)}, u32[]{:S(2)}) copy-start(s32[256,4]{0,1:T(4,128)} %param.7) | copy-start | bytes 12292
  3.1 9.0 %copy-start.1 = (f32[256,4]{0,1:T(4,128)S(1)}, f32[256,4]{0,1:T(4,128)}, u32[]{:S(2)}) copy-start(f32[256,4]{0,1:T(4,128)} %param.8) | copy-start | bytes 12292
  16.1 10.7 %collective-permute-start.3 = (bf16[256,768]{1,0:T(8,128)(2,1)S(1)}, bf16[256,768]{1,0:T(8,128)(2,1)S(1)}, u32[]{:S(2)}, u32[]{:S(2)}) collective-permute-start(bf16[256,768]{1,0:T(8,128)(2,1)S(1)} %get-tuple-element.28), channel_id=1, source_target_pairs={{0,4},{4,0},{1,5},{5,1},{2,6},{6,2},{3,7},{7,3},{8,12},{12,8},{9,1... | collective-permute-start | bytes 1179656 | tf_op jit(solution)/shard_map/ppermute | solution.py:305
  26.4 10.1 %collective-permute-start.2 = (bf16[256,768]{1,0:T(8,128)(2,1)S(1)}, bf16[256,768]{1,0:T(8,128)(2,1)S(1)}, u32[]{:S(2)}, u32[]{:S(2)}) collective-permute-start(bf16[256,768]{1,0:T(8,128)(2,1)S(1)} %get-tuple-element.26.refs_2_), channel_id=1, source_target_pairs={{0,4},{4,0},{1,5},{5,1},{2,6},{6,2},{3,7},{7,3},{8,12},{12,8},{9,1... | collective-permute-start | bytes 1179656 | tf_op jit(solution)/shard_map/ppermute | solution.py:305
  26.9 10.0 %collective-permute-start.4 = (bf16[256,768]{1,0:T(8,128)(2,1)S(1)}, bf16[256,768]{1,0:T(8,128)(2,1)S(1)}, u32[]{:S(2)}, u32[]{:S(2)}) collective-permute-start(bf16[256,768]{1,0:T(8,128)(2,1)S(1)} %fold.8.refs_2_), channel_id=1, source_target_pairs={{0,1},{1,0},{2,3},{3,2},{4,5},{5,4},{6,7},{7,6},{8,9},{9,8},{10,11... | collective-permute-start | bytes 1179656 | tf_op jit(solution)/shard_map/ppermute | solution.py:309
  37.0 19.1 %collective-permute-start.5 = (bf16[256,768]{1,0:T(8,128)(2,1)S(1)}, bf16[256,768]{1,0:T(8,128)(2,1)S(1)}, u32[]{:S(2)}, u32[]{:S(2)}) collective-permute-start(bf16[256,768]{1,0:T(8,128)(2,1)S(1)} %fold.9.refs_2_), channel_id=1, source_target_pairs={{0,2},{1,3},{2,0},{3,1},{4,6},{5,7},{6,4},{7,5},{8,10},{9,11},{10,... | collective-permute-start | bytes 1179656 | tf_op jit(solution)/shard_map/ppermute | solution.py:309
  40.0 13.5 %collective-permute-start.9 = (bf16[256,512]{1,0:T(8,128)(2,1)S(1)}, bf16[256,512]{1,0:T(8,128)(2,1)S(1)}, u32[]{:S(2)}, u32[]{:S(2)}) collective-permute-start(bf16[256,512]{1,0:T(8,128)(2,1)S(1)} %slice.11), channel_id=1, source_target_pairs={{0,4},{4,0},{1,5},{5,1},{2,6},{6,2},{3,7},{7,3},{8,12},{12,8},{9,1... | collective-permute-start | bytes 786440 | tf_op jit(solution)/shard_map/ppermute | solution.py:305
  41.6 9.3 %collective-permute-start.7 = (bf16[256,256]{1,0:T(8,128)(2,1)S(1)}, bf16[256,256]{1,0:T(8,128)(2,1)S(1)}, u32[]{:S(2)}, u32[]{:S(2)}) collective-permute-start(bf16[256,256]{1,0:T(8,128)(2,1)S(1)} %slice.10), channel_id=1, source_target_pairs={{0,1},{1,0},{2,3},{3,2},{4,5},{5,4},{6,7},{7,6},{8,9},{9,8},{10,11... | collective-permute-start | bytes 393224 | tf_op jit(solution)/shard_map/ppermute | solution.py:309
  43.4 12.7 %collective-permute-start.6 = (bf16[256,256]{1,0:T(8,128)(2,1)S(1)}, bf16[256,256]{1,0:T(8,128)(2,1)S(1)}, u32[]{:S(2)}, u32[]{:S(2)}) collective-permute-start(bf16[256,256]{1,0:T(8,128)(2,1)S(1)} %slice.9), channel_id=1, source_target_pairs={{0,1},{1,0},{2,3},{3,2},{4,5},{5,4},{6,7},{7,6},{8,9},{9,8},{10,11... | collective-permute-start | bytes 393224 | tf_op jit(solution)/shard_map/ppermute | solution.py:309
  43.7 12.4 %copy-start.2 = (bf16[256,768]{1,0:T(8,128)(2,1)S(1)}, bf16[256,768]{1,0:T(8,128)(2,1)}, u32[]{:S(2)}) copy-start(bf16[256,768]{1,0:T(8,128)(2,1)} %refs_0_.1) | copy-start | bytes 1179652
  50.9 8.3 %collective-permute-start.8 = (bf16[256,768]{1,0:T(8,128)(2,1)S(1)}, bf16[256,768]{1,0:T(8,128)(2,1)S(1)}, u32[]{:S(2)}, u32[]{:S(2)}) collective-permute-start(bf16[256,768]{1,0:T(8,128)(2,1)S(1)} %fold.12.refs_2_), channel_id=1, source_target_pairs={{0,4},{4,0},{1,5},{5,1},{2,6},{6,2},{3,7},{7,3},{8,12},{12,8},{9,1... | collective-permute-start | bytes 1179656 | tf_op jit(solution)/shard_map/ppermute | solution.py:305
  53.5 7.7 %collective-permute-start.10 = (bf16[256,512]{1,0:T(8,128)(2,1)S(1)}, bf16[256,512]{1,0:T(8,128)(2,1)S(1)}, u32[]{:S(2)}, u32[]{:S(2)}) collective-permute-start(bf16[256,512]{1,0:T(8,128)(2,1)S(1)} %fold.14), channel_id=1, source_target_pairs={{0,1},{1,0},{2,3},{3,2},{4,5},{5,4},{6,7},{7,6},{8,9},{9,8},{10,11... | collective-permute-start | bytes 786440 | tf_op jit(solution)/shard_map/ppermute | solution.py:309

commit v5 on v3

--- a/solution.py
+++ b/solution.py
@@ -9,9 +9,9 @@
 
 LANES = 128
 TILE = 256
-AHEAD = 2
-WINDOW = 4
-CHUNKS = (((3, 0, 3),), ((2, 0, 3), (1, 0, 1)), ((1, 1, 3), (0, 0, 1)), ((0, 1, 3),))
+AHEAD = (2, 3, 3)
+WINDOW = 6
+CHUNKS = (((3, 0, 3),), ((2, 0, 3),), ((1, 0, 3),), ((0, 0, 3),))
 
 LATE = 10**10
 
@@ -70,16 +70,23 @@
     balanced_dot(rows_ref[...].reshape(sources * capacity, depth), weight_ref, finish)
 
 
-def combine(ids_ref, table_refs, partial, outs):
+def combine(ids_ref, table_refs, partial, outs, early_ref=None):
     mine = ids_ref[0]
     if len(outs) == 2:
         order = [(outs[0], table_refs[0], 1 - mine), (outs[1], table_refs[1], mine)]
     else:
         order = [(outs[0].at[s], table_refs[0].at[s], s) for s in range(partial.shape[0])]
-    for out_ref, table_ref, source in order:
-
-        def finish(start, stop, value, out_ref=out_ref):
-            out_ref[:, start:stop] = value.astype(out_ref.dtype)
+    for i, (out_ref, table_ref, source) in enumerate(order):
+
+        def finish(start, stop, value, i=i, out_ref=out_ref):
+            tokens, room = out_ref.shape
+            value = value.astype(out_ref.dtype)
+            cut = min(stop, room)
+            if start < cut:
+                out_ref[:, start:cut] = value[:, : cut - start]
+            if cut < stop:
+                low = max(start, room)
+                early_ref[i * tokens : (i + 1) * tokens, low - room : stop - room] = value[:, low - start :]
 
         balanced_dot(table_ref[...], partial.at[source], finish)
 
@@ -166,11 +173,12 @@
     stream.finish()
 
 
-def chunk_kernel(chunk, following, groups, ids_ref, hidden_ref, weight_ref, held_ref, *refs):
+def chunk_kernel(chunk, following, groups, early, ids_ref, hidden_ref, weight_ref, held_ref, *refs):
     refs = list(refs)
     table_refs = [refs.pop(0) for _ in range(groups)]
     del refs[0]
     outs = [refs.pop(0) for _ in range(groups)]
+    early_ref = refs.pop(0) if early else None
     next_ref = refs.pop(0) if following else None
     weights, partial, sems, next_sems = refs
     local, ahead = hidden_ref.shape[0], held_ref.shape[0]
@@ -181,7 +189,7 @@
     ]
     later = [
         [Strips(ids_ref, weight_ref, following, e, next_ref.at[e], next_sems.at[e])]
-        for e in range(ahead if following else 0)
+        for e in range(next_ref.shape[0] if following else 0)
     ]
     stream = Stream(own + later)
     for expert in range(local):
@@ -190,17 +198,18 @@
             product(hidden_ref.at[expert], weights.at[expert - ahead], partial, expert)
         else:
             product(hidden_ref.at[expert], held_ref.at[expert], partial, expert)
-    combine(ids_ref, table_refs, partial, outs)
+    combine(ids_ref, table_refs, partial, outs, early_ref)
     stream.finish()
 
 
 def fold_kernel(spans, *refs):
     *terms, _, sum_ref = refs
-    edges = sorted({edge for _, at, width in spans for edge in (at, at + width)})
+    tokens = sum_ref.shape[0]
+    edges = sorted({edge for _, _, at, width in spans for edge in (at, at + width)})
     for low, high in zip(edges[:-1], edges[1:]):
         parts = [
-            term[:, source + low - at : source + high - at].astype(jnp.float32)
-            for term, (source, at, width) in zip(terms, spans)
+            term[row : row + tokens, source + low - at : source + high - at].astype(jnp.float32)
+            for term, (row, source, at, width) in zip(terms, spans)
             if at <= low < at + width
         ]
         sum_ref[:, low:high] = functools.reduce(jnp.add, parts).astype(sum_ref.dtype)
@@ -245,7 +254,7 @@
     pair = len(routes) == 2
     tokens = routes[0].shape[-1]
     depth = weight.shape[1]
-    ahead = min(AHEAD, width // capacity)
+    ahead = min(AHEAD[0], width // capacity)
     table = [shape(tokens, width)] * 2 if pair else [shape(sources, tokens, width)]
     outs = group_shapes(pair, sources, tokens, columns)
     results = pl.pallas_call(
@@ -261,18 +270,20 @@
     return results[: len(table)], results[len(table) : -1], results[-1]
 
 
-def chunk_sums(chunk, following, ids, hidden, weight, table, held, after):
+def chunk_sums(chunk, following, ahead_next, early, ids, hidden, weight, table, held, after):
     local, sources, capacity, depth = hidden.shape
     tokens = table[0].shape[-2]
     ahead, _, columns = held.shape
     brought = max(local - ahead, 1)
     groups = len(table)
-    outs = group_shapes(groups == 2, sources, tokens, columns)
+    outs = group_shapes(groups == 2, sources, tokens, columns - early)
+    if early:
+        outs.append(shape(groups * tokens, early))
     if following:
-        outs.append(shape(ahead, depth, columns_of(following)))
+        outs.append(shape(min(ahead_next, local), depth, columns_of(following)))
     flops = 2 * sources * local * capacity * columns * (depth + tokens)
     results = pl.pallas_call(
-        functools.partial(chunk_kernel, chunk, following, groups),
+        functools.partial(chunk_kernel, chunk, following, groups, early),
         in_specs=[SMEM, VMEM, HBM, VMEM] + [VMEM] * groups + [ANY],
         out_specs=[VMEM] * len(outs),
         out_shape=outs,
@@ -280,22 +291,23 @@
             pltpu.VMEM((brought, depth, columns), BF16),
             pltpu.VMEM((sources, local * capacity, columns), BF16),
             pltpu.SemaphoreType.DMA((brought,)),
-            pltpu.SemaphoreType.DMA((ahead,)),
+            pltpu.SemaphoreType.DMA((local,)),
         ],
         cost_estimate=cost(flops, local * depth * columns) if following else COST,
-        compiler_params=pltpu.CompilerParams(vmem_limit_bytes=28 << 20),
+        compiler_params=pltpu.CompilerParams(vmem_limit_bytes=20 << 20),
         name="chunk",
     )(ids, hidden, weight, held, *table, after)
-    return results[:groups], results[groups] if following else None
-
-
-def fold(width, terms, after, dtype=BF16, flops=1000):
+    results = list(results)
+    return results[:groups], results[groups] if early else None, results[-1] if following else None
+
+
+def fold(tokens, width, terms, after, dtype=BF16, flops=1000):
     arrays, spans = [term[0] for term in terms], [term[1:] for term in terms]
     return pl.pallas_call(
         functools.partial(fold_kernel, spans),
         in_specs=[VMEM] * len(terms) + [ANY],
         out_specs=VMEM,
-        out_shape=jax.ShapeDtypeStruct((arrays[0].shape[0], width), dtype),
+        out_shape=jax.ShapeDtypeStruct((tokens, width), dtype),
         cost_estimate=cost(flops, 1000),
         compiler_params=pltpu.CompilerParams(vmem_limit_bytes=6 << 20),
         name="fold",
@@ -315,56 +327,51 @@
     else:
         routes, scores = [lax.all_gather(routes, "expert")], [lax.all_gather(scores, "expert")]
 
+    third = features // 3
     chunks = [
-        tuple((block, start * features // 3, stop * features // 3, features) for block, start, stop in chunk)
-        for chunk in CHUNKS
+        tuple((block, start * third, stop * third, features) for block, start, stop in chunk) for chunk in CHUNKS
     ]
-    over, along = [], {}
 
     def send_over(sums):
         if pair:
-            over.append([sums[1], lax.ppermute(sums[0], "expert", swap)])
-        else:
-            whole = lax.psum_scatter(sums[0], "expert", scatter_dimension=0, tiled=True)
-            over.append([whole.reshape(tokens, -1)])
-
-    def terms(i, block, base):
-        column = 0
-        for which, start, stop, _ in chunks[i]:
-            if which == block:
-                found = [(array, column, start - base, stop - start) for array in over[i]]
-                for array, first, width in along.get(block, []):
-                    low, high = max(start, first), min(stop, first + width)
-                    if low < high:
-                        found.append((array, low - first, low - base, high - low))
-                return found
-            column += stop - start
-
-    def send_along(i, block, flip, after):
-        start, stop = next((start, stop) for which, start, stop, _ in chunks[i] if which == block)
-        total = fold(stop - start, terms(i, block, start), after)
-        got = lax.ppermute(total, "tp", [(r, r ^ flip) for r in range(ranks)])
-        along.setdefault(block ^ flip, []).append((got, start, stop - start))
-        return total
+            return [sums[1], lax.ppermute(sums[0], "expert", swap)]
+        return [lax.psum_scatter(sums[0], "expert", scatter_dimension=0, tiled=True).reshape(tokens, -1)]
+
+    def send_along(total, flip):
+        return lax.ppermute(total, "tp", [(r, r ^ flip) for r in range(ranks)])
+
+    def spans(arrays, source=0, at=0, width=features, row=0):
+        return [(array, row, source, at, width) for array in arrays]
+
+    def total(width, terms, after, dtype=BF16, flops=1000):
+        return fold(tokens, width, terms, after, dtype, flops)
 
     partial, hidden = first_products(chunks[0], ids, hidden, down_weight)
     table, sums, held = tables(chunks[1], ids, partial, down_weight, routes, scores, capacity)
-    send_over(sums)
-    sums, held = chunk_sums(chunks[1], chunks[2], ids, hidden, down_weight, table, held, ids)
-    send_over(sums)
-    total = send_along(0, 3, 1, sums[0])
-    sums, held = chunk_sums(chunks[2], chunks[3], ids, hidden, down_weight, table, held, total)
-    send_over(sums)
-    total = send_along(1, 2, 2, sums[0])
-    total = send_along(1, 1, 1, total)
-    sums, _ = chunk_sums(chunks[3], None, ids, hidden, down_weight, table, held, total)
-    send_over(sums)
-    send_along(2, 1, 1, sums[0])
-    far, near, last = [(array, 0, first, width) for array, first, width in along[0]]
-    here = [(residual, 0, 0, features)]
-    rest = fold(features, here + [far, near] + [(a, c, at, w) for a, c, at, w in terms(2, 0, 0)[: len(over[2])]], ids, f32, LATE)
-    rest = fold(features, [(rest, 0, 0, features)] + terms(3, 0, 0)[: len(over[3])], ids, f32, LATE)
-    return fold(features, [(rest, 0, 0, features), last], ids)
+    over3 = send_over(sums)
+    sums, _, held = chunk_sums(chunks[1], chunks[2], AHEAD[1], 0, ids, hidden, down_weight, table, held, ids)
+    over2 = send_over(sums)
+    total3 = total(features, spans(over3), sums[0])
+    near2 = send_along(total3, 1)
+    early = third if pair else 0
+    sums, part, held = chunk_sums(chunks[2], chunks[3], AHEAD[2], early, ids, hidden, down_weight, table, held, total3)
+    over1 = send_over(sums)
+    parts = [send_along(part[at : at + tokens], 1) for at in (0, tokens)] if pair else []
+    total2 = total(features, spans(over2 + [near2]), sums[0])
+    far0 = send_along(total2, 2)
+    sums, _, _ = chunk_sums(chunks[3], None, 0, 0, ids, hidden, down_weight, table, held, total2)
+    kept = features - early
+    if pair:
+        over0 = spans([sums[1], lax.ppermute(sums[0][:, :kept], "expert", swap)], width=kept)
+        late = total(early, spans(sums[:1], kept, 0, early) + spans(parts[:1], width=early), ids)
+        ends = spans([sums[1]], kept, kept, early) + spans([lax.ppermute(late, "expert", swap), parts[1]], 0, kept, early)
+    else:
+        over0, ends = spans(send_over(sums)), []
+    near0 = send_along(total(kept, spans(over1, width=kept), sums[0]), 1)
+    rest = total(features, spans([residual, far0]), ids, f32, LATE)
+    for terms in (over0, ends):
+        rest = total(features, spans([rest]) + terms, ids, f32, LATE) if terms else rest
+    return total(features, spans([rest]) + spans([near0], width=kept), ids)
 
 
 def solution(mesh):

time: 63.8 us -> 61.2 us (0.959)
  waiting for transfers between devices: 10.7 us -> 6.97 us
  starting transfers between devices: 14.9 us -> 17.3 us
  Pallas kernels: 37.9 us -> 36.5 us
    ppermute x8 -> x10, waiting for transfers between devices: 10.7 us -> 6.96 us  [the longest x1 4.9 us: on_device(): lax.ppermute(sums[0][:, :kept], 'expert', swap)]
    ppermute x8 -> x10, starting transfers between devices: 11.9 us -> 14.3 us  [the longest x5 8.58 us: send_along(): return lax.ppermute(total, 'tp', [(r, r ^ flip) for r in range(ranks)])]
    pallas_call x3, Pallas kernels: 23.2 us -> 22.2 us  [chunk_sums(): pl.pallas_call(functools.partial(chunk_kernel, chunk, following, groups,...]
    pallas_call x7 -> x8, Pallas kernels: 1.36 us -> 1.38 us  [fold(): pl.pallas_call(functools.partial(fold_kernel, spans), in_specs=[VMEM] * l...]
  transfers between devices with their start and end apart: 10 -> 12, of which waited for: 5 -> 4; matrix products, arithmetic and copies ran while one was open for 0% -> 0% of each run, Pallas kernels for 51% -> 52%
where the time goes in v5:
time: 61.2 us; the launch traced here: 61.1 us
  Pallas kernels  36.5 us (60%)
  starting transfers between devices  17.3 us (28%)
  waiting for transfers between devices  6.97 us (11%)
    pallas_call x3, Pallas kernels, chunk_sums(): pl.pallas_call(functools.partial(chunk_kernel, chunk, following, groups,...  22.2 us
    pallas_call x1, Pallas kernels, first_products(): pl.pallas_call(functools.partial(first_kernel, chunk), in_specs=[SMEM, HB...  8.92 us
    ppermute x5, starting transfers between devices, send_along(): return lax.ppermute(total, 'tp', [(r, r ^ flip) for r in range(ranks)])  8.58 us
    ppermute x1, waiting for transfers between devices, on_device(): lax.ppermute(sums[0][:, :kept], 'expert', swap)  4.9 us
    pallas_call x1, Pallas kernels, tables(): pl.pallas_call(functools.partial(table_kernel, following, pair, capacity)...  4.07 us
    ppermute x3, starting transfers between devices, send_over(): return [sums[1], lax.ppermute(sums[0], 'expert', swap)]  3.66 us
    ppermute x1, starting transfers between devices, on_device(): lax.ppermute(routes, 'expert', swap)  2.97 us
    pallas_call x8, Pallas kernels, fold(): pl.pallas_call(functools.partial(fold_kernel, spans), in_specs=[VMEM] * l...  1.38 us
  transfers between devices with their start and end apart: 12, of which 4 were waited for; matrix products, arithmetic and copies ran while one was open for 0% of the time, Pallas kernels for 52%

profile of v5, /device:TPU:0, one launch (start us, length us, event | category | flops | bytes accessed | tf_op | source)
XLA Modules:
  0.0 61.1 jit_solution(3527128702853242116)
XLA Ops:
  0.0 3.0 %collective-permute-start = (s32[4,256]{1,0:T(4,128)}, s32[4,256]{1,0:T(4,128)S(1)}, u32[]{:S(2)}, u32[]{:S(2)}) collective-permute-start(s32[4,256]{1,0:T(4,128)} %bitcast.4), channel_id=1, source_target_pairs={{0,4},{4,0},{1,5},{5,1},{2,6},{6,2},{3,7},{7,3},{8,12},{12,8},{9,1... | collective-permute-start | bytes 12296 | tf_op jit(solution)/shard_map/ppermute | solution.py:326
  3.0 0.0 collective-permute-start.1
  3.0 0.1 pad_add_fusion.ids_ref.refs_0_.refs_2_.refs_3_.refs_4_
  3.1 8.9 %first.1 = (bf16[2,768,768]{2,1,0:T(8,128)(2,1)S(1)}, bf16[8,2,96,1408]{3,2,1,0:T(8,128)(2,1)S(1)}) custom-call(s32[2]{0:T(128)S(1)} %pad_add_fusion.ids_ref.refs_0_.refs_2_.refs_3_.refs_4_, bf16[8,2,96,1408]{3,2,1,0:T(8,128)(2,1)} %hidden_ref.1, bf16[8,1408,3072]{2,1,0:T(8,128)(2,1)} %weight_ref.7), custom_call_target="tpu_custom_call" | custom-call | flops 3321888768 | bytes 17301504 | tf_op jit(solution)/shard_map/first/pallas_call | solution.py:232
  12.0 0.0 collective-permute-done.refs_3_
  12.1 4.1 %tables.1 = (bf16[256,768]{1,0:T(8,128)(2,1)S(1)}, bf16[256,768]{1,0:T(8,128)(2,1)S(1)}, bf16[256,768]{1,0:T(8,128)(2,1)S(1)}, bf16[256,768]{1,0:T(8,128)(2,1)S(1)}, bf16[2,1408,768]{2,1,0:T(8,128)(2,1)S(1)}) custom-call(s32[2]{0:T(128)S(1)} %pad_add_fusion.ids_ref.refs_0_.refs_2_.refs_3_.refs_4_, bf16[2,768,768]{2,1,0:T(8,128)(2,1)S(1)} %get-tuple-element.22.refs_1_, ...), custom_call_target="tpu_custom_call" | custom-call | flops 1000 | bytes 2000 | tf_op jit(solution)/shard_map/tables/pallas_call | solution.py:260
  16.1 2.1 %collective-permute-start.3 = (bf16[256,768]{1,0:T(8,128)(2,1)S(1)}, bf16[256,768]{1,0:T(8,128)(2,1)S(1)}, u32[]{:S(2)}, u32[]{:S(2)}) collective-permute-start(bf16[256,768]{1,0:T(8,128)(2,1)S(1)} %get-tuple-element.29), channel_id=1, source_target_pairs={{0,4},{4,0},{1,5},{5,1},{2,6},{6,2},{3,7},{7,3},{8,12},{12,8},{9,1... | collective-permute-start | bytes 1179656 | tf_op jit(solution)/shard_map/ppermute | solution.py:337
  18.2 7.8 %chunk.3 = (bf16[256,768]{1,0:T(8,128)(2,1)S(1)}, bf16[256,768]{1,0:T(8,128)(2,1)S(1)}, bf16[3,1408,768]{2,1,0:T(8,128)(2,1)S(1)}) custom-call(s32[2]{0:T(128)S(1)} %pad_add_fusion.ids_ref.refs_0_.refs_2_.refs_3_.refs_4_, bf16[8,2,96,1408]{3,2,1,0:T(8,128)(2,1)S(1)} %get-tuple-element.21.hidden_ref, bf16[8,1408,3072]{2,1,0:T(8,128)(2,1)} %weight_ref.7, ...), custom_call_target="tpu_custom_call" | custom-call | flops 3925868544 | bytes 17301504 | tf_op jit(solution)/shard_map/chunk/pallas_call | solution.py:285
  26.0 0.1 collective-permute-start.2
  26.1 0.7 %collective-permute-done.3.refs_1_ = bf16[256,768]{1,0:T(8,128)(2,1)S(1)} collective-permute-done((bf16[256,768]{1,0:T(8,128)(2,1)S(1)}, bf16[256,768]{1,0:T(8,128)(2,1)S(1)}, u32[]{:S(2)}, u32[]{:S(2)}) %collective-permute-start.3) | collective-permute-done | bytes 393248 | tf_op jit(solution)/shard_map/ppermute | solution.py:337
  26.8 0.1 fold.8.refs_2_
  26.9 1.9 %collective-permute-start.4 = (bf16[256,768]{1,0:T(8,128)(2,1)S(1)}, bf16[256,768]{1,0:T(8,128)(2,1)S(1)}, u32[]{:S(2)}, u32[]{:S(2)}) collective-permute-start(bf16[256,768]{1,0:T(8,128)(2,1)S(1)} %fold.8.refs_2_), channel_id=1, source_target_pairs={{0,1},{1,0},{2,3},{3,2},{4,5},{5,4},{6,7},{7,6},{8,9},{9,8},{10,11... | collective-permute-start | bytes 1179656 | tf_op jit(solution)/shard_map/ppermute | solution.py:341
  28.8 7.3 %chunk.4 = (bf16[256,512]{1,0:T(8,128)(2,1)S(1)}, bf16[256,512]{1,0:T(8,128)(2,1)S(1)}, bf16[512,256]{1,0:T(8,128)(2,1)S(1)}, bf16[3,1408,768]{2,1,0:T(8,128)(2,1)S(1)}) custom-call(s32[2]{0:T(128)S(1)} %pad_add_fusion.ids_ref.refs_0_.refs_2_.refs_3_.refs_4_, bf16[8,2,96,1408]{3,2,1,0:T(8,128)(2,1)S(1)} %get-tuple-element.21.hidden_ref, ...), custom_call_target="tpu_custom_call" | custom-call | flops 3925868544 | bytes 17301504 | tf_op jit(solution)/shard_map/chunk/pallas_call | solution.py:285
  36.1 0.0 collective-permute-done.2.refs_1_
  36.1 0.5 collective-permute-done.4.refs_2_
  36.6 0.1 fold.9.refs_2_
  36.8 2.8 %collective-permute-start.5 = (bf16[256,768]{1,0:T(8,128)(2,1)S(1)}, bf16[256,768]{1,0:T(8,128)(2,1)S(1)}, u32[]{:S(2)}, u32[]{:S(2)}) collective-permute-start(bf16[256,768]{1,0:T(8,128)(2,1)S(1)} %fold.9.refs_2_), channel_id=1, source_target_pairs={{0,2},{1,3},{2,0},{3,1},{4,6},{5,7},{6,4},{7,5},{8,10},{9,11},{10,... | collective-permute-start | bytes 1179656 | tf_op jit(solution)/shard_map/ppermute | solution.py:341
  39.5 1.5 %collective-permute-start.10 = (bf16[256,512]{1,0:T(8,128)(2,1)S(1)}, bf16[256,512]{1,0:T(8,128)(2,1)S(1)}, u32[]{:S(2)}, u32[]{:S(2)}) collective-permute-start(bf16[256,512]{1,0:T(8,128)(2,1)S(1)} %get-tuple-element.31.refs_3_), channel_id=1, source_target_pairs={{0,4},{4,0},{1,5},{5,1},{2,6},{6,2},{3,7},{7,3},{8,12},{12,8},{9,1... | collective-permute-start | bytes 786440 | tf_op jit(solution)/shard_map/ppermute | solution.py:337
  41.1 1.8 %collective-permute-start.7 = (bf16[256,256]{1,0:T(8,128)(2,1)S(1)}, bf16[256,256]{1,0:T(8,128)(2,1)S(1)}, u32[]{:S(2)}, u32[]{:S(2)}) collective-permute-start(bf16[256,256]{1,0:T(8,128)(2,1)S(1)} %get-tuple-element.38), channel_id=1, source_target_pairs={{0,1},{1,0},{2,3},{3,2},{4,5},{5,4},{6,7},{7,6},{8,9},{9,8},{10,11... | collective-permute-start | bytes 393224 | tf_op jit(solution)/shard_map/ppermute | solution.py:341
  42.9 0.3 collective-permute-start.9
  43.2 7.1 %chunk.5 = (bf16[256,768]{1,0:T(8,128)(2,1)S(1)}, bf16[256,768]{1,0:T(8,128)(2,1)S(1)}) custom-call(s32[2]{0:T(128)S(1)} %pad_add_fusion.ids_ref.refs_0_.refs_2_.refs_3_.refs_4_, bf16[8,2,96,1408]{3,2,1,0:T(8,128)(2,1)S(1)} %get-tuple-element.21.hidden_ref, bf16[8,1408,3072]{2,1,0:T(8,128)(2,1)} %weight_ref.7, ...), custom_call_target="tpu_custom_call" | custom-call | flops 1000 | bytes 2000 | tf_op jit(solution)/shard_map/chunk/pallas_call | solution.py:285
  50.3 0.1 fold.14
  50.4 1.8 %collective-permute-start.11 = (bf16[256,512]{1,0:T(8,128)(2,1)S(1)}, bf16[256,512]{1,0:T(8,128)(2,1)S(1)}, u32[]{:S(2)}, u32[]{:S(2)}) collective-permute-start(bf16[256,512]{1,0:T(8,128)(2,1)S(1)} %fold.14), channel_id=1, source_target_pairs={{0,1},{1,0},{2,3},{3,2},{4,5},{5,4},{6,7},{7,6},{8,9},{9,8},{10,11... | collective-permute-start | bytes 786440 | tf_op jit(solution)/shard_map/ppermute | solution.py:341
  52.2 1.3 %collective-permute-start.8 = (bf16[256,256]{1,0:T(8,128)(2,1)S(1)}, bf16[256,256]{1,0:T(8,128)(2,1)S(1)}, u32[]{:S(2)}, u32[]{:S(2)}) collective-permute-start(bf16[256,256]{1,0:T(8,128)(2,1)S(1)} %fold.12), channel_id=1, source_target_pairs={{0,4},{4,0},{1,5},{5,1},{2,6},{6,2},{3,7},{7,3},{8,12},{12,8},{9,1... | collective-permute-start | bytes 393224 | tf_op jit(solution)/shard_map/ppermute | solution.py:367
  53.5 0.8 %collective-permute-start.6 = (bf16[256,512]{1,0:T(8,128)(2,1)S(1)}, bf16[256,512]{1,0:T(8,128)(2,1)S(1)}, u32[]{:S(2)}, u32[]{:S(2)}) collective-permute-start(bf16[256,512]{1,0:T(8,128)(2,1)S(1)} %slice.9), channel_id=1, source_target_pairs={{0,4},{4,0},{1,5},{5,1},{2,6},{6,2},{3,7},{7,3},{8,12},{12,8},{9,1... | collective-permute-start | bytes 786440 | tf_op jit(solution)/shard_map/ppermute | solution.py:365
  54.3 0.8 %collective-permute-done.5.refs_1_ = bf16[256,768]{1,0:T(8,128)(2,1)S(1)} collective-permute-done((bf16[256,768]{1,0:T(8,128)(2,1)S(1)}, bf16[256,768]{1,0:T(8,128)(2,1)S(1)}, u32[]{:S(2)}, u32[]{:S(2)}) %collective-permute-start.5) | collective-permute-done | bytes 393248 | tf_op jit(solution)/shard_map/ppermute | solution.py:341
  55.1 0.1 fold.10.refs_0_
  55.2 4.9 %collective-permute-done.6.refs_2_ = bf16[256,512]{1,0:T(8,128)(2,1)S(1)} collective-permute-done((bf16[256,512]{1,0:T(8,128)(2,1)S(1)}, bf16[256,512]{1,0:T(8,128)(2,1)S(1)}, u32[]{:S(2)}, u32[]{:S(2)}) %collective-permute-start.6) | collective-permute-done | bytes 262176 | tf_op jit(solution)/shard_map/ppermute | solution.py:365
  60.0 0.1 fold.11.refs_0_
  60.2 0.1 fold.13.refs_0_
  60.3 0.0 collective-permute-done.11.refs_1_
  60.3 0.8 %fold.15 = bf16[256,768]{1,0:T(8,128)(2,1)} custom-call(f32[256,768]{1,0:T(8,128)S(1)} %fold.13.refs_0_, bf16[256,512]{1,0:T(8,128)(2,1)S(1)} %collective-permute-done.11.refs_1_, s32[2]{0:T(128)S(1)} %pad_add_fusion.ids_ref.refs_0_.refs_2_.refs_3_.refs_4_), custom_call_target="tpu_custom_call" | custom-call | flops 1000 | bytes 2000 | tf_op jit(solution)/shard_map/fold/pallas_call | solution.py:306
  (14 shorter events, 0.1 us)
Async XLA Ops:
  0.0 12.0 %collective-permute-start = (s32[4,256]{1,0:T(4,128)}, s32[4,256]{1,0:T(4,128)S(1)}, u32[]{:S(2)}, u32[]{:S(2)}) collective-permute-start(s32[4,256]{1,0:T(4,128)} %bitcast.4), channel_id=1, source_target_pairs={{0,4},{4,0},{1,5},{5,1},{2,6},{6,2},{3,7},{7,3},{8,12},{12,8},{9,1... | collective-permute-start | bytes 12296 | tf_op jit(solution)/shard_map/ppermute | solution.py:326
  3.0 9.1 %collective-permute-start.1 = (f32[4,256]{1,0:T(4,128)}, f32[4,256]{1,0:T(4,128)S(1)}, u32[]{:S(2)}, u32[]{:S(2)}) collective-permute-start(f32[4,256]{1,0:T(4,128)} %bitcast.6), channel_id=1, source_target_pairs={{0,4},{4,0},{1,5},{5,1},{2,6},{6,2},{3,7},{7,3},{8,12},{12,8},{9,1... | collective-permute-start | bytes 12296 | tf_op jit(solution)/shard_map/ppermute | solution.py:326
  3.1 9.0 %copy-start = (s32[256,4]{0,1:T(4,128)S(1)}, s32[256,4]{0,1:T(4,128)}, u32[]{:S(2)}) copy-start(s32[256,4]{0,1:T(4,128)} %param.7) | copy-start | bytes 12292
  3.1 9.0 %copy-start.1 = (f32[256,4]{0,1:T(4,128)S(1)}, f32[256,4]{0,1:T(4,128)}, u32[]{:S(2)}) copy-start(f32[256,4]{0,1:T(4,128)} %param.8) | copy-start | bytes 12292
  16.1 10.7 %collective-permute-start.3 = (bf16[256,768]{1,0:T(8,128)(2,1)S(1)}, bf16[256,768]{1,0:T(8,128)(2,1)S(1)}, u32[]{:S(2)}, u32[]{:S(2)}) collective-permute-start(bf16[256,768]{1,0:T(8,128)(2,1)S(1)} %get-tuple-element.29), channel_id=1, source_target_pairs={{0,4},{4,0},{1,5},{5,1},{2,6},{6,2},{3,7},{7,3},{8,12},{12,8},{9,1... | collective-permute-start | bytes 1179656 | tf_op jit(solution)/shard_map/ppermute | solution.py:337
  26.0 10.1 %collective-permute-start.2 = (bf16[256,768]{1,0:T(8,128)(2,1)S(1)}, bf16[256,768]{1,0:T(8,128)(2,1)S(1)}, u32[]{:S(2)}, u32[]{:S(2)}) collective-permute-start(bf16[256,768]{1,0:T(8,128)(2,1)S(1)} %get-tuple-element.27.refs_2_), channel_id=1, source_target_pairs={{0,4},{4,0},{1,5},{5,1},{2,6},{6,2},{3,7},{7,3},{8,12},{12,8},{9,1... | collective-permute-start | bytes 1179656 | tf_op jit(solution)/shard_map/ppermute | solution.py:337
  26.9 9.7 %collective-permute-start.4 = (bf16[256,768]{1,0:T(8,128)(2,1)S(1)}, bf16[256,768]{1,0:T(8,128)(2,1)S(1)}, u32[]{:S(2)}, u32[]{:S(2)}) collective-permute-start(bf16[256,768]{1,0:T(8,128)(2,1)S(1)} %fold.8.refs_2_), channel_id=1, source_target_pairs={{0,1},{1,0},{2,3},{3,2},{4,5},{5,4},{6,7},{7,6},{8,9},{9,8},{10,11... | collective-permute-start | bytes 1179656 | tf_op jit(solution)/shard_map/ppermute | solution.py:341
  36.8 18.3 %collective-permute-start.5 = (bf16[256,768]{1,0:T(8,128)(2,1)S(1)}, bf16[256,768]{1,0:T(8,128)(2,1)S(1)}, u32[]{:S(2)}, u32[]{:S(2)}) collective-permute-start(bf16[256,768]{1,0:T(8,128)(2,1)S(1)} %fold.9.refs_2_), channel_id=1, source_target_pairs={{0,2},{1,3},{2,0},{3,1},{4,6},{5,7},{6,4},{7,5},{8,10},{9,11},{10,... | collective-permute-start | bytes 1179656 | tf_op jit(solution)/shard_map/ppermute | solution.py:341
  39.5 10.7 %collective-permute-start.10 = (bf16[256,512]{1,0:T(8,128)(2,1)S(1)}, bf16[256,512]{1,0:T(8,128)(2,1)S(1)}, u32[]{:S(2)}, u32[]{:S(2)}) collective-permute-start(bf16[256,512]{1,0:T(8,128)(2,1)S(1)} %get-tuple-element.31.refs_3_), channel_id=1, source_target_pairs={{0,4},{4,0},{1,5},{5,1},{2,6},{6,2},{3,7},{7,3},{8,12},{12,8},{9,1... | collective-permute-start | bytes 786440 | tf_op jit(solution)/shard_map/ppermute | solution.py:337
  41.1 11.1 %collective-permute-start.7 = (bf16[256,256]{1,0:T(8,128)(2,1)S(1)}, bf16[256,256]{1,0:T(8,128)(2,1)S(1)}, u32[]{:S(2)}, u32[]{:S(2)}) collective-permute-start(bf16[256,256]{1,0:T(8,128)(2,1)S(1)} %get-tuple-element.38), channel_id=1, source_target_pairs={{0,1},{1,0},{2,3},{3,2},{4,5},{5,4},{6,7},{7,6},{8,9},{9,8},{10,11... | collective-permute-start | bytes 393224 | tf_op jit(solution)/shard_map/ppermute | solution.py:341
  42.9 17.3 %collective-permute-start.9 = (bf16[256,256]{1,0:T(8,128)(2,1)S(1)}, bf16[256,256]{1,0:T(8,128)(2,1)S(1)}, u32[]{:S(2)}, u32[]{:S(2)}) collective-permute-start(bf16[256,256]{1,0:T(8,128)(2,1)S(1)} %get-tuple-element.37), channel_id=1, source_target_pairs={{0,1},{1,0},{2,3},{3,2},{4,5},{5,4},{6,7},{7,6},{8,9},{9,8},{10,11... | collective-permute-start | bytes 393224 | tf_op jit(solution)/shard_map/ppermute | solution.py:341
  43.2 11.9 %copy-start.2 = (bf16[256,768]{1,0:T(8,128)(2,1)S(1)}, bf16[256,768]{1,0:T(8,128)(2,1)}, u32[]{:S(2)}) copy-start(bf16[256,768]{1,0:T(8,128)(2,1)} %refs_0_.1) | copy-start | bytes 1179652
  50.4 9.9 %collective-permute-start.11 = (bf16[256,512]{1,0:T(8,128)(2,1)S(1)}, bf16[256,512]{1,0:T(8,128)(2,1)S(1)}, u32[]{:S(2)}, u32[]{:S(2)}) collective-permute-start(bf16[256,512]{1,0:T(8,128)(2,1)S(1)} %fold.14), channel_id=1, source_target_pairs={{0,1},{1,0},{2,3},{3,2},{4,5},{5,4},{6,7},{7,6},{8,9},{9,8},{10,11... | collective-permute-start | bytes 786440 | tf_op jit(solution)/shard_map/ppermute | solution.py:341
  52.2 7.9 %collective-permute-start.8 = (bf16[256,256]{1,0:T(8,128)(2,1)S(1)}, bf16[256,256]{1,0:T(8,128)(2,1)S(1)}, u32[]{:S(2)}, u32[]{:S(2)}) collective-permute-start(bf16[256,256]{1,0:T(8,128)(2,1)S(1)} %fold.12), channel_id=1, source_target_pairs={{0,4},{4,0},{1,5},{5,1},{2,6},{6,2},{3,7},{7,3},{8,12},{12,8},{9,1... | collective-permute-start | bytes 393224 | tf_op jit(solution)/shard_map/ppermute | solution.py:367
  53.5 6.5 %collective-permute-start.6 = (bf16[256,512]{1,0:T(8,128)(2,1)S(1)}, bf16[256,512]{1,0:T(8,128)(2,1)S(1)}, u32[]{:S(2)}, u32[]{:S(2)}) collective-permute-start(bf16[256,512]{1,0:T(8,128)(2,1)S(1)} %slice.9), channel_id=1, source_target_pairs={{0,4},{4,0},{1,5},{5,1},{2,6},{6,2},{3,7},{7,3},{8,12},{12,8},{9,1... | collective-permute-start | bytes 786440 | tf_op jit(solution)/shard_map/ppermute | solution.py:365

commit v6 on v5

--- a/solution.py
+++ b/solution.py
@@ -362,9 +362,9 @@
     sums, _, _ = chunk_sums(chunks[3], None, 0, 0, ids, hidden, down_weight, table, held, total2)
     kept = features - early
     if pair:
-        over0 = spans([sums[1], lax.ppermute(sums[0][:, :kept], "expert", swap)], width=kept)
-        late = total(early, spans(sums[:1], kept, 0, early) + spans(parts[:1], width=early), ids)
-        ends = spans([sums[1]], kept, kept, early) + spans([lax.ppermute(late, "expert", swap), parts[1]], 0, kept, early)
+        late = total(features, spans(sums[:1]) + spans(parts[:1], 0, kept, early), ids)
+        over0 = spans([sums[1], lax.ppermute(late, "expert", swap)])
+        ends = spans([parts[1]], 0, kept, early)
     else:
         over0, ends = spans(send_over(sums)), []
     near0 = send_along(total(kept, spans(over1, width=kept), sums[0]), 1)

time: 61.2 us -> 61.2 us (level)
  waiting for transfers between devices: 6.97 us -> 7.72 us
  starting transfers between devices: 17.3 us -> 16.6 us
    ppermute x5, waiting for transfers between devices: 1.34 us -> 2.11 us  [send_along(): return lax.ppermute(total, 'tp', [(r, r ^ flip) for r in range(ranks)])]
    ppermute x2 -> x1, starting transfers between devices: 2.09 us -> 1.34 us  [on_device(): over0 = spans([sums[1], lax.ppermute(late, 'expert', swap)])]
    ppermute x2 -> x1, waiting for transfers between devices: 4.9 us -> 4.89 us  [on_device(): over0 = spans([sums[1], lax.ppermute(late, 'expert', swap)])]
  transfers between devices with their start and end apart: 12 -> 11, of which waited for: 4 -> 5; matrix products, arithmetic and copies ran while one was open for 0% -> 0% of each run, Pallas kernels for 52% -> 52%
where the time goes in v6:
time: 61.2 us; the launch traced here: 61.1 us
  Pallas kernels  36.6 us (60%)
  starting transfers between devices  16.6 us (27%)
  waiting for transfers between devices  7.72 us (13%)
    pallas_call x3, Pallas kernels, chunk_sums(): pl.pallas_call(functools.partial(chunk_kernel, chunk, following, groups,...  22.2 us
    pallas_call x1, Pallas kernels, first_products(): pl.pallas_call(functools.partial(first_kernel, chunk), in_specs=[SMEM, HB...  8.92 us
    ppermute x5, starting transfers between devices, send_along(): return lax.ppermute(total, 'tp', [(r, r ^ flip) for r in range(ranks)])  8.58 us
    ppermute x1, waiting for transfers between devices, on_device(): over0 = spans([sums[1], lax.ppermute(late, 'expert', swap)])  4.89 us
    pallas_call x1, Pallas kernels, tables(): pl.pallas_call(functools.partial(table_kernel, following, pair, capacity)...  4.07 us
    ppermute x3, starting transfers between devices, send_over(): return [sums[1], lax.ppermute(sums[0], 'expert', swap)]  3.66 us
    ppermute x1, starting transfers between devices, on_device(): lax.ppermute(routes, 'expert', swap)  2.97 us
    ppermute x5, waiting for transfers between devices, send_along(): return lax.ppermute(total, 'tp', [(r, r ^ flip) for r in range(ranks)])  2.11 us
  transfers between devices with their start and end apart: 11, of which 5 were waited for; matrix products, arithmetic and copies ran while one was open for 0% of the time, Pallas kernels for 52%

profile of v6, /device:TPU:0, one launch (start us, length us, event | category | flops | bytes accessed | tf_op | source)
XLA Modules:
  0.0 61.1 jit_solution(18195919514944883630)
XLA Ops:
  0.0 3.0 %collective-permute-start = (s32[4,256]{1,0:T(4,128)}, s32[4,256]{1,0:T(4,128)S(1)}, u32[]{:S(2)}, u32[]{:S(2)}) collective-permute-start(s32[4,256]{1,0:T(4,128)} %bitcast.4), channel_id=1, source_target_pairs={{0,4},{4,0},{1,5},{5,1},{2,6},{6,2},{3,7},{7,3},{8,12},{12,8},{9,1... | collective-permute-start | bytes 12296 | tf_op jit(solution)/shard_map/ppermute | solution.py:326
  3.0 0.0 collective-permute-start.1
  3.0 0.1 pad_add_fusion.ids_ref.refs_0_.refs_2_.refs_3_
  3.1 8.9 %first.1 = (bf16[2,768,768]{2,1,0:T(8,128)(2,1)S(1)}, bf16[8,2,96,1408]{3,2,1,0:T(8,128)(2,1)S(1)}) custom-call(s32[2]{0:T(128)S(1)} %pad_add_fusion.ids_ref.refs_0_.refs_2_.refs_3_, bf16[8,2,96,1408]{3,2,1,0:T(8,128)(2,1)} %hidden_ref.1, bf16[8,1408,3072]{2,1,0:T(8,128)(2,1)} %weight_ref.7), custom_call_target="tpu_custom_call" | custom-call | flops 3321888768 | bytes 17301504 | tf_op jit(solution)/shard_map/first/pallas_call | solution.py:232
  12.0 0.0 collective-permute-done.1.refs_5_
  12.1 4.1 %tables.1 = (bf16[256,768]{1,0:T(8,128)(2,1)S(1)}, bf16[256,768]{1,0:T(8,128)(2,1)S(1)}, bf16[256,768]{1,0:T(8,128)(2,1)S(1)}, bf16[256,768]{1,0:T(8,128)(2,1)S(1)}, bf16[2,1408,768]{2,1,0:T(8,128)(2,1)S(1)}) custom-call(s32[2]{0:T(128)S(1)} %pad_add_fusion.ids_ref.refs_0_.refs_2_.refs_3_, bf16[2,768,768]{2,1,0:T(8,128)(2,1)S(1)} %get-tuple-element.22.refs_1_, ...), custom_call_target="tpu_custom_call" | custom-call | flops 1000 | bytes 2000 | tf_op jit(solution)/shard_map/tables/pallas_call | solution.py:260
  16.1 2.1 %collective-permute-start.3 = (bf16[256,768]{1,0:T(8,128)(2,1)S(1)}, bf16[256,768]{1,0:T(8,128)(2,1)S(1)}, u32[]{:S(2)}, u32[]{:S(2)}) collective-permute-start(bf16[256,768]{1,0:T(8,128)(2,1)S(1)} %get-tuple-element.29), channel_id=1, source_target_pairs={{0,4},{4,0},{1,5},{5,1},{2,6},{6,2},{3,7},{7,3},{8,12},{12,8},{9,1... | collective-permute-start | bytes 1179656 | tf_op jit(solution)/shard_map/ppermute | solution.py:337
  18.2 7.8 %chunk.3 = (bf16[256,768]{1,0:T(8,128)(2,1)S(1)}, bf16[256,768]{1,0:T(8,128)(2,1)S(1)}, bf16[3,1408,768]{2,1,0:T(8,128)(2,1)S(1)}) custom-call(s32[2]{0:T(128)S(1)} %pad_add_fusion.ids_ref.refs_0_.refs_2_.refs_3_, bf16[8,2,96,1408]{3,2,1,0:T(8,128)(2,1)S(1)} %get-tuple-element.21.hidden_ref, bf16[8,1408,3072]{2,1,0:T(8,128)(2,1)} %weight_ref.7, ...), custom_call_target="tpu_custom_call" | custom-call | flops 3925868544 | bytes 17301504 | tf_op jit(solution)/shard_map/chunk/pallas_call | solution.py:285
  26.0 0.1 collective-permute-start.2
  26.1 0.7 %collective-permute-done.3.refs_1_ = bf16[256,768]{1,0:T(8,128)(2,1)S(1)} collective-permute-done((bf16[256,768]{1,0:T(8,128)(2,1)S(1)}, bf16[256,768]{1,0:T(8,128)(2,1)S(1)}, u32[]{:S(2)}, u32[]{:S(2)}) %collective-permute-start.3) | collective-permute-done | bytes 393248 | tf_op jit(solution)/shard_map/ppermute | solution.py:337
  26.8 0.1 fold.8.refs_2_
  26.9 1.9 %collective-permute-start.4 = (bf16[256,768]{1,0:T(8,128)(2,1)S(1)}, bf16[256,768]{1,0:T(8,128)(2,1)S(1)}, u32[]{:S(2)}, u32[]{:S(2)}) collective-permute-start(bf16[256,768]{1,0:T(8,128)(2,1)S(1)} %fold.8.refs_2_), channel_id=1, source_target_pairs={{0,1},{1,0},{2,3},{3,2},{4,5},{5,4},{6,7},{7,6},{8,9},{9,8},{10,11... | collective-permute-start | bytes 1179656 | tf_op jit(solution)/shard_map/ppermute | solution.py:341
  28.8 7.3 %chunk.4 = (bf16[256,512]{1,0:T(8,128)(2,1)S(1)}, bf16[256,512]{1,0:T(8,128)(2,1)S(1)}, bf16[512,256]{1,0:T(8,128)(2,1)S(1)}, bf16[3,1408,768]{2,1,0:T(8,128)(2,1)S(1)}) custom-call(s32[2]{0:T(128)S(1)} %pad_add_fusion.ids_ref.refs_0_.refs_2_.refs_3_, bf16[8,2,96,1408]{3,2,1,0:T(8,128)(2,1)S(1)} %get-tuple-element.21.hidden_ref, ...), custom_call_target="tpu_custom_call" | custom-call | flops 3925868544 | bytes 17301504 | tf_op jit(solution)/shard_map/chunk/pallas_call | solution.py:285
  36.1 0.0 collective-permute-done.2.refs_1_
  36.1 0.5 collective-permute-done.4.refs_2_
  36.6 0.1 fold.9.refs_2_
  36.8 2.8 %collective-permute-start.5 = (bf16[256,768]{1,0:T(8,128)(2,1)S(1)}, bf16[256,768]{1,0:T(8,128)(2,1)S(1)}, u32[]{:S(2)}, u32[]{:S(2)}) collective-permute-start(bf16[256,768]{1,0:T(8,128)(2,1)S(1)} %fold.9.refs_2_), channel_id=1, source_target_pairs={{0,2},{1,3},{2,0},{3,1},{4,6},{5,7},{6,4},{7,5},{8,10},{9,11},{10,... | collective-permute-start | bytes 1179656 | tf_op jit(solution)/shard_map/ppermute | solution.py:341
  39.5 1.5 %collective-permute-start.9 = (bf16[256,512]{1,0:T(8,128)(2,1)S(1)}, bf16[256,512]{1,0:T(8,128)(2,1)S(1)}, u32[]{:S(2)}, u32[]{:S(2)}) collective-permute-start(bf16[256,512]{1,0:T(8,128)(2,1)S(1)} %get-tuple-element.31.refs_3_), channel_id=1, source_target_pairs={{0,4},{4,0},{1,5},{5,1},{2,6},{6,2},{3,7},{7,3},{8,12},{12,8},{9,1... | collective-permute-start | bytes 786440 | tf_op jit(solution)/shard_map/ppermute | solution.py:337
  41.1 1.8 %collective-permute-start.6 = (bf16[256,256]{1,0:T(8,128)(2,1)S(1)}, bf16[256,256]{1,0:T(8,128)(2,1)S(1)}, u32[]{:S(2)}, u32[]{:S(2)}) collective-permute-start(bf16[256,256]{1,0:T(8,128)(2,1)S(1)} %get-tuple-element.38), channel_id=1, source_target_pairs={{0,1},{1,0},{2,3},{3,2},{4,5},{5,4},{6,7},{7,6},{8,9},{9,8},{10,11... | collective-permute-start | bytes 393224 | tf_op jit(solution)/shard_map/ppermute | solution.py:341
  42.9 0.3 collective-permute-start.8
  43.2 7.1 %chunk.5 = (bf16[256,768]{1,0:T(8,128)(2,1)S(1)}, bf16[256,768]{1,0:T(8,128)(2,1)S(1)}) custom-call(s32[2]{0:T(128)S(1)} %pad_add_fusion.ids_ref.refs_0_.refs_2_.refs_3_, bf16[8,2,96,1408]{3,2,1,0:T(8,128)(2,1)S(1)} %get-tuple-element.21.hidden_ref, bf16[8,1408,3072]{2,1,0:T(8,128)(2,1)} %weight_ref.7, bf16[3,1408,768]{2,1,0:T(8,128)(2,1)S(1)} %get-tuple-element.32.held_ref, ...), custom_call_target="tpu_custom_call" | custom-call | flops 1000 | bytes 2000 | tf_op jit(solution)/shard_map/chunk/pallas_call | solution.py:285
  50.2 0.0 collective-permute-done.9.refs_1_
  50.3 0.1 fold.14
  50.3 1.8 %collective-permute-start.10 = (bf16[256,512]{1,0:T(8,128)(2,1)S(1)}, bf16[256,512]{1,0:T(8,128)(2,1)S(1)}, u32[]{:S(2)}, u32[]{:S(2)}) collective-permute-start(bf16[256,512]{1,0:T(8,128)(2,1)S(1)} %fold.14), channel_id=1, source_target_pairs={{0,1},{1,0},{2,3},{3,2},{4,5},{5,4},{6,7},{7,6},{8,9},{9,8},{10,11... | collective-permute-start | bytes 786440 | tf_op jit(solution)/shard_map/ppermute | solution.py:341
  52.2 1.3 %collective-permute-start.7 = (bf16[256,768]{1,0:T(8,128)(2,1)S(1)}, bf16[256,768]{1,0:T(8,128)(2,1)S(1)}, u32[]{:S(2)}, u32[]{:S(2)}) collective-permute-start(bf16[256,768]{1,0:T(8,128)(2,1)S(1)} %fold.11), channel_id=1, source_target_pairs={{0,4},{4,0},{1,5},{5,1},{2,6},{6,2},{3,7},{7,3},{8,12},{12,8},{9,1... | collective-permute-start | bytes 1179656 | tf_op jit(solution)/shard_map/ppermute | solution.py:366
  53.5 1.5 %collective-permute-done.5.refs_1_ = bf16[256,768]{1,0:T(8,128)(2,1)S(1)} collective-permute-done((bf16[256,768]{1,0:T(8,128)(2,1)S(1)}, bf16[256,768]{1,0:T(8,128)(2,1)S(1)}, u32[]{:S(2)}, u32[]{:S(2)}) %collective-permute-start.5) | collective-permute-done | bytes 393248 | tf_op jit(solution)/shard_map/ppermute | solution.py:341
  55.1 0.1 fold.10.refs_0_
  55.2 4.9 %collective-permute-done.7.refs_2_ = bf16[256,768]{1,0:T(8,128)(2,1)S(1)} collective-permute-done((bf16[256,768]{1,0:T(8,128)(2,1)S(1)}, bf16[256,768]{1,0:T(8,128)(2,1)S(1)}, u32[]{:S(2)}, u32[]{:S(2)}) %collective-permute-start.7) | collective-permute-done | bytes 393248 | tf_op jit(solution)/shard_map/ppermute | solution.py:366
  60.0 0.1 fold.12.refs_0_
  60.2 0.1 fold.13.refs_0_
  60.2 0.1 collective-permute-done.10.refs_1_
  60.3 0.8 %fold.15 = bf16[256,768]{1,0:T(8,128)(2,1)} custom-call(f32[256,768]{1,0:T(8,128)S(1)} %fold.13.refs_0_, bf16[256,512]{1,0:T(8,128)(2,1)S(1)} %collective-permute-done.10.refs_1_, s32[2]{0:T(128)S(1)} %pad_add_fusion.ids_ref.refs_0_.refs_2_.refs_3_), custom_call_target="tpu_custom_call" | custom-call | flops 1000 | bytes 2000 | tf_op jit(solution)/shard_map/fold/pallas_call | solution.py:306
  (11 shorter events, 0.1 us)
Async XLA Ops:
  0.0 12.0 %collective-permute-start = (s32[4,256]{1,0:T(4,128)}, s32[4,256]{1,0:T(4,128)S(1)}, u32[]{:S(2)}, u32[]{:S(2)}) collective-permute-start(s32[4,256]{1,0:T(4,128)} %bitcast.4), channel_id=1, source_target_pairs={{0,4},{4,0},{1,5},{5,1},{2,6},{6,2},{3,7},{7,3},{8,12},{12,8},{9,1... | collective-permute-start | bytes 12296 | tf_op jit(solution)/shard_map/ppermute | solution.py:326
  3.0 9.1 %collective-permute-start.1 = (f32[4,256]{1,0:T(4,128)}, f32[4,256]{1,0:T(4,128)S(1)}, u32[]{:S(2)}, u32[]{:S(2)}) collective-permute-start(f32[4,256]{1,0:T(4,128)} %bitcast.6), channel_id=1, source_target_pairs={{0,4},{4,0},{1,5},{5,1},{2,6},{6,2},{3,7},{7,3},{8,12},{12,8},{9,1... | collective-permute-start | bytes 12296 | tf_op jit(solution)/shard_map/ppermute | solution.py:326
  3.1 9.0 %copy-start = (s32[256,4]{0,1:T(4,128)S(1)}, s32[256,4]{0,1:T(4,128)}, u32[]{:S(2)}) copy-start(s32[256,4]{0,1:T(4,128)} %param.7) | copy-start | bytes 12292
  3.1 9.0 %copy-start.1 = (f32[256,4]{0,1:T(4,128)S(1)}, f32[256,4]{0,1:T(4,128)}, u32[]{:S(2)}) copy-start(f32[256,4]{0,1:T(4,128)} %param.8) | copy-start | bytes 12292
  16.1 10.7 %collective-permute-start.3 = (bf16[256,768]{1,0:T(8,128)(2,1)S(1)}, bf16[256,768]{1,0:T(8,128)(2,1)S(1)}, u32[]{:S(2)}, u32[]{:S(2)}) collective-permute-start(bf16[256,768]{1,0:T(8,128)(2,1)S(1)} %get-tuple-element.29), channel_id=1, source_target_pairs={{0,4},{4,0},{1,5},{5,1},{2,6},{6,2},{3,7},{7,3},{8,12},{12,8},{9,1... | collective-permute-start | bytes 1179656 | tf_op jit(solution)/shard_map/ppermute | solution.py:337
  26.0 10.1 %collective-permute-start.2 = (bf16[256,768]{1,0:T(8,128)(2,1)S(1)}, bf16[256,768]{1,0:T(8,128)(2,1)S(1)}, u32[]{:S(2)}, u32[]{:S(2)}) collective-permute-start(bf16[256,768]{1,0:T(8,128)(2,1)S(1)} %get-tuple-element.27.refs_2_), channel_id=1, source_target_pairs={{0,4},{4,0},{1,5},{5,1},{2,6},{6,2},{3,7},{7,3},{8,12},{12,8},{9,1... | collective-permute-start | bytes 1179656 | tf_op jit(solution)/shard_map/ppermute | solution.py:337
  26.9 9.7 %collective-permute-start.4 = (bf16[256,768]{1,0:T(8,128)(2,1)S(1)}, bf16[256,768]{1,0:T(8,128)(2,1)S(1)}, u32[]{:S(2)}, u32[]{:S(2)}) collective-permute-start(bf16[256,768]{1,0:T(8,128)(2,1)S(1)} %fold.8.refs_2_), channel_id=1, source_target_pairs={{0,1},{1,0},{2,3},{3,2},{4,5},{5,4},{6,7},{7,6},{8,9},{9,8},{10,11... | collective-permute-start | bytes 1179656 | tf_op jit(solution)/shard_map/ppermute | solution.py:341
  36.8 18.3 %collective-permute-start.5 = (bf16[256,768]{1,0:T(8,128)(2,1)S(1)}, bf16[256,768]{1,0:T(8,128)(2,1)S(1)}, u32[]{:S(2)}, u32[]{:S(2)}) collective-permute-start(bf16[256,768]{1,0:T(8,128)(2,1)S(1)} %fold.9.refs_2_), channel_id=1, source_target_pairs={{0,2},{1,3},{2,0},{3,1},{4,6},{5,7},{6,4},{7,5},{8,10},{9,11},{10,... | collective-permute-start | bytes 1179656 | tf_op jit(solution)/shard_map/ppermute | solution.py:341
  39.5 10.7 %collective-permute-start.9 = (bf16[256,512]{1,0:T(8,128)(2,1)S(1)}, bf16[256,512]{1,0:T(8,128)(2,1)S(1)}, u32[]{:S(2)}, u32[]{:S(2)}) collective-permute-start(bf16[256,512]{1,0:T(8,128)(2,1)S(1)} %get-tuple-element.31.refs_3_), channel_id=1, source_target_pairs={{0,4},{4,0},{1,5},{5,1},{2,6},{6,2},{3,7},{7,3},{8,12},{12,8},{9,1... | collective-permute-start | bytes 786440 | tf_op jit(solution)/shard_map/ppermute | solution.py:337
  41.1 11.1 %collective-permute-start.6 = (bf16[256,256]{1,0:T(8,128)(2,1)S(1)}, bf16[256,256]{1,0:T(8,128)(2,1)S(1)}, u32[]{:S(2)}, u32[]{:S(2)}) collective-permute-start(bf16[256,256]{1,0:T(8,128)(2,1)S(1)} %get-tuple-element.38), channel_id=1, source_target_pairs={{0,1},{1,0},{2,3},{3,2},{4,5},{5,4},{6,7},{7,6},{8,9},{9,8},{10,11... | collective-permute-start | bytes 393224 | tf_op jit(solution)/shard_map/ppermute | solution.py:341
  42.9 17.3 %collective-permute-start.8 = (bf16[256,256]{1,0:T(8,128)(2,1)S(1)}, bf16[256,256]{1,0:T(8,128)(2,1)S(1)}, u32[]{:S(2)}, u32[]{:S(2)}) collective-permute-start(bf16[256,256]{1,0:T(8,128)(2,1)S(1)} %get-tuple-element.37), channel_id=1, source_target_pairs={{0,1},{1,0},{2,3},{3,2},{4,5},{5,4},{6,7},{7,6},{8,9},{9,8},{10,11... | collective-permute-start | bytes 393224 | tf_op jit(solution)/shard_map/ppermute | solution.py:341
  43.2 11.9 %copy-start.2 = (bf16[256,768]{1,0:T(8,128)(2,1)S(1)}, bf16[256,768]{1,0:T(8,128)(2,1)}, u32[]{:S(2)}) copy-start(bf16[256,768]{1,0:T(8,128)(2,1)} %refs_0_.1) | copy-start | bytes 1179652
  50.3 10.0 %collective-permute-start.10 = (bf16[256,512]{1,0:T(8,128)(2,1)S(1)}, bf16[256,512]{1,0:T(8,128)(2,1)S(1)}, u32[]{:S(2)}, u32[]{:S(2)}) collective-permute-start(bf16[256,512]{1,0:T(8,128)(2,1)S(1)} %fold.14), channel_id=1, source_target_pairs={{0,1},{1,0},{2,3},{3,2},{4,5},{5,4},{6,7},{7,6},{8,9},{9,8},{10,11... | collective-permute-start | bytes 786440 | tf_op jit(solution)/shard_map/ppermute | solution.py:341
  52.2 7.8 %collective-permute-start.7 = (bf16[256,768]{1,0:T(8,128)(2,1)S(1)}, bf16[256,768]{1,0:T(8,128)(2,1)S(1)}, u32[]{:S(2)}, u32[]{:S(2)}) collective-permute-start(bf16[256,768]{1,0:T(8,128)(2,1)S(1)} %fold.11), channel_id=1, source_target_pairs={{0,4},{4,0},{1,5},{5,1},{2,6},{6,2},{3,7},{7,3},{8,12},{12,8},{9,1... | collective-permute-start | bytes 1179656 | tf_op jit(solution)/shard_map/ppermute | solution.py:366
